TPU v7x, 256 devices: a whole 4x4x8 slice. The times are simulated.
256 devices in a mesh: rep: 4 (over x), gx: 16 (over y, z_hi, core), gy: 4 (over z_lo).
Axes of the slice: x: 4, y: 4, z: 8 (z_hi: 2, z_lo: 4; z = z_hi * 4 + z_lo), core: 2. Of those that a mesh axis runs over, the one named last changes fastest.
Arguments:
- field: float32 [4, 4, 64, 64, 512], P('rep', None, None, 'gx', 'gy'), may hold values from -4 to 4
- momenta: float32 [4, 4, 64, 64, 512], P('rep', None, None, 'gx', 'gy'), may hold values from -9 to 9
- kappa: float32 [4], P('rep'), may hold values from 0.08 to 0.3
- quartic: float32 [4], P('rep'), may hold values from 0.2 to 1
- acceptance: int32 [4], replicated, may hold values from 0 to 3, as said below
Outputs:
- new_field: float32 [4, 4, 64, 64, 512], P('rep', None, None, 'gx', 'gy')
- new_momenta: float32 [4, 4, 64, 64, 512], P('rep', None, None, 'gx', 'gy')
- energy: float32 [4, 2], P('rep')
Inputs may be any that keep to these rules, and one draw needn't show every extreme that they name: acceptance[r] is r - 1, r or r + 1; it pairs replicas (acceptance[acceptance[r]] = r), and all swapped pairs start at the same parity.
All inputs are finite; a program needn't handle non-finite values.
Results may differ from a plain program's by a relative error of at most 0.00016.
Values sent between devices are 32-bit elements; how exact they have to be, the bound alone decides.
No kernel may reach another device: no remote copies, remote signals or barrier semaphores. Data moves between devices by JAX's collectives and lax.ppermute only.
A program may use at most 64 MiB of HBM per device.

v0:
```python
import functools

import jax
import jax.numpy as jnp
from jax import lax
from jax.experimental import pallas as pl
from jax.experimental.pallas import tpu as pltpu
from jax.sharding import PartitionSpec as P

LEAPS = 4
STEP = 0.05
COMPS = 4
NZ = 64
OCT = NZ // 8
WIDE = 4
LANES = 128


def f32(*shape):
    return jax.ShapeDtypeStruct(shape, jnp.float32)


def lanes():
    return lax.broadcasted_iota(jnp.int32, (8, LANES), 1)


def rows():
    return lax.broadcasted_iota(jnp.int32, (8, LANES), 0)


def packed(load):
    octet = lanes() // 16
    out = None
    for o in range(OCT):
        moved = pltpu.roll(load(o), (16 * o + 8) % LANES, 1)
        out = moved if out is None else jnp.where(octet == o, moved, out)
    return out


def layer_of(main, edge=None):
    return (lambda c, o: main[c, 8 * o : 8 * o + 8, :], None if edge is None else (lambda c: edge[c]))


def joint(ref):
    return (lambda c, o: ref[c, 8 * o : 8 * o + 8, :], lambda c: ref[c, NZ : NZ + 8, :])


def store_main(q, p):
    def put(c, o, new_p, new_q):
        if p is not None:
            p[c, 8 * o : 8 * o + 8, :] = new_p
        if q is not None:
            q[c, 8 * o : 8 * o + 8, :] = new_q

    return put


def store_edge(q, p):
    def put(c, new_p, new_q):
        p[c, NZ : NZ + 8, :] = new_p
        q[c, NZ : NZ + 8, :] = new_q

    return put


def main_eval(down, here, up, mom, put, kap, qua, dt, energy):
    lane, row = (lanes(), rows())
    zero_lane, last_lane = (lane == 0, lane == LANES - 1)
    first_row, last_row = (row == 0, row == 7)
    nsums = {}
    for c in range(COMPS):
        cells = [here[0](c, o) for o in range(OCT)]
        edge = here[1](c)
        ghosts = [pltpu.roll(edge, (120 - 16 * o) % LANES, 1) for o in range(OCT)]
        above = [pltpu.roll(q, 7, 0) for q in cells]
        below = [pltpu.roll(q, 1, 0) for q in cells]
        left = [pltpu.roll(jnp.where(last_lane, g, q), 1, 1) for g, q in zip(ghosts, cells)]
        right = [pltpu.roll(jnp.where(zero_lane, g, q), LANES - 1, 1) for g, q in zip(ghosts, cells)]
        for o in range(OCT):
            z_up = jnp.where(last_row, above[(o + 1) % OCT], above[o])
            z_down = jnp.where(first_row, below[o - 1], below[o])
            nsums[c, o] = (down[0](c, o) + up[0](c, o)) + (left[o] + right[o]) + (z_up + z_down)
    waiting = []
    for o in range(OCT):
        cells = [here[0](c, o) for c in range(COMPS)]
        moms = [mom[0](c, o) for c in range(COMPS)]
        square = cells[0] * cells[0]
        for c in range(1, COMPS):
            square = square + cells[c] * cells[c]
        coef = (2.0 - 4.0 * qua) + (4.0 * qua) * square
        dots = None
        results = []
        for c in range(COMPS):
            q, p, nsum = (cells[c], moms[c], nsums[c, o])
            new = p + dt * ((2.0 * kap) * nsum - coef * q)
            results.append((new, q + STEP * new))
            if energy is not None:
                dots = q * nsum if dots is None else dots + q * nsum
                kin = new if energy[1] else p
                energy[0] = energy[0] + 0.5 * (kin * kin)
        if energy is not None:
            energy[0] = energy[0] + (square - kap * dots + qua * ((square - 1.0) * (square - 1.0)))
        waiting.append((o, results))
        while len(waiting) > (2 if o < OCT - 1 else 0):
            at, ready = waiting.pop(0)
            for c in range(COMPS):
                put(c, at, *ready[c])


def edge_eval(jobs, kap, qua, dt):
    lane, row = (lanes(), rows())
    slot = lane % 16
    first_row, last_row = (row == 0, row == 7)
    results = []
    for down, here, up, mom, _ in jobs:
        cells = [here[1](c) for c in range(COMPS)]
        square = cells[0] * cells[0]
        for c in range(1, COMPS):
            square = square + cells[c] * cells[c]
        coef = (2.0 - 4.0 * qua) + (4.0 * qua) * square
        for c in range(COMPS):
            q = cells[c]
            own = packed(lambda o: here[0](c, o))
            right = pltpu.roll(jnp.where(slot == 8, own, q), LANES - 1, 1)
            left = pltpu.roll(jnp.where(slot == 7, own, q), 1, 1)
            above = pltpu.roll(q, 7, 0)
            below = pltpu.roll(q, 1, 0)
            z_up = jnp.where(last_row, pltpu.roll(above, LANES - 16, 1), above)
            z_down = jnp.where(first_row, pltpu.roll(below, 16, 1), below)
            nsum = (down[1](c) + up[1](c)) + (left + right) + (z_up + z_down)
            new = mom[1](c) + dt * ((2.0 * kap) * nsum - coef * q)
            results.append((new, q + STEP * new))
    for job, (*_, put) in enumerate(jobs):
        for c in range(COMPS):
            put(c, *results[job * COMPS + c])


def ingest_kernel(flags, field, momenta, *refs):
    mains, messages, (held, sems) = ((refs[:4], refs[4:8]), refs[8:10], refs[10:])
    copies = {
        (k, c): pltpu.make_async_copy(src.at[c], held.at[k, c], sems.at[k, c])
        for c in range(COMPS)
        for k, src in enumerate((field, momenta))
    }
    for copy in copies.values():
        copy.start()
    low = lanes() % 16 < 8
    odd = jnp.broadcast_to(flags[1], (8, LANES)) == 1
    for c in range(COMPS):
        copies[0, c].wait()
        copies[1, c].wait()
        for core in range(2):

            @pl.when(flags[0] == core)
            def _():
                for u in range(WIDE):
                    x = u if core == 0 else WIDE - 1 - u
                    packs = []
                    for k in range(2):
                        value = held[k, c, pl.ds(x, NZ, stride=WIDE), :]
                        mains[k][u][c] = value
                        packs.append(packed(lambda o: value[8 * o : 8 * o + 8, :]))
                    right = jnp.where(low, packs[0], pltpu.roll(packs[1], 8, 1))
                    left = jnp.where(low, pltpu.roll(packs[0], LANES - 8, 1), packs[1])
                    messages[0][u, c] = jnp.where(odd, left, right)
                    messages[1][u, c] = jnp.where(odd, right, left)


def ghost_kernel(flags, first, second, m1, k0, qg, pg, near, far):
    low = lanes() % 16 < 8
    odd = jnp.broadcast_to(flags[1], (8, LANES)) == 1
    for u in range(WIDE):
        for c in range(COMPS):
            left = jnp.where(odd, first[u, c], second[u, c])
            right = jnp.where(odd, second[u, c], first[u, c])
            q = jnp.where(low, left, pltpu.roll(right, 8, 1))
            p = jnp.where(low, pltpu.roll(left, LANES - 8, 1), right)
            qg[u, c] = q
            pg[u, c] = p
            if u == WIDE - 1:
                near[c] = q
            if u == 0:
                far[c, 2 * NZ + 8 : 2 * NZ + 16, :] = p
                far[c, 2 * NZ + 16 :, :] = q
            if u == 1:
                far[c, NZ : NZ + 8, :] = q
    for c in range(COMPS):
        far[c, :NZ, :] = m1[c]
        far[c, NZ + 8 : 2 * NZ + 8, :] = k0[c]


def fresh():
    return jnp.zeros((8, LANES), jnp.float32)


def step(around, moms, outs, kap, qua, dt, energy=None, edges=True):
    spans = [around[i : i + 3] for i in range(len(moms))]
    if edges:
        jobs = [(*span, mom, store_edge(*out)) for span, mom, out in zip(spans, moms, outs)]
        edge_eval(jobs, kap, qua, dt)
    for span, mom, out in zip(spans, moms, outs):
        main_eval(*span, mom, store_main(*out), kap, qua, dt, energy)


def inner_start(
    par, far, m0, m1, m2, m3, k0, k1, k2, k3, qg, pg, near, near_g, z, zp, q1, p1, q2, p2, q3, p3, energy
):
    kap, qua = (par[0], par[1])
    around = [layer_of(main, qg.at[u]) for u, main in enumerate((m0, m1, m2, m3))] + [layer_of(near, near_g)]
    total = [fresh(), False]
    held = [layer_of(mom, pg.at[u + 1]) for u, mom in enumerate((k1, k2, k3))]
    step(around, held, [(q1, p1), (q2, p2), (q3, p3)], kap, qua, 0.5 * STEP, total)
    store = store_main(z, zp)
    main_eval(layer_of(far), around[0], around[1], layer_of(k0), store, kap, qua, 0.5 * STEP, total)
    energy[...] = total[0]


def part_of(ref, main, edge):
    return (lambda c, o: ref[c, main + 8 * o : main + 8 * o + 8, :], lambda c: ref[c, edge : edge + 8, :])


def second_kernel(par, beyond, m0, qg, pg, z, q1, p1, q2, zg, zpg, n1, r1):
    kap, qua = (par[0], par[1])
    down, up = (part_of(beyond, 0, 2 * NZ + 16), (None, lambda c: qg[1, c]))

    def put(c, new_p, new_q):
        zpg[c] = new_p
        zg[c] = new_q

    edge_eval([(down, layer_of(m0, qg.at[0]), up, (None, lambda c: pg[0, c]), put)], kap, qua, 0.5 * STEP)
    step([layer_of(z, zg), joint(q1), joint(q2)], [joint(p1)], [(n1, r1)], kap, qua, STEP)


def third_kernel(
    par, beyond, far, m0, qg, z, zg, zp, zpg, old1, q1, p1, q2, hq, hp, nz, nzp, n1, r1, msg
):
    kap, qua = (par[0], par[1])
    halo = (layer_of(far)[0], part_of(beyond, 0, 2 * NZ + 16)[1])
    mom = part_of(beyond, NZ + 8, 2 * NZ + 8)
    step([part_of(beyond, 0, NZ), halo, layer_of(m0, qg.at[0])], [mom], [(hq, hp)], kap, qua, 0.5 * STEP)
    step([joint(hq), layer_of(z, zg), joint(old1)], [layer_of(zp, zpg)], [(nz, nzp)], kap, qua, STEP)
    step([joint(nz), joint(q1), joint(q2)], [joint(p1)], [(n1, r1)], kap, qua, STEP)
    for c in range(COMPS):
        msg[c] = n1[c, :NZ, :]


def outer_kernel(par, beyond, hq, hp, zold, zold_g, z, zp, old1, q1, p1, q2, nhq, nhp, nz, nzp, n1, r1):
    kap, qua = (par[0], par[1])
    step([joint(beyond), joint(hq), layer_of(zold, zold_g)], [joint(hp)], [(nhq, nhp)], kap, qua, STEP)
    step([joint(nhq), joint(z), joint(old1)], [joint(zp)], [(nz, nzp)], kap, qua, STEP)
    step([joint(nz), joint(q1), joint(q2)], [joint(p1)], [(n1, r1)], kap, qua, STEP)


def inner_kernel(par, q1, q2, p2, q3, p3, near, n2, r2, n3, r3):
    around = [joint(q1), joint(q2), joint(q3), joint(near)]
    step(around, [joint(p2), joint(p3)], [(n2, r2), (n3, r3)], par[0], par[1], STEP)


def inner_final(par, q1, q2, p2, q3, p3, near, r2, r3, energy):
    around = [joint(q1), joint(q2), joint(q3), joint(near)]
    total = [fresh(), True]
    outs = [(None, r2), (None, r3)]
    step(around, [joint(p2), joint(p3)], outs, par[0], par[1], 0.5 * STEP, total, False)
    energy[...] = total[0]


def outer_last(par, beyond, hq, hp, zold, z, zp, old1, q1, p1, q2, q3, nhq, nhp, nz, nzp, whole, r1, energy):
    kap, qua = (par[0], par[1])
    step([joint(beyond), joint(hq), joint(zold)], [joint(hp)], [(nhq, nhp)], kap, qua, STEP)
    step([joint(nhq), joint(z), joint(old1)], [joint(zp)], [(nz, nzp)], kap, qua, STEP)
    for u, ref in enumerate((nz, q1, q2, q3)):
        for c in range(COMPS):
            whole[u, c] = ref[c, :NZ, :]
    total = [fresh(), True]
    step([joint(nz), joint(q1), joint(q2)], [joint(p1)], [(None, r1)], kap, qua, 0.5 * STEP, total, False)
    energy[...] = total[0]


def final_kernel(par, beyond, hq, hp, zold, z, zp, q1, r1, r2, r3, start, some, more, whole, energy, nhq):
    kap, qua = (par[0], par[1])
    main_eval(layer_of(beyond), joint(hq), joint(zold), joint(hp), store_main(nhq, None), kap, qua, STEP, None)
    total = [some[...] + more[...], True]
    store = store_main(None, whole.at[0])
    main_eval(layer_of(nhq), joint(z), joint(q1), joint(zp), store, kap, qua, 0.5 * STEP, total)
    for u, ref in enumerate((r1, r2, r3)):
        for c in range(COMPS):
            whole[u + 1, c] = ref[c]
    before = jnp.sum(start[...], axis=0, keepdims=True)
    after = jnp.sum(total[0], axis=0, keepdims=True)
    row = rows()
    energy[...] = jnp.where(row == 0, before, jnp.where(row == 1, after, 0.0))


def place_kernel(flags, own, first, second, out):
    for core in range(2):
        for pick, src in enumerate((own, first, second)):

            @pl.when((flags[0] == core) & (flags[1] == pick))
            def _():
                for u in range(WIDE):
                    x = u if core == 0 else WIDE - 1 - u
                    for c in range(COMPS):
                        out[c, pl.ds(x, NZ, stride=WIDE), :] = src[u, c]


def add_kernel(one, two, out):
    out[...] = one[...] + two[...]


def run(kernel, outs, scalars, arrays, scratch=(), cost=1000, held=True, raw=False, after=()):
    vmem = pl.BlockSpec(memory_space=pltpu.VMEM)
    smem = pl.BlockSpec(memory_space=pltpu.SMEM)
    place = pl.BlockSpec(memory_space=pltpu.HBM) if raw else vmem
    if held:
        outs = [pltpu.VMEM(out.shape, out.dtype) for out in outs]
    given = len(scalars) + len(arrays)

    def body(*refs):
        kernel(*refs[:given], *refs[given + len(after) :])

    return pl.pallas_call(
        body,
        out_shape=outs,
        in_specs=[smem] * len(scalars) + [place] * len(arrays) + [pl.BlockSpec(memory_space=pl.ANY)] * len(after),
        out_specs=[vmem] * len(outs),
        scratch_shapes=list(scratch),
        cost_estimate=pl.CostEstimate(flops=cost * 4, bytes_accessed=cost, transcendentals=0),
        compiler_params=pltpu.CompilerParams(vmem_limit_bytes=12 * 1024 * 1024),
    )(*scalars, *arrays, *after)


def pair_swap(value, axis, other):
    return lax.ppermute(value, axis, [(i, other(i)) for i in range(lax.axis_size(axis)) if other(i) is not None])


def local(field, momenta, kappa, quartic, acceptance):
    gx, gy, reps = (lax.axis_size("gx"), lax.axis_size("gy"), lax.axis_size("rep"))
    volume = NZ * WIDE * LANES * gx * gy
    core = lax.axis_index("gx") % 2
    flags = jnp.stack([core, lax.axis_index("gy") % 2]).astype(jnp.int32)
    position = lax.axis_index("rep")
    partner = acceptance[position]
    pick = jnp.where(partner == position, 0, jnp.where(partner == position ^ 1, 1, 2))
    choice = jnp.stack([core, pick]).astype(jnp.int32)
    par = jnp.concatenate([kappa, quartic])

    def far(value):
        return pair_swap(value, "gx", lambda i: (i + 1) % gx if i % 2 == 1 else (i - 1) % gx)

    def near(value):
        return pair_swap(value, "gx", lambda i: i ^ 1)

    def beside(value, parity):
        return pair_swap(value, "gy", lambda i: (i + 1) % gy if i % 2 == parity else (i - 1) % gy)

    def exchanged(value):
        first = pair_swap(value, "rep", lambda i: i ^ 1 if i ^ 1 < reps else None)
        second = pair_swap(value, "rep", lambda i: ((i - 1) ^ 1) + 1 if 0 < i and ((i - 1) ^ 1) + 1 < reps else None)
        return (first, second)

    main, both = (f32(COMPS, NZ, LANES), f32(COMPS, NZ + 8, LANES))
    edges, whole, vreg = (f32(WIDE, COMPS, 8, LANES), f32(WIDE, COMPS, NZ, LANES), f32(8, LANES))
    edge = f32(COMPS, 8, LANES)

    m0, m1, m2, m3, k0, k1, k2, k3, to_first, to_second = run(
        ingest_kernel,
        [main] * 8 + [edges] * 2,
        [flags],
        [
            pltpu.with_memory_space_constraint(value.reshape(COMPS, NZ * WIDE, LANES), pltpu.HBM)
            for value in (field, momenta)
        ],
        scratch=[pltpu.VMEM((2, COMPS, NZ * WIDE, LANES), jnp.float32), pltpu.SemaphoreType.DMA((2, COMPS))],
        raw=True,
    )
    far0, near0 = (far(m0), near(m3))
    first, second = (beside(to_first, 0), beside(to_second, 1))
    qg, pg, near_g, to_far = run(
        ghost_kernel, [edges, edges, edge, f32(COMPS, 2 * NZ + 24, LANES)], [flags], [first, second, m1, k0]
    )
    near_ghost, beyond0 = (near(near_g), far(to_far))
    z1, zp1, a1, b1, a2, b2, a3, b3, start = run(
        inner_start,
        [main, main] + [both] * 6 + [vreg],
        [par],
        [far0, m0, m1, m2, m3, k0, k1, k2, k3, qg, pg, near0, near_ghost],
    )
    beyond1, near1 = (far(a1), near(a3))
    c2, d2, c3, d3 = run(inner_kernel, [both] * 4, [par], [a1, a2, b2, a3, b3, near1], after=[choice])
    zg1, zpg1, c1, d1 = run(
        second_kernel,
        [edge] * 2 + [both] * 2,
        [par],
        [beyond0, m0, qg, pg, z1, a1, b1, a2],
        after=[c2],
    )
    beyond2 = far(c1)
    near2 = near(c3)
    hq1, hp1, z2, zp2, e1, f1, msg = run(
        third_kernel,
        [both] * 6 + [main],
        [par],
        [beyond0, far0, m0, qg, z1, zg1, zp1, zpg1, a1, c1, d1, c2],
    )
    beyond3 = far(msg)
    e2, f2, e3, f3 = run(inner_kernel, [both] * 4, [par], [c1, c2, d2, c3, d3, near2], after=[hq1])
    near3 = near(e3)
    hq2, hp2, z3, zp3, g1, h1 = run(
        outer_kernel,
        [both] * 6,
        [par],
        [beyond1, hq1, hp1, z1, zg1, z2, zp2, c1, e1, f1, e2],
    )
    g2, h2, g3, h3 = run(inner_kernel, [both] * 4, [par], [e1, e2, f2, e3, f3, near3], after=[hq2])
    near4 = near(g3)
    hq3, hp3, z4, zp4, final_q, r1, some = run(
        outer_last,
        [both] * 4 + [whole, main, vreg],
        [par],
        [beyond2, hq2, hp2, z2, z3, zp3, e1, g1, h1, g2, g3],
    )
    r2, r3, more = run(inner_final, [main, main, vreg], [par], [g1, g2, h2, g3, h3, near4], after=[hq3])
    first_q, second_q = exchanged(final_q)
    final_p, energy = run(
        final_kernel,
        [whole, vreg],
        [par],
        [beyond3, hq3, hp3, z3, z4, zp4, g1, r1, r2, r3, start, some, more],
        scratch=[pltpu.VMEM((COMPS, NZ, LANES), jnp.float32)],
    )
    first_p, second_p = exchanged(final_p)

    def placed(own, first, second):
        shape = f32(COMPS, NZ * WIDE, LANES)
        return run(place_kernel, [shape], [choice], [own, first, second], held=False)[0].reshape(field.shape)

    def summed(value, axes, other, after=None):
        sizes = [lax.axis_size(axis) for axis in axes]
        pairs = []
        for i in range(sizes[0]):
            for j in range(sizes[1] if len(axes) > 1 else 1):
                to = other(i, j)
                pairs.append((i, to[0]) if len(axes) == 1 else (i * sizes[1] + j, to[0] * sizes[1] + to[1]))
        got = lax.ppermute(value, axes, pairs)
        if after is None:
            return value + got
        later = pltpu.with_memory_space_constraint(after, pltpu.HBM)
        return run(add_kernel, [vreg], [], [value, got], after=[later])[0]

    new_q = placed(final_q, first_q, second_q)
    new_p = placed(final_p, first_p, second_p)
    energy = energy + near(energy)
    y_bits = (gx // 4).bit_length() - 1
    for bit in range(y_bits):
        energy = summed(energy, ("gx",), lambda i, j, bit=bit: (i ^ (4 * (2 ** (bit + 1) - 1)),))
    z_bits = gy.bit_length() - 1
    for bit in range(z_bits):
        after = new_q if bit == z_bits - 1 else None
        energy = summed(energy, ("gy",), lambda i, j, bit=bit: (i ^ (1 << bit),), after)
    energy = summed(energy, ("gx", "gy"), lambda i, j: (i ^ 2, gy - 1 - j), new_p)
    energy = (jnp.sum(energy[:2], axis=1) / volume)[None, :]
    return (new_q, new_p, energy)


def solution(mesh):
    placed = (
        P("rep", None, None, "gx", "gy"),
        P("rep", None, None, "gx", "gy"),
        P("rep"),
        P("rep"),
        P(),
    )
    return jax.shard_map(
        local,
        mesh=mesh,
        in_specs=placed,
        out_specs=(
            P("rep", None, None, "gx", "gy"),
            P("rep", None, None, "gx", "gy"),
            P("rep", None),
        ),
        check_vma=False,
    )
```

profile of v0, /device:TPU:34, one launch (start us, length us, event | category | flops | bytes accessed | tf_op | source)
XLA Modules:
  0.0 95.6 jit_solution(13162826205230398250)
XLA Ops:
  0.6 0.1 pad_add_fusion.1.refs_0_
  0.7 2.4 %shard_map.76 = (f32[4,64,128]{2,1,0:T(8,128)S(1)}, f32[4,64,128]{2,1,0:T(8,128)S(1)}, f32[4,64,128]{2,1,0:T(8,128)S(1)}, f32[4,64,128]{2,1,0:T(8,128)S(1)}, f32...) custom-call(s32[2]{0:T(128)S(1)} %pad_add_fusion.1.refs_0_, ...), custom_call_target="tpu_custom_call" | custom-call | flops 4000 | bytes 1000 | tf_op jit(solution)/shard_map/pallas_call | solution.py:321
  3.1 0.2 collective-permute-start
  3.3 3.7 %collective-permute-start.1 = (f32[4,4,8,128]{3,2,1,0:T(8,128)S(1)}, f32[4,4,8,128]{3,2,1,0:T(8,128)S(1)}, u32[]{:S(2)}, u32[]{:S(2)}) collective-permute-start(f32[4,4,8,128]{3,2,1,0:T(8,128)S(1)} %get-tuple-element.68), channel_id=1, source_target_pairs={{0,3},{1,2},{2,1},{3,0},{4,7},{5,6},{6,5},{7,4},{8,11},{9,10},{10,... | collective-permute-start | bytes 196616 | tf_op jit(solution)/shard_map/ppermute | solution.py:333
  7.1 5.8 %collective-permute-start.3 = (f32[4,64,128]{2,1,0:T(8,128)S(1)}, f32[4,64,128]{2,1,0:T(8,128)S(1)}, u32[]{:S(2)}, u32[]{:S(2)}) collective-permute-start(f32[4,64,128]{2,1,0:T(8,128)S(1)} %get-tuple-element.72.refs_2_.refs_3_), channel_id=1, source_target_pairs={{0,60},{4,8},{8,4},{12,16},{16,12},{20,24},{24,20},{28,32},{32,28}... | collective-permute-start | bytes 393224 | tf_op jit(solution)/shard_map/ppermute | solution.py:333
  14.2 0.6 shard_map.77
  14.9 0.6 collective-permute-start.5
  15.5 8.7 %collective-permute-start.2 = (f32[4,152,128]{2,1,0:T(8,128)S(1)}, f32[4,152,128]{2,1,0:T(8,128)S(1)}, u32[]{:S(2)}, u32[]{:S(2)}) collective-permute-start(f32[4,152,128]{2,1,0:T(8,128)S(1)} %get-tuple-element.71), channel_id=1, source_target_pairs={{0,60},{4,8},{8,4},{12,16},{16,12},{20,24},{24,20},{28,32},{32,28}... | collective-permute-start | bytes 933896 | tf_op jit(solution)/shard_map/ppermute | solution.py:333
  24.2 2.4 %shard_map.78 = (f32[4,64,128]{2,1,0:T(8,128)S(1)}, f32[4,64,128]{2,1,0:T(8,128)S(1)}, f32[4,72,128]{2,1,0:T(8,128)S(1)}, f32[4,72,128]{2,1,0:T(8,128)S(1)}, f32...) custom-call(f32[2]{0:T(128)S(1)} %pad_maximum_fusion.refs_0_, ...), custom_call_target="tpu_custom_call" | custom-call | flops 4000 | bytes 1000 | tf_op jit(solution)/shard_map/pallas_call | solution.py:321
  26.6 0.1 collective-permute-start.6
  26.8 0.6 copy-done
  27.4 0.6 dynamic_slice.3
  29.3 0.1 pad_add_fusion.refs_7_.refs_0_
  29.4 1.5 %shard_map.79 = (f32[4,72,128]{2,1,0:T(8,128)S(1)}, f32[4,72,128]{2,1,0:T(8,128)S(1)}, f32[4,72,128]{2,1,0:T(8,128)S(1)}, f32[4,72,128]{2,1,0:T(8,128)S(1)}) custom-call(f32[2]{0:T(128)S(1)} %pad_maximum_fusion.refs_0_, f32[4,72,128]{2,1,0:T(8,128)S(1)} %get-tuple-element.82.refs_1_.refs_6_.refs_9_, f32[4,72,128]{2,1,0:T(8,128)S(1)} %get-tuple-element.84.refs_2_.refs_8_, ...), custom_call_target="tpu_custom_call" | custom-call | flops 4000 | bytes 1000 | tf_op jit(solution)/shard_map/pallas_call | solution.py:321
  30.8 0.6 collective-permute-start.9
  31.4 2.9 %collective-permute-start.8 = (f32[4,72,128]{2,1,0:T(8,128)S(1)}, f32[4,72,128]{2,1,0:T(8,128)S(1)}, u32[]{:S(2)}, u32[]{:S(2)}) collective-permute-start(f32[4,72,128]{2,1,0:T(8,128)S(1)} %get-tuple-element.82.refs_1_.refs_6_.refs_9_), channel_id=1, source_target_pairs={{0,60},{4,8},{8,4},{12,16},{16,12},{20,24},{24,20},{28,32},{32,28}... | collective-permute-start | bytes 442376 | tf_op jit(solution)/shard_map/ppermute | solution.py:333
  34.3 4.3 %collective-permute-done.2.refs_1_ = f32[4,152,128]{2,1,0:T(8,128)S(1)} collective-permute-done((f32[4,152,128]{2,1,0:T(8,128)S(1)}, f32[4,152,128]{2,1,0:T(8,128)S(1)}, u32[]{:S(2)}, u32[]{:S(2)}) %collective-permute-start.2) | collective-permute-done | bytes 311328 | tf_op jit(solution)/shard_map/ppermute | solution.py:333
  38.6 1.1 %shard_map.80 = (f32[4,8,128]{2,1,0:T(8,128)S(1)}, f32[4,8,128]{2,1,0:T(8,128)S(1)}, f32[4,72,128]{2,1,0:T(8,128)S(1)}, f32[4,72,128]{2,1,0:T(8,128)S(1)}) custom-call(f32[2]{0:T(128)S(1)} %pad_maximum_fusion.refs_0_, f32[4,152,128]{2,1,0:T(8,128)S(1)} %collective-permute-done.2.refs_1_, f32[4,64,128]{2,1,0:T(8,128)S(1)} %get-tuple-element.72.refs_2_.refs_3_, ...), custom_call_target="tpu_custom_call" | custom-call | flops 4000 | bytes 1000 | tf_op jit(solution)/shard_map/pallas_call | solution.py:321
  39.7 2.2 %shard_map.81 = (f32[4,72,128]{2,1,0:T(8,128)S(1)}, f32[4,72,128]{2,1,0:T(8,128)S(1)}, f32[4,72,128]{2,1,0:T(8,128)S(1)}, f32[4,72,128]{2,1,0:T(8,128)S(1)}, f32...) custom-call(f32[2]{0:T(128)S(1)} %pad_maximum_fusion.refs_0_, ...), custom_call_target="tpu_custom_call" | custom-call | flops 4000 | bytes 1000 | tf_op jit(solution)/shard_map/pallas_call | solution.py:321
  41.9 1.5 %shard_map.82 = (f32[4,72,128]{2,1,0:T(8,128)S(1)}, f32[4,72,128]{2,1,0:T(8,128)S(1)}, f32[4,72,128]{2,1,0:T(8,128)S(1)}, f32[4,72,128]{2,1,0:T(8,128)S(1)}) custom-call(f32[2]{0:T(128)S(1)} %pad_maximum_fusion.refs_0_, f32[4,72,128]{2,1,0:T(8,128)S(1)} %get-tuple-element.89.refs_10_.refs_1_.refs_8_, ...), custom_call_target="tpu_custom_call" | custom-call | flops 4000 | bytes 1000 | tf_op jit(solution)/shard_map/pallas_call | solution.py:321
  43.4 0.1 collective-permute-start.10
  43.5 6.2 %collective-permute-start.7 = (f32[4,72,128]{2,1,0:T(8,128)S(1)}, f32[4,72,128]{2,1,0:T(8,128)S(1)}, u32[]{:S(2)}, u32[]{:S(2)}) collective-permute-start(f32[4,72,128]{2,1,0:T(8,128)S(1)} %get-tuple-element.89.refs_10_.refs_1_.refs_8_), channel_id=1, source_target_pairs={{0,60},{4,8},{8,4},{12,16},{16,12},{20,24},{24,20},{28,32},{32,28}... | collective-permute-start | bytes 442376 | tf_op jit(solution)/shard_map/ppermute | solution.py:333
  49.6 2.2 %shard_map.83 = (f32[4,72,128]{2,1,0:T(8,128)S(1)}, f32[4,72,128]{2,1,0:T(8,128)S(1)}, f32[4,72,128]{2,1,0:T(8,128)S(1)}, f32[4,72,128]{2,1,0:T(8,128)S(1)}, f32...) custom-call(f32[2]{0:T(128)S(1)} %pad_maximum_fusion.refs_0_, f32[4,72,128]{2,1,0:T(8,128)S(1)} %collective-permute-done.8.refs_1_, ...), custom_call_target="tpu_custom_call" | custom-call | flops 4000 | bytes 1000 | tf_op jit(solution)/shard_map/pallas_call | solution.py:321
  51.9 1.5 %shard_map.84 = (f32[4,72,128]{2,1,0:T(8,128)S(1)}, f32[4,72,128]{2,1,0:T(8,128)S(1)}, f32[4,72,128]{2,1,0:T(8,128)S(1)}, f32[4,72,128]{2,1,0:T(8,128)S(1)}) custom-call(f32[2]{0:T(128)S(1)} %pad_maximum_fusion.refs_0_, f32[4,72,128]{2,1,0:T(8,128)S(1)} %get-tuple-element.98.refs_9_.refs_1_.refs_7_, f32[4,72,128]{2,1,0:T(8,128)S(1)} %get-tuple-element.103.refs_11_.refs_2_, ...), custom_call_target="tpu_custom_call" | custom-call | flops 4000 | bytes 1000 | tf_op jit(solution)/shard_map/pallas_call | solution.py:321
  53.3 0.1 collective-permute-start.14
  53.4 1.9 %collective-permute-start.13 = (f32[4,64,128]{2,1,0:T(8,128)S(1)}, f32[4,64,128]{2,1,0:T(8,128)S(1)}, u32[]{:S(2)}, u32[]{:S(2)}) collective-permute-start(f32[4,64,128]{2,1,0:T(8,128)S(1)} %get-tuple-element.116), channel_id=1, source_target_pairs={{0,60},{4,8},{8,4},{12,16},{16,12},{20,24},{24,20},{28,32},{32,28}... | collective-permute-start | bytes 393224 | tf_op jit(solution)/shard_map/ppermute | solution.py:333
  55.4 1.1 %collective-permute-done.7.refs_1_ = f32[4,72,128]{2,1,0:T(8,128)S(1)} collective-permute-done((f32[4,72,128]{2,1,0:T(8,128)S(1)}, f32[4,72,128]{2,1,0:T(8,128)S(1)}, u32[]{:S(2)}, u32[]{:S(2)}) %collective-permute-start.7) | collective-permute-done | bytes 147488 | tf_op jit(solution)/shard_map/ppermute | solution.py:333
  56.5 1.8 %shard_map.85 = (f32[4,72,128]{2,1,0:T(8,128)S(1)}, f32[4,72,128]{2,1,0:T(8,128)S(1)}, f32[4,72,128]{2,1,0:T(8,128)S(1)}, f32[4,72,128]{2,1,0:T(8,128)S(1)}, f32...) custom-call(f32[2]{0:T(128)S(1)} %pad_maximum_fusion.refs_0_, ...), custom_call_target="tpu_custom_call" | custom-call | flops 4000 | bytes 1000 | tf_op jit(solution)/shard_map/pallas_call | solution.py:321
  58.3 0.6 collective-permute-start.11
  58.9 4.0 %collective-permute-start.12 = (f32[4,4,64,128]{3,2,1,0:T(8,128)S(1)}, f32[4,4,64,128]{3,2,1,0:T(8,128)S(1)}, u32[]{:S(2)}, u32[]{:S(2)}) collective-permute-start(f32[4,4,64,128]{3,2,1,0:T(8,128)S(1)} %get-tuple-element.115.refs_1_), channel_id=1, source_target_pairs={{64,128},{128,64},{65,129},{129,65},{66,130},{130,66},{67,131},{13... | collective-permute-start | bytes 1572872 | tf_op jit(solution)/shard_map/ppermute | solution.py:333
  63.0 0.9 shard_map.87
  63.9 1.0 %collective-permute-done.13.refs_1_ = f32[4,64,128]{2,1,0:T(8,128)S(1)} collective-permute-done((f32[4,64,128]{2,1,0:T(8,128)S(1)}, f32[4,64,128]{2,1,0:T(8,128)S(1)}, u32[]{:S(2)}, u32[]{:S(2)}) %collective-permute-start.13) | collective-permute-done | bytes 131104 | tf_op jit(solution)/shard_map/ppermute | solution.py:333
  64.9 1.0 %shard_map.88 = (f32[4,4,64,128]{3,2,1,0:T(8,128)S(1)}, f32[8,128]{1,0:T(8,128)S(1)}) custom-call(f32[2]{0:T(128)S(1)} %pad_maximum_fusion.refs_0_, f32[4,64,128]{2,1,0:T(8,128)S(1)} %collective-permute-done.13.refs_1_, f32[4,72,128]{2,1,0:T(8,128)S(1)} %get-tuple-element.117.refs_7_.refs_2_, f32[4,72,128]{2,1,0:T(8,128)S(1)} %get-tuple-element.118.refs_3_, ...), custom_call_target="tpu_custom_call" | custom-call | flops 4000 | bytes 1000 | tf_op jit(solution)/shard_map/pallas_call | solution.py:321
  65.9 0.6 collective-permute-start.15
  66.5 4.0 %collective-permute-start.16 = (f32[4,4,64,128]{3,2,1,0:T(8,128)S(1)}, f32[4,4,64,128]{3,2,1,0:T(8,128)S(1)}, u32[]{:S(2)}, u32[]{:S(2)}) collective-permute-start(f32[4,4,64,128]{3,2,1,0:T(8,128)S(1)} %get-tuple-element.129.refs_1_), channel_id=1, source_target_pairs={{64,128},{128,64},{65,129},{129,65},{66,130},{130,66},{67,131},{13... | collective-permute-start | bytes 1572872 | tf_op jit(solution)/shard_map/ppermute | solution.py:333
  70.5 0.1 collective-permute-start.17
  70.6 1.2 %collective-permute-done.17 = f32[8,128]{1,0:T(8,128)S(1)} collective-permute-done((f32[8,128]{1,0:T(8,128)S(1)}, f32[8,128]{1,0:T(8,128)S(1)}, u32[]{:S(2)}, u32[]{:S(2)}) %collective-permute-start.17) | collective-permute-done | bytes 4128 | tf_op jit(solution)/shard_map/ppermute | solution.py:333
  71.8 3.6 %collective-permute-done.18 = f32[8,128]{1,0:T(8,128)S(1)} collective-permute-done((f32[8,128]{1,0:T(8,128)S(1)}, f32[8,128]{1,0:T(8,128)S(1)}, u32[]{:S(2)}, u32[]{:S(2)}) %collective-permute-start.18) | collective-permute-done | bytes 4128 | tf_op jit(solution)/shard_map/ppermute | solution.py:444
  75.4 4.8 %collective-permute-done.19 = f32[8,128]{1,0:T(8,128)S(1)} collective-permute-done((f32[8,128]{1,0:T(8,128)S(1)}, f32[8,128]{1,0:T(8,128)S(1)}, u32[]{:S(2)}, u32[]{:S(2)}) %collective-permute-start.19) | collective-permute-done | bytes 4128 | tf_op jit(solution)/shard_map/ppermute | solution.py:444
  80.2 3.6 %collective-permute-done.20 = f32[8,128]{1,0:T(8,128)S(1)} collective-permute-done((f32[8,128]{1,0:T(8,128)S(1)}, f32[8,128]{1,0:T(8,128)S(1)}, u32[]{:S(2)}, u32[]{:S(2)}) %collective-permute-start.20) | collective-permute-done | bytes 4128 | tf_op jit(solution)/shard_map/ppermute | solution.py:444
  83.8 0.6 collective-permute-start.21
  84.4 1.4 %shard_map.86 = f32[4,256,128]{2,1,0:T(8,128)} custom-call(s32[2]{0:T(128)S(1)} %pad_add_fusion.refs_7_.refs_0_, f32[4,4,64,128]{3,2,1,0:T(8,128)S(1)} %get-tuple-element.115.refs_1_, f32[4,4,64,128]{3,2,1,0:T(8,128)S(1)} %collective-permute-done.11.refs_2_, f32[4,4,64,128]{3,2,1,0:T(8,128)S(1)} %collective-permute-done.12.refs_3_), custom_call_target="tpu_custom_call" | custom-call | flops 4000 | bytes 1000 | tf_op jit(solution)/shard_map/pallas_call | solution.py:321
  85.9 2.5 %collective-permute-done.21.refs_1_ = f32[8,128]{1,0:T(8,128)S(1)} collective-permute-done((f32[8,128]{1,0:T(8,128)S(1)}, f32[8,128]{1,0:T(8,128)S(1)}, u32[]{:S(2)}, u32[]{:S(2)}) %collective-permute-start.21) | collective-permute-done | bytes 4128 | tf_op jit(solution)/shard_map/ppermute | solution.py:444
  88.3 0.9 collective-permute-start.22
  89.3 1.4 %shard_map.89 = f32[4,256,128]{2,1,0:T(8,128)} custom-call(s32[2]{0:T(128)S(1)} %pad_add_fusion.refs_7_.refs_0_, f32[4,4,64,128]{3,2,1,0:T(8,128)S(1)} %get-tuple-element.129.refs_1_, f32[4,4,64,128]{3,2,1,0:T(8,128)S(1)} %collective-permute-done.15.refs_2_, f32[4,4,64,128]{3,2,1,0:T(8,128)S(1)} %collective-permute-done.16.refs_3_), custom_call_target="tpu_custom_call" | custom-call | flops 4000 | bytes 1000 | tf_op jit(solution)/shard_map/pallas_call | solution.py:321
  90.7 4.2 %collective-permute-done.22.refs_1_ = f32[8,128]{1,0:T(8,128)S(1)} collective-permute-done((f32[8,128]{1,0:T(8,128)S(1)}, f32[8,128]{1,0:T(8,128)S(1)}, u32[]{:S(2)}, u32[]{:S(2)}) %collective-permute-start.22) | collective-permute-done | bytes 4128 | tf_op jit(solution)/shard_map/ppermute | solution.py:444
  95.0 0.1 slice_reduce_fusion
  95.1 0.5 multiply_bitcast_fusion
  (26 shorter events, 0.1 us)
Async XLA Ops:
  3.1 11.1 %collective-permute-start = (f32[4,4,8,128]{3,2,1,0:T(8,128)S(1)}, f32[4,4,8,128]{3,2,1,0:T(8,128)S(1)}, u32[]{:S(2)}, u32[]{:S(2)}) collective-permute-start(f32[4,4,8,128]{3,2,1,0:T(8,128)S(1)} %get-tuple-element.67), channel_id=1, source_target_pairs={{0,1},{1,0},{2,3},{3,2},{4,5},{5,4},{6,7},{7,6},{8,9},{9,8},{10,11... | collective-permute-start | bytes 196616 | tf_op jit(solution)/shard_map/ppermute | solution.py:333
  3.3 10.9 %collective-permute-start.1 = (f32[4,4,8,128]{3,2,1,0:T(8,128)S(1)}, f32[4,4,8,128]{3,2,1,0:T(8,128)S(1)}, u32[]{:S(2)}, u32[]{:S(2)}) collective-permute-start(f32[4,4,8,128]{3,2,1,0:T(8,128)S(1)} %get-tuple-element.68), channel_id=1, source_target_pairs={{0,3},{1,2},{2,1},{3,0},{4,7},{5,6},{6,5},{7,4},{8,11},{9,10},{10,... | collective-permute-start | bytes 196616 | tf_op jit(solution)/shard_map/ppermute | solution.py:333
  7.1 17.2 %collective-permute-start.3 = (f32[4,64,128]{2,1,0:T(8,128)S(1)}, f32[4,64,128]{2,1,0:T(8,128)S(1)}, u32[]{:S(2)}, u32[]{:S(2)}) collective-permute-start(f32[4,64,128]{2,1,0:T(8,128)S(1)} %get-tuple-element.72.refs_2_.refs_3_), channel_id=1, source_target_pairs={{0,60},{4,8},{8,4},{12,16},{16,12},{20,24},{24,20},{28,32},{32,28}... | collective-permute-start | bytes 393224 | tf_op jit(solution)/shard_map/ppermute | solution.py:333
  12.9 11.3 %collective-permute-start.4 = (f32[4,64,128]{2,1,0:T(8,128)S(1)}, f32[4,64,128]{2,1,0:T(8,128)S(1)}, u32[]{:S(2)}, u32[]{:S(2)}) collective-permute-start(f32[4,64,128]{2,1,0:T(8,128)S(1)} %get-tuple-element.76.refs_5_), channel_id=1, source_target_pairs={{0,4},{4,0},{8,12},{12,8},{16,20},{20,16},{24,28},{28,24},{32,36},... | collective-permute-start | bytes 393224 | tf_op jit(solution)/shard_map/ppermute | solution.py:333
  14.9 9.4 %collective-permute-start.5 = (f32[4,8,128]{2,1,0:T(8,128)S(1)}, f32[4,8,128]{2,1,0:T(8,128)S(1)}, u32[]{:S(2)}, u32[]{:S(2)}) collective-permute-start(f32[4,8,128]{2,1,0:T(8,128)S(1)} %get-tuple-element.80), channel_id=1, source_target_pairs={{0,4},{4,0},{8,12},{12,8},{16,20},{20,16},{24,28},{28,24},{32,36},... | collective-permute-start | bytes 49160 | tf_op jit(solution)/shard_map/ppermute | solution.py:333
  15.5 23.1 %collective-permute-start.2 = (f32[4,152,128]{2,1,0:T(8,128)S(1)}, f32[4,152,128]{2,1,0:T(8,128)S(1)}, u32[]{:S(2)}, u32[]{:S(2)}) collective-permute-start(f32[4,152,128]{2,1,0:T(8,128)S(1)} %get-tuple-element.71), channel_id=1, source_target_pairs={{0,60},{4,8},{8,4},{12,16},{16,12},{20,24},{24,20},{28,32},{32,28}... | collective-permute-start | bytes 933896 | tf_op jit(solution)/shard_map/ppermute | solution.py:333
  26.6 2.7 %collective-permute-start.6 = (f32[4,72,128]{2,1,0:T(8,128)S(1)}, f32[4,72,128]{2,1,0:T(8,128)S(1)}, u32[]{:S(2)}, u32[]{:S(2)}) collective-permute-start(f32[4,72,128]{2,1,0:T(8,128)S(1)} %get-tuple-element.86.refs_4_), channel_id=1, source_target_pairs={{0,4},{4,0},{8,12},{12,8},{16,20},{20,16},{24,28},{28,24},{32,36},... | collective-permute-start | bytes 442376 | tf_op jit(solution)/shard_map/ppermute | solution.py:333
  26.8 0.7 copy-start
  30.8 11.1 %collective-permute-start.9 = (f32[4,72,128]{2,1,0:T(8,128)S(1)}, f32[4,72,128]{2,1,0:T(8,128)S(1)}, u32[]{:S(2)}, u32[]{:S(2)}) collective-permute-start(f32[4,72,128]{2,1,0:T(8,128)S(1)} %get-tuple-element.101.refs_4_), channel_id=1, source_target_pairs={{0,4},{4,0},{8,12},{12,8},{16,20},{20,16},{24,28},{28,24},{32,36},... | collective-permute-start | bytes 442376 | tf_op jit(solution)/shard_map/ppermute | solution.py:333
  31.4 18.2 %collective-permute-start.8 = (f32[4,72,128]{2,1,0:T(8,128)S(1)}, f32[4,72,128]{2,1,0:T(8,128)S(1)}, u32[]{:S(2)}, u32[]{:S(2)}) collective-permute-start(f32[4,72,128]{2,1,0:T(8,128)S(1)} %get-tuple-element.82.refs_1_.refs_6_.refs_9_), channel_id=1, source_target_pairs={{0,60},{4,8},{8,4},{12,16},{16,12},{20,24},{24,20},{28,32},{32,28}... | collective-permute-start | bytes 442376 | tf_op jit(solution)/shard_map/ppermute | solution.py:333
  43.4 8.5 %collective-permute-start.10 = (f32[4,72,128]{2,1,0:T(8,128)S(1)}, f32[4,72,128]{2,1,0:T(8,128)S(1)}, u32[]{:S(2)}, u32[]{:S(2)}) collective-permute-start(f32[4,72,128]{2,1,0:T(8,128)S(1)} %get-tuple-element.111.refs_4_), channel_id=1, source_target_pairs={{0,4},{4,0},{8,12},{12,8},{16,20},{20,16},{24,28},{28,24},{32,36},... | collective-permute-start | bytes 442376 | tf_op jit(solution)/shard_map/ppermute | solution.py:333
  43.5 13.0 %collective-permute-start.7 = (f32[4,72,128]{2,1,0:T(8,128)S(1)}, f32[4,72,128]{2,1,0:T(8,128)S(1)}, u32[]{:S(2)}, u32[]{:S(2)}) collective-permute-start(f32[4,72,128]{2,1,0:T(8,128)S(1)} %get-tuple-element.89.refs_10_.refs_1_.refs_8_), channel_id=1, source_target_pairs={{0,60},{4,8},{8,4},{12,16},{16,12},{20,24},{24,20},{28,32},{32,28}... | collective-permute-start | bytes 442376 | tf_op jit(solution)/shard_map/ppermute | solution.py:333
  53.3 9.6 %collective-permute-start.14 = (f32[4,72,128]{2,1,0:T(8,128)S(1)}, f32[4,72,128]{2,1,0:T(8,128)S(1)}, u32[]{:S(2)}, u32[]{:S(2)}) collective-permute-start(f32[4,72,128]{2,1,0:T(8,128)S(1)} %get-tuple-element.114.refs_11_.refs_4_), channel_id=1, source_target_pairs={{0,4},{4,0},{8,12},{12,8},{16,20},{20,16},{24,28},{28,24},{32,36},... | collective-permute-start | bytes 442376 | tf_op jit(solution)/shard_map/ppermute | solution.py:333
  53.4 11.4 %collective-permute-start.13 = (f32[4,64,128]{2,1,0:T(8,128)S(1)}, f32[4,64,128]{2,1,0:T(8,128)S(1)}, u32[]{:S(2)}, u32[]{:S(2)}) collective-permute-start(f32[4,64,128]{2,1,0:T(8,128)S(1)} %get-tuple-element.116), channel_id=1, source_target_pairs={{0,60},{4,8},{8,4},{12,16},{16,12},{20,24},{24,20},{28,32},{32,28}... | collective-permute-start | bytes 393224 | tf_op jit(solution)/shard_map/ppermute | solution.py:333
  58.3 26.2 %collective-permute-start.11 = (f32[4,4,64,128]{3,2,1,0:T(8,128)S(1)}, f32[4,4,64,128]{3,2,1,0:T(8,128)S(1)}, u32[]{:S(2)}, u32[]{:S(2)}) collective-permute-start(f32[4,4,64,128]{3,2,1,0:T(8,128)S(1)} %get-tuple-element.115.refs_1_), channel_id=1, source_target_pairs={{0,64},{64,0},{128,192},{192,128},{1,65},{65,1},{129,193},{193,129... | collective-permute-start | bytes 1572872 | tf_op jit(solution)/shard_map/ppermute | solution.py:333
  58.9 25.6 %collective-permute-start.12 = (f32[4,4,64,128]{3,2,1,0:T(8,128)S(1)}, f32[4,4,64,128]{3,2,1,0:T(8,128)S(1)}, u32[]{:S(2)}, u32[]{:S(2)}) collective-permute-start(f32[4,4,64,128]{3,2,1,0:T(8,128)S(1)} %get-tuple-element.115.refs_1_), channel_id=1, source_target_pairs={{64,128},{128,64},{65,129},{129,65},{66,130},{130,66},{67,131},{13... | collective-permute-start | bytes 1572872 | tf_op jit(solution)/shard_map/ppermute | solution.py:333
  65.9 23.4 %collective-permute-start.15 = (f32[4,4,64,128]{3,2,1,0:T(8,128)S(1)}, f32[4,4,64,128]{3,2,1,0:T(8,128)S(1)}, u32[]{:S(2)}, u32[]{:S(2)}) collective-permute-start(f32[4,4,64,128]{3,2,1,0:T(8,128)S(1)} %get-tuple-element.129.refs_1_), channel_id=1, source_target_pairs={{0,64},{64,0},{128,192},{192,128},{1,65},{65,1},{129,193},{193,129... | collective-permute-start | bytes 1572872 | tf_op jit(solution)/shard_map/ppermute | solution.py:333
  66.5 22.8 %collective-permute-start.16 = (f32[4,4,64,128]{3,2,1,0:T(8,128)S(1)}, f32[4,4,64,128]{3,2,1,0:T(8,128)S(1)}, u32[]{:S(2)}, u32[]{:S(2)}) collective-permute-start(f32[4,4,64,128]{3,2,1,0:T(8,128)S(1)} %get-tuple-element.129.refs_1_), channel_id=1, source_target_pairs={{64,128},{128,64},{65,129},{129,65},{66,130},{130,66},{67,131},{13... | collective-permute-start | bytes 1572872 | tf_op jit(solution)/shard_map/ppermute | solution.py:333
  70.5 1.3 %collective-permute-start.17 = (f32[8,128]{1,0:T(8,128)S(1)}, f32[8,128]{1,0:T(8,128)S(1)}, u32[]{:S(2)}, u32[]{:S(2)}) collective-permute-start(f32[8,128]{1,0:T(8,128)S(1)} %get-tuple-element.130), channel_id=1, source_target_pairs={{0,4},{4,0},{8,12},{12,8},{16,20},{20,16},{24,28},{28,24},{32,36},... | collective-permute-start | bytes 12296 | tf_op jit(solution)/shard_map/ppermute | solution.py:333
  71.8 3.6 %collective-permute-start.18 = (f32[8,128]{1,0:T(8,128)S(1)}, f32[8,128]{1,0:T(8,128)S(1)}, u32[]{:S(2)}, u32[]{:S(2)}) collective-permute-start(f32[8,128]{1,0:T(8,128)S(1)} %add.25), channel_id=1, source_target_pairs={{0,16},{4,20},{8,24},{12,28},{16,0},{20,4},{24,8},{28,12},{32,48},... | collective-permute-start | bytes 12296 | tf_op jit(solution)/shard_map/ppermute | solution.py:444
  75.4 4.8 %collective-permute-start.19 = (f32[8,128]{1,0:T(8,128)S(1)}, f32[8,128]{1,0:T(8,128)S(1)}, u32[]{:S(2)}, u32[]{:S(2)}) collective-permute-start(f32[8,128]{1,0:T(8,128)S(1)} %add.26), channel_id=1, source_target_pairs={{0,48},{4,52},{8,56},{12,60},{16,32},{20,36},{24,40},{28,44},{32,1... | collective-permute-start | bytes 12296 | tf_op jit(solution)/shard_map/ppermute | solution.py:444
  80.2 3.6 %collective-permute-start.20 = (f32[8,128]{1,0:T(8,128)S(1)}, f32[8,128]{1,0:T(8,128)S(1)}, u32[]{:S(2)}, u32[]{:S(2)}) collective-permute-start(f32[8,128]{1,0:T(8,128)S(1)} %add.27), channel_id=1, source_target_pairs={{0,1},{1,0},{2,3},{3,2},{4,5},{5,4},{6,7},{7,6},{8,9},{9,8},{10,11... | collective-permute-start | bytes 12296 | tf_op jit(solution)/shard_map/ppermute | solution.py:444
  83.8 4.5 %collective-permute-start.21 = (f32[8,128]{1,0:T(8,128)S(1)}, f32[8,128]{1,0:T(8,128)S(1)}, u32[]{:S(2)}, u32[]{:S(2)}) collective-permute-start(f32[8,128]{1,0:T(8,128)S(1)} %add.28.refs_0_), channel_id=1, source_target_pairs={{0,2},{1,3},{2,0},{3,1},{4,6},{5,7},{6,4},{7,5},{8,10},{9,11},{10,... | collective-permute-start | bytes 12296 | tf_op jit(solution)/shard_map/ppermute | solution.py:444
  88.3 6.6 %collective-permute-start.22 = (f32[8,128]{1,0:T(8,128)S(1)}, f32[8,128]{1,0:T(8,128)S(1)}, u32[]{:S(2)}, u32[]{:S(2)}) collective-permute-start(f32[8,128]{1,0:T(8,128)S(1)} %shard_map.90.refs_0_), channel_id=1, source_target_pairs={{0,11},{1,10},{2,9},{3,8},{4,15},{5,14},{6,13},{7,12},{8,3},{9,2},... | collective-permute-start | bytes 12296 | tf_op jit(solution)/shard_map/ppermute | solution.py:444
where the time goes:
time: 95.8 us; the launch traced here: 95.6 us
  starting transfers between devices  41.9 us (44%)
  waiting for transfers between devices  26.3 us (27%)
  Pallas kernels  21.9 us (23%)
  between operations  3.46 us (4%)
  local copies, waits for them, and re-layouts  1.23 us (1%)
    ppermute x18, starting transfers between devices, pair_swap(): lax.ppermute(value, axis, [(i, other(i)) for i in range(lax.axis_size(axi...  40.3 us
    pallas_call x16, Pallas kernels, run(): pl.pallas_call(body, out_shape=outs, in_specs=[smem] * len(scalars) + [pl...  21.9 us
    ppermute x5, waiting for transfers between devices, summed(): got = lax.ppermute(value, axes, pairs)  18.7 us
    ppermute x18, waiting for transfers between devices, pair_swap(): lax.ppermute(value, axis, [(i, other(i)) for i in range(lax.axis_size(axi...  7.56 us
  transfers between devices with their start and end apart: 23, of which 9 were waited for; matrix products, arithmetic and copies ran while one was open for 1% of the time, Pallas kernels for 20%

commit v1 on v0

--- a/solution.py
+++ b/solution.py
@@ -14,6 +14,7 @@
 OCT = NZ // 8
 WIDE = 4
 LANES = 128
+SITES = COMPS * NZ
 
 
 def f32(*shape):
@@ -130,9 +131,13 @@
             nsum = (down[1](c) + up[1](c)) + (left + right) + (z_up + z_down)
             new = mom[1](c) + dt * ((2.0 * kap) * nsum - coef * q)
             results.append((new, q + STEP * new))
-    for job, (*_, put) in enumerate(jobs):
-        for c in range(COMPS):
-            put(c, *results[job * COMPS + c])
+
+    def store():
+        for job, (*_, put) in enumerate(jobs):
+            for c in range(COMPS):
+                put(c, *results[job * COMPS + c])
+
+    return store
 
 
 def ingest_kernel(flags, field, momenta, *refs):
@@ -179,14 +184,11 @@
             pg[u, c] = p
             if u == WIDE - 1:
                 near[c] = q
-            if u == 0:
-                far[c, 2 * NZ + 8 : 2 * NZ + 16, :] = p
-                far[c, 2 * NZ + 16 :, :] = q
-            if u == 1:
-                far[c, NZ : NZ + 8, :] = q
-    for c in range(COMPS):
-        far[c, :NZ, :] = m1[c]
-        far[c, NZ + 8 : 2 * NZ + 8, :] = k0[c]
+    write_main(far, 0, lambda c, o: m1[c, 8 * o : 8 * o + 8, :])
+    write_main(far, SITES, lambda c, o: k0[c, 8 * o : 8 * o + 8, :])
+    write_edge(far, 2 * SITES, lambda c: qg[0, c])
+    write_edge(far, 2 * SITES + 16, lambda c: qg[1, c])
+    write_edge(far, 2 * SITES + 32, lambda c: pg[0, c])
 
 
 def fresh():
@@ -195,58 +197,80 @@
 
 def step(around, moms, outs, kap, qua, dt, energy=None, edges=True):
     spans = [around[i : i + 3] for i in range(len(moms))]
+    store = None
     if edges:
         jobs = [(*span, mom, store_edge(*out)) for span, mom, out in zip(spans, moms, outs)]
-        edge_eval(jobs, kap, qua, dt)
+        store = edge_eval(jobs, kap, qua, dt)
     for span, mom, out in zip(spans, moms, outs):
         main_eval(*span, mom, store_main(*out), kap, qua, dt, energy)
+    if edges:
+        store()
+
+
+def inside(ref, main, edge):
+    def ghosts(c):
+        value = ref[edge + 8 * (c % 2) : edge + 8 * (c % 2) + 8, :]
+        return value if c < 2 else pltpu.roll(value, LANES - 8, 1)
+
+    return (lambda c, o: ref[main + NZ * c + 8 * o : main + NZ * c + 8 * o + 8, :], ghosts)
+
+
+def write_main(ref, main, load):
+    for c in range(COMPS):
+        for o in range(OCT):
+            ref[main + NZ * c + 8 * o : main + NZ * c + 8 * o + 8, :] = load(c, o)
+
+
+def write_edge(ref, edge, load):
+    slot = lanes() % 16
+    for c in range(2):
+        both = jnp.where((slot >= 4) & (slot < 12), load(c), pltpu.roll(load(c + 2), 8, 1))
+        ref[edge + 8 * c : edge + 8 * c + 8, :] = both
 
 
 def inner_start(
-    par, far, m0, m1, m2, m3, k0, k1, k2, k3, qg, pg, near, near_g, z, zp, q1, p1, q2, p2, q3, p3, energy
+    par, far, m0, m1, m2, m3, k0, k1, k2, k3, qg, pg, near, near_g, z, zp, q1, p1, q2, p2, q3, p3, energy, msg
 ):
     kap, qua = (par[0], par[1])
     around = [layer_of(main, qg.at[u]) for u, main in enumerate((m0, m1, m2, m3))] + [layer_of(near, near_g)]
     total = [fresh(), False]
     held = [layer_of(mom, pg.at[u + 1]) for u, mom in enumerate((k1, k2, k3))]
     step(around, held, [(q1, p1), (q2, p2), (q3, p3)], kap, qua, 0.5 * STEP, total)
+    write_main(msg, 0, joint(q1)[0])
+    write_edge(msg, SITES, joint(q1)[1])
     store = store_main(z, zp)
     main_eval(layer_of(far), around[0], around[1], layer_of(k0), store, kap, qua, 0.5 * STEP, total)
     energy[...] = total[0]
 
 
-def part_of(ref, main, edge):
-    return (lambda c, o: ref[c, main + 8 * o : main + 8 * o + 8, :], lambda c: ref[c, edge : edge + 8, :])
-
-
-def second_kernel(par, beyond, m0, qg, pg, z, q1, p1, q2, zg, zpg, n1, r1):
+def outer_first(par, beyond, far, m0, qg, pg, z, zp, q1, p1, q2, zg, n1, r1, hq, hp, nz, nzp, zpg):
     kap, qua = (par[0], par[1])
-    down, up = (part_of(beyond, 0, 2 * NZ + 16), (None, lambda c: qg[1, c]))
+    outer, halo = (inside(beyond, 0, 2 * SITES + 16), inside(beyond, 0, 2 * SITES))
+    halo = (layer_of(far)[0], halo[1])
+    here = layer_of(m0, qg.at[0])
 
     def put(c, new_p, new_q):
         zpg[c] = new_p
         zg[c] = new_q
 
-    edge_eval([(down, layer_of(m0, qg.at[0]), up, (None, lambda c: pg[0, c]), put)], kap, qua, 0.5 * STEP)
+    edge_eval([(halo, here, (None, lambda c: qg[1, c]), (None, lambda c: pg[0, c]), put)], kap, qua, 0.5 * STEP)()
+    step([outer, halo, here], [inside(beyond, SITES, 2 * SITES + 32)], [(hq, hp)], kap, qua, 0.5 * STEP)
     step([layer_of(z, zg), joint(q1), joint(q2)], [joint(p1)], [(n1, r1)], kap, qua, STEP)
-
-
-def third_kernel(
-    par, beyond, far, m0, qg, z, zg, zp, zpg, old1, q1, p1, q2, hq, hp, nz, nzp, n1, r1, msg
-):
-    kap, qua = (par[0], par[1])
-    halo = (layer_of(far)[0], part_of(beyond, 0, 2 * NZ + 16)[1])
-    mom = part_of(beyond, NZ + 8, 2 * NZ + 8)
-    step([part_of(beyond, 0, NZ), halo, layer_of(m0, qg.at[0])], [mom], [(hq, hp)], kap, qua, 0.5 * STEP)
-    step([joint(hq), layer_of(z, zg), joint(old1)], [layer_of(zp, zpg)], [(nz, nzp)], kap, qua, STEP)
-    step([joint(nz), joint(q1), joint(q2)], [joint(p1)], [(n1, r1)], kap, qua, STEP)
-    for c in range(COMPS):
-        msg[c] = n1[c, :NZ, :]
+    step([joint(hq), layer_of(z, zg), joint(q1)], [layer_of(zp, zpg)], [(nz, nzp)], kap, qua, STEP)
+
+
+def inner_second(par, z, q1, p1, q2, p2, q3, p3, near, n1, r1, n2, r2, n3, r3, msg):
+    around = [joint(z), joint(q1), joint(q2), joint(q3), joint(near)]
+    moms = [joint(p1), joint(p2), joint(p3)]
+    step(around, moms, [(n1, r1), (n2, r2), (n3, r3)], par[0], par[1], STEP)
+    write_main(msg, 0, joint(q1)[0])
+    write_edge(msg, SITES, joint(q1)[1])
+    write_main(msg, SITES + 16, joint(n1)[0])
 
 
 def outer_kernel(par, beyond, hq, hp, zold, zold_g, z, zp, old1, q1, p1, q2, nhq, nhp, nz, nzp, n1, r1):
     kap, qua = (par[0], par[1])
-    step([joint(beyond), joint(hq), layer_of(zold, zold_g)], [joint(hp)], [(nhq, nhp)], kap, qua, STEP)
+    step([inside(beyond, 0, SITES), joint(hq), layer_of(zold, zold_g)], [joint(hp)], [(nhq, nhp)], kap, qua, STEP)
     step([joint(nhq), joint(z), joint(old1)], [joint(zp)], [(nz, nzp)], kap, qua, STEP)
     step([joint(nz), joint(q1), joint(q2)], [joint(p1)], [(n1, r1)], kap, qua, STEP)
 
@@ -254,6 +278,13 @@
 def inner_kernel(par, q1, q2, p2, q3, p3, near, n2, r2, n3, r3):
     around = [joint(q1), joint(q2), joint(q3), joint(near)]
     step(around, [joint(p2), joint(p3)], [(n2, r2), (n3, r3)], par[0], par[1], STEP)
+
+
+def inner_third(par, q1, q2, p2, q3, p3, near, n2, r2, n3, r3, whole):
+    inner_kernel(par, q1, q2, p2, q3, p3, near, n2, r2, n3, r3)
+    for u, ref in enumerate((n2, n3)):
+        for c in range(COMPS):
+            whole[u, c] = ref[c, :NZ, :]
 
 
 def inner_final(par, q1, q2, p2, q3, p3, near, r2, r3, energy):
@@ -264,43 +295,48 @@
     energy[...] = total[0]
 
 
-def outer_last(par, beyond, hq, hp, zold, z, zp, old1, q1, p1, q2, q3, nhq, nhp, nz, nzp, whole, r1, energy):
+def outer_last(
+    par, beyond, hq, hp, zold, z, zp, old1, q1, p1, q2, r2, r3, start, more,
+    whole, energy, nhq, nhp, nz, nzp, last,
+):
     kap, qua = (par[0], par[1])
-    step([joint(beyond), joint(hq), joint(zold)], [joint(hp)], [(nhq, nhp)], kap, qua, STEP)
+    step([inside(beyond, 0, SITES), joint(hq), joint(zold)], [joint(hp)], [(nhq, nhp)], kap, qua, STEP)
     step([joint(nhq), joint(z), joint(old1)], [joint(zp)], [(nz, nzp)], kap, qua, STEP)
-    for u, ref in enumerate((nz, q1, q2, q3)):
-        for c in range(COMPS):
-            whole[u, c] = ref[c, :NZ, :]
-    total = [fresh(), True]
-    step([joint(nz), joint(q1), joint(q2)], [joint(p1)], [(None, r1)], kap, qua, 0.5 * STEP, total, False)
-    energy[...] = total[0]
-
-
-def final_kernel(par, beyond, hq, hp, zold, z, zp, q1, r1, r2, r3, start, some, more, whole, energy, nhq):
-    kap, qua = (par[0], par[1])
-    main_eval(layer_of(beyond), joint(hq), joint(zold), joint(hp), store_main(nhq, None), kap, qua, STEP, None)
-    total = [some[...] + more[...], True]
-    store = store_main(None, whole.at[0])
-    main_eval(layer_of(nhq), joint(z), joint(q1), joint(zp), store, kap, qua, 0.5 * STEP, total)
-    for u, ref in enumerate((r1, r2, r3)):
-        for c in range(COMPS):
-            whole[u + 1, c] = ref[c]
+    store = store_main(last, None)
+    outer = inside(beyond, SITES + 16, 0)
+    main_eval(outer, joint(nhq), joint(z), joint(nhp), store, kap, qua, STEP, None)
+    total = [more[...], True]
+    store = store_main(None, whole.at[2])
+    main_eval(layer_of(last), joint(nz), joint(q1), joint(nzp), store, kap, qua, 0.5 * STEP, total)
+    store = store_main(None, whole.at[3])
+    main_eval(joint(nz), joint(q1), joint(q2), joint(p1), store, kap, qua, 0.5 * STEP, total)
     before = jnp.sum(start[...], axis=0, keepdims=True)
     after = jnp.sum(total[0], axis=0, keepdims=True)
     row = rows()
     energy[...] = jnp.where(row == 0, before, jnp.where(row == 1, after, 0.0))
-
-
-def place_kernel(flags, own, first, second, out):
+    for c in range(COMPS):
+        whole[0, c] = nz[c, :NZ, :]
+        whole[1, c] = q1[c, :NZ, :]
+        whole[4, c] = r2[c]
+        whole[5, c] = r3[c]
+
+
+def place_kernel(part, flags, *refs):
+    *sources, out = refs
     for core in range(2):
-        for pick, src in enumerate((own, first, second)):
+        for pick in range(3):
 
             @pl.when((flags[0] == core) & (flags[1] == pick))
             def _():
+                late = sources[pick]
                 for u in range(WIDE):
                     x = u if core == 0 else WIDE - 1 - u
                     for c in range(COMPS):
-                        out[c, pl.ds(x, NZ, stride=WIDE), :] = src[u, c]
+                        if part == 1:
+                            value = late[u + 2, c]
+                        else:
+                            value = late[u, c] if u < 2 else sources[3 + pick][u - 2, c]
+                        out[c, pl.ds(x, NZ, stride=WIDE), :] = value
 
 
 def add_kernel(one, two, out):
@@ -376,34 +412,32 @@
     far0, near0 = (far(m0), near(m3))
     first, second = (beside(to_first, 0), beside(to_second, 1))
     qg, pg, near_g, to_far = run(
-        ghost_kernel, [edges, edges, edge, f32(COMPS, 2 * NZ + 24, LANES)], [flags], [first, second, m1, k0]
+        ghost_kernel, [edges, edges, edge, f32(2 * SITES + 80, LANES)], [flags], [first, second, m1, k0]
     )
     near_ghost, beyond0 = (near(near_g), far(to_far))
-    z1, zp1, a1, b1, a2, b2, a3, b3, start = run(
+    z1, zp1, a1, b1, a2, b2, a3, b3, start, msg = run(
         inner_start,
-        [main, main] + [both] * 6 + [vreg],
+        [main, main] + [both] * 6 + [vreg, f32(SITES + 32, LANES)],
         [par],
         [far0, m0, m1, m2, m3, k0, k1, k2, k3, qg, pg, near0, near_ghost],
     )
-    beyond1, near1 = (far(a1), near(a3))
+    beyond1, near1 = (far(msg), near(a3))
     c2, d2, c3, d3 = run(inner_kernel, [both] * 4, [par], [a1, a2, b2, a3, b3, near1], after=[choice])
-    zg1, zpg1, c1, d1 = run(
-        second_kernel,
-        [edge] * 2 + [both] * 2,
+    near2 = near(c3)
+    zg1, c1, d1, hq1, hp1, z2, zp2 = run(
+        outer_first,
+        [edge] + [both] * 6,
         [par],
-        [beyond0, m0, qg, pg, z1, a1, b1, a2],
-        after=[c2],
-    )
-    beyond2 = far(c1)
-    near2 = near(c3)
-    hq1, hp1, z2, zp2, e1, f1, msg = run(
-        third_kernel,
-        [both] * 6 + [main],
+        [beyond0, far0, m0, qg, pg, z1, zp1, a1, b1, a2],
+        scratch=[pltpu.VMEM((COMPS, 8, LANES), jnp.float32)],
+    )
+    e1, f1, e2, f2, e3, f3, msg = run(
+        inner_second,
+        [both] * 6 + [f32(2 * SITES + 16, LANES)],
         [par],
-        [beyond0, far0, m0, qg, z1, zg1, zp1, zpg1, a1, c1, d1, c2],
-    )
-    beyond3 = far(msg)
-    e2, f2, e3, f3 = run(inner_kernel, [both] * 4, [par], [c1, c2, d2, c3, d3, near2], after=[hq1])
+        [z2, c1, d1, c2, d2, c3, d3, near2],
+    )
+    beyond2 = far(msg)
     near3 = near(e3)
     hq2, hp2, z3, zp3, g1, h1 = run(
         outer_kernel,
@@ -411,28 +445,29 @@
         [par],
         [beyond1, hq1, hp1, z1, zg1, z2, zp2, c1, e1, f1, e2],
     )
-    g2, h2, g3, h3 = run(inner_kernel, [both] * 4, [par], [e1, e2, f2, e3, f3, near3], after=[hq2])
+    g2, h2, g3, h3, early = run(
+        inner_third,
+        [both] * 4 + [f32(2, COMPS, NZ, LANES)],
+        [par],
+        [e1, e2, f2, e3, f3, near3],
+        after=[hq2],
+    )
     near4 = near(g3)
-    hq3, hp3, z4, zp4, final_q, r1, some = run(
+    first_early, second_early = exchanged(early)
+    r2, r3, more = run(inner_final, [main, main, vreg], [par], [g1, g2, h2, g3, h3, near4])
+    late, energy = run(
         outer_last,
-        [both] * 4 + [whole, main, vreg],
+        [f32(6, COMPS, NZ, LANES), vreg],
         [par],
-        [beyond2, hq2, hp2, z2, z3, zp3, e1, g1, h1, g2, g3],
-    )
-    r2, r3, more = run(inner_final, [main, main, vreg], [par], [g1, g2, h2, g3, h3, near4], after=[hq3])
-    first_q, second_q = exchanged(final_q)
-    final_p, energy = run(
-        final_kernel,
-        [whole, vreg],
-        [par],
-        [beyond3, hq3, hp3, z3, z4, zp4, g1, r1, r2, r3, start, some, more],
-        scratch=[pltpu.VMEM((COMPS, NZ, LANES), jnp.float32)],
-    )
-    first_p, second_p = exchanged(final_p)
-
-    def placed(own, first, second):
-        shape = f32(COMPS, NZ * WIDE, LANES)
-        return run(place_kernel, [shape], [choice], [own, first, second], held=False)[0].reshape(field.shape)
+        [beyond2, hq2, hp2, z2, z3, zp3, e1, g1, h1, g2, r2, r3, start, more],
+        after=[first_early, second_early],
+        scratch=[pltpu.VMEM((COMPS, NZ + 8, LANES), jnp.float32)] * 4 + [pltpu.VMEM((COMPS, NZ, LANES), jnp.float32)],
+    )
+    first_late, second_late = exchanged(late)
+
+    def placed(part, arrays):
+        kernel = functools.partial(place_kernel, part)
+        return run(kernel, [f32(COMPS, NZ * WIDE, LANES)], [choice], arrays, held=False)[0].reshape(field.shape)
 
     def summed(value, axes, other, after=None):
         sizes = [lax.axis_size(axis) for axis in axes]
@@ -447,8 +482,8 @@
         later = pltpu.with_memory_space_constraint(after, pltpu.HBM)
         return run(add_kernel, [vreg], [], [value, got], after=[later])[0]
 
-    new_q = placed(final_q, first_q, second_q)
-    new_p = placed(final_p, first_p, second_p)
+    new_q = placed(0, [late, first_late, second_late, early, first_early, second_early])
+    new_p = placed(1, [late, first_late, second_late])
     energy = energy + near(energy)
     y_bits = (gx // 4).bit_length() - 1
     for bit in range(y_bits):

time: 95.8 us -> 91.5 us (0.955)
  the two profiles are of different devices: /device:TPU:34 before, /device:TPU:2 now
where the time goes in v1:
time: 91.5 us; the launch traced here: 91.3 us
  starting transfers between devices  33.9 us (37%)
  waiting for transfers between devices  30.3 us (33%)
  Pallas kernels  21.5 us (23%)
  between operations  3.41 us (4%)
  local copies, waits for them, and re-layouts  1.24 us (1%)
    ppermute x17, starting transfers between devices, pair_swap(): lax.ppermute(value, axis, [(i, other(i)) for i in range(lax.axis_size(axi...  33.2 us
    pallas_call x14, Pallas kernels, run(): pl.pallas_call(body, out_shape=outs, in_specs=[smem] * len(scalars) + [pl...  21.5 us
    ppermute x5, waiting for transfers between devices, summed(): got = lax.ppermute(value, axes, pairs)  16.5 us
    ppermute x17, waiting for transfers between devices, pair_swap(): lax.ppermute(value, axis, [(i, other(i)) for i in range(lax.axis_size(axi...  13.8 us
  transfers between devices with their start and end apart: 22, of which 11 were waited for; matrix products, arithmetic and copies ran while one was open for 1% of the time, Pallas kernels for 18%

profile of v1, /device:TPU:2, one launch (start us, length us, event | category | flops | bytes accessed | tf_op | source)
XLA Modules:
  0.0 91.3 jit_solution(11453618805801919002)
XLA Ops:
  0.6 0.1 pad_add_fusion.1.refs_0_
  0.7 2.4 %shard_map.76 = (f32[4,64,128]{2,1,0:T(8,128)S(1)}, f32[4,64,128]{2,1,0:T(8,128)S(1)}, f32[4,64,128]{2,1,0:T(8,128)S(1)}, f32[4,64,128]{2,1,0:T(8,128)S(1)}, f32...) custom-call(s32[2]{0:T(128)S(1)} %pad_add_fusion.1.refs_0_, ...), custom_call_target="tpu_custom_call" | custom-call | flops 4000 | bytes 1000 | tf_op jit(solution)/shard_map/pallas_call | solution.py:357
  3.1 2.0 %collective-permute-start = (f32[4,4,8,128]{3,2,1,0:T(8,128)S(1)}, f32[4,4,8,128]{3,2,1,0:T(8,128)S(1)}, u32[]{:S(2)}, u32[]{:S(2)}) collective-permute-start(f32[4,4,8,128]{3,2,1,0:T(8,128)S(1)} %get-tuple-element.61), channel_id=1, source_target_pairs={{0,1},{1,0},{2,3},{3,2},{4,5},{5,4},{6,7},{7,6},{8,9},{9,8},{10,11... | collective-permute-start | bytes 196616 | tf_op jit(solution)/shard_map/ppermute | solution.py:369
  5.1 2.8 %collective-permute-start.1 = (f32[4,4,8,128]{3,2,1,0:T(8,128)S(1)}, f32[4,4,8,128]{3,2,1,0:T(8,128)S(1)}, u32[]{:S(2)}, u32[]{:S(2)}) collective-permute-start(f32[4,4,8,128]{3,2,1,0:T(8,128)S(1)} %get-tuple-element.62), channel_id=1, source_target_pairs={{0,3},{1,2},{2,1},{3,0},{4,7},{5,6},{6,5},{7,4},{8,11},{9,10},{10,... | collective-permute-start | bytes 196616 | tf_op jit(solution)/shard_map/ppermute | solution.py:369
  8.0 6.7 %collective-permute-start.3 = (f32[4,64,128]{2,1,0:T(8,128)S(1)}, f32[4,64,128]{2,1,0:T(8,128)S(1)}, u32[]{:S(2)}, u32[]{:S(2)}) collective-permute-start(f32[4,64,128]{2,1,0:T(8,128)S(1)} %get-tuple-element.66.refs_2_.refs_3_), channel_id=1, source_target_pairs={{0,60},{4,8},{8,4},{12,16},{16,12},{20,24},{24,20},{28,32},{32,28}... | collective-permute-start | bytes 393224 | tf_op jit(solution)/shard_map/ppermute | solution.py:369
  16.0 0.7 shard_map.77
  16.7 2.2 %collective-permute-start.2 = (f32[592,128]{1,0:T(8,128)S(1)}, f32[592,128]{1,0:T(8,128)S(1)}, u32[]{:S(2)}, u32[]{:S(2)}) collective-permute-start(f32[592,128]{1,0:T(8,128)S(1)} %get-tuple-element.65), channel_id=1, source_target_pairs={{0,60},{4,8},{8,4},{12,16},{16,12},{20,24},{24,20},{28,32},{32,28}... | collective-permute-start | bytes 909320 | tf_op jit(solution)/shard_map/ppermute | solution.py:369
  18.9 0.1 collective-permute-start.5
  19.1 0.1 pad_maximum_fusion.refs_0_
  19.1 1.0 %collective-permute-done.5.refs_13_ = f32[4,8,128]{2,1,0:T(8,128)S(1)} collective-permute-done((f32[4,8,128]{2,1,0:T(8,128)S(1)}, f32[4,8,128]{2,1,0:T(8,128)S(1)}, u32[]{:S(2)}, u32[]{:S(2)}) %collective-permute-start.5) | collective-permute-done | bytes 16416 | tf_op jit(solution)/shard_map/ppermute | solution.py:369
  20.1 2.4 %shard_map.78 = (f32[4,64,128]{2,1,0:T(8,128)S(1)}, f32[4,64,128]{2,1,0:T(8,128)S(1)}, f32[4,72,128]{2,1,0:T(8,128)S(1)}, f32[4,72,128]{2,1,0:T(8,128)S(1)}, f32...) custom-call(f32[2]{0:T(128)S(1)} %pad_maximum_fusion.refs_0_, ...), custom_call_target="tpu_custom_call" | custom-call | flops 4000 | bytes 1000 | tf_op jit(solution)/shard_map/pallas_call | solution.py:357
  22.5 0.3 collective-permute-start.6
  22.8 0.7 copy-done
  23.5 0.6 dynamic_slice.3
  25.3 0.1 pad_add_fusion.refs_7_.refs_0_
  25.4 1.5 %shard_map.80 = (f32[4,72,128]{2,1,0:T(8,128)S(1)}, f32[4,72,128]{2,1,0:T(8,128)S(1)}, f32[4,72,128]{2,1,0:T(8,128)S(1)}, f32[4,72,128]{2,1,0:T(8,128)S(1)}) custom-call(f32[2]{0:T(128)S(1)} %pad_maximum_fusion.refs_0_, f32[4,72,128]{2,1,0:T(8,128)S(1)} %get-tuple-element.77.refs_8_.refs_1_, f32[4,72,128]{2,1,0:T(8,128)S(1)} %get-tuple-element.79.refs_10_.refs_2_, ...), custom_call_target="tpu_custom_call" | custom-call | flops 4000 | bytes 1000 | tf_op jit(solution)/shard_map/pallas_call | solution.py:357
  26.9 0.4 collective-permute-start.7
  27.3 6.5 %collective-permute-start.9 = (f32[288,128]{1,0:T(8,128)S(1)}, f32[288,128]{1,0:T(8,128)S(1)}, u32[]{:S(2)}, u32[]{:S(2)}) collective-permute-start(f32[288,128]{1,0:T(8,128)S(1)} %get-tuple-element.91), channel_id=1, source_target_pairs={{0,60},{4,8},{8,4},{12,16},{16,12},{20,24},{24,20},{28,32},{32,28}... | collective-permute-start | bytes 442376 | tf_op jit(solution)/shard_map/ppermute | solution.py:369
  33.8 5.0 %collective-permute-done.2.refs_1_ = f32[592,128]{1,0:T(8,128)S(1)} collective-permute-done((f32[592,128]{1,0:T(8,128)S(1)}, f32[592,128]{1,0:T(8,128)S(1)}, u32[]{:S(2)}, u32[]{:S(2)}) %collective-permute-start.2) | collective-permute-done | bytes 303136 | tf_op jit(solution)/shard_map/ppermute | solution.py:369
  38.8 2.5 %shard_map.79 = (f32[4,8,128]{2,1,0:T(8,128)S(1)}, f32[4,72,128]{2,1,0:T(8,128)S(1)}, f32[4,72,128]{2,1,0:T(8,128)S(1)}, f32[4,72,128]{2,1,0:T(8,128)S(1)}, f32[...) custom-call(f32[2]{0:T(128)S(1)} %pad_maximum_fusion.refs_0_, ...), custom_call_target="tpu_custom_call" | custom-call | flops 4000 | bytes 1000 | tf_op jit(solution)/shard_map/pallas_call | solution.py:357
  41.4 2.1 %shard_map.81 = (f32[4,72,128]{2,1,0:T(8,128)S(1)}, f32[4,72,128]{2,1,0:T(8,128)S(1)}, f32[4,72,128]{2,1,0:T(8,128)S(1)}, f32[4,72,128]{2,1,0:T(8,128)S(1)}, f32...) custom-call(f32[2]{0:T(128)S(1)} %pad_maximum_fusion.refs_0_, ...), custom_call_target="tpu_custom_call" | custom-call | flops 4000 | bytes 1000 | tf_op jit(solution)/shard_map/pallas_call | solution.py:357
  43.5 0.1 collective-permute-start.10
  43.6 2.3 %collective-permute-start.8 = (f32[528,128]{1,0:T(8,128)S(1)}, f32[528,128]{1,0:T(8,128)S(1)}, u32[]{:S(2)}, u32[]{:S(2)}) collective-permute-start(f32[528,128]{1,0:T(8,128)S(1)} %get-tuple-element.90), channel_id=1, source_target_pairs={{0,60},{4,8},{8,4},{12,16},{16,12},{20,24},{24,20},{28,32},{32,28}... | collective-permute-start | bytes 811016 | tf_op jit(solution)/shard_map/ppermute | solution.py:369
  45.9 2.2 %shard_map.82 = (f32[4,72,128]{2,1,0:T(8,128)S(1)}, f32[4,72,128]{2,1,0:T(8,128)S(1)}, f32[4,72,128]{2,1,0:T(8,128)S(1)}, f32[4,72,128]{2,1,0:T(8,128)S(1)}, f32...) custom-call(f32[2]{0:T(128)S(1)} %pad_maximum_fusion.refs_0_, f32[288,128]{1,0:T(8,128)S(1)} %collective-permute-done.9.refs_1_, ...), custom_call_target="tpu_custom_call" | custom-call | flops 4000 | bytes 1000 | tf_op jit(solution)/shard_map/pallas_call | solution.py:357
  48.1 1.5 %shard_map.83 = (f32[4,72,128]{2,1,0:T(8,128)S(1)}, f32[4,72,128]{2,1,0:T(8,128)S(1)}, f32[4,72,128]{2,1,0:T(8,128)S(1)}, f32[4,72,128]{2,1,0:T(8,128)S(1)}, f32[2,4,64,128]{3,2,1,0:T(8,128)S(1)}) custom-call(f32[2]{0:T(128)S(1)} %pad_maximum_fusion.refs_0_, f32[4,72,128]{2,1,0:T(8,128)S(1)} %get-tuple-element.96.refs_9_.refs_1_.refs_7_, ...), custom_call_target="tpu_custom_call" | custom-call | flops 4000 | bytes 1000 | tf_op jit(solution)/shard_map/pallas_call | solution.py:357
  49.6 0.6 collective-permute-start.12
  50.2 4.0 %collective-permute-start.13 = (f32[2,4,64,128]{3,2,1,0:T(8,128)S(1)}, f32[2,4,64,128]{3,2,1,0:T(8,128)S(1)}, u32[]{:S(2)}, u32[]{:S(2)}) collective-permute-start(f32[2,4,64,128]{3,2,1,0:T(8,128)S(1)} %get-tuple-element.116.refs_4_), channel_id=1, source_target_pairs={{64,128},{128,64},{65,129},{129,65},{66,130},{130,66},{67,131},{13... | collective-permute-start | bytes 786440 | tf_op jit(solution)/shard_map/ppermute | solution.py:369
  54.2 0.3 collective-permute-start.11
  54.5 1.4 %collective-permute-done.11.refs_6_ = f32[4,72,128]{2,1,0:T(8,128)S(1)} collective-permute-done((f32[4,72,128]{2,1,0:T(8,128)S(1)}, f32[4,72,128]{2,1,0:T(8,128)S(1)}, u32[]{:S(2)}, u32[]{:S(2)}) %collective-permute-start.11) | collective-permute-done | bytes 147488 | tf_op jit(solution)/shard_map/ppermute | solution.py:369
  55.9 0.9 %shard_map.84 = (f32[4,64,128]{2,1,0:T(8,128)S(1)}, f32[4,64,128]{2,1,0:T(8,128)S(1)}, f32[8,128]{1,0:T(8,128)S(1)}) custom-call(f32[2]{0:T(128)S(1)} %pad_maximum_fusion.refs_0_, f32[4,72,128]{2,1,0:T(8,128)S(1)} %get-tuple-element.103.refs_1_.refs_8_, f32[4,72,128]{2,1,0:T(8,128)S(1)} %get-tuple-element.108.refs_2_.refs_10_, ...), custom_call_target="tpu_custom_call" | custom-call | flops 4000 | bytes 1000 | tf_op jit(solution)/shard_map/pallas_call | solution.py:357
  56.8 4.1 %collective-permute-done.8.refs_1_ = f32[528,128]{1,0:T(8,128)S(1)} collective-permute-done((f32[528,128]{1,0:T(8,128)S(1)}, f32[528,128]{1,0:T(8,128)S(1)}, u32[]{:S(2)}, u32[]{:S(2)}) %collective-permute-start.8) | collective-permute-done | bytes 270368 | tf_op jit(solution)/shard_map/ppermute | solution.py:369
  60.9 2.5 %shard_map.85 = (f32[6,4,64,128]{3,2,1,0:T(8,128)S(1)}, f32[8,128]{1,0:T(8,128)S(1)}) custom-call(f32[2]{0:T(128)S(1)} %pad_maximum_fusion.refs_0_, f32[528,128]{1,0:T(8,128)S(1)} %collective-permute-done.8.refs_1_, f32[4,72,128]{2,1,0:T(8,128)S(1)} %get-tuple-element.99.refs_7_.refs_2_, f32[4,72,128]{2,1,0:T(8,128)S(1)} %get-tuple-element.100.refs_3_, ...), custom_call_target="tpu_custom_call" | custom-call | flops 4000 | bytes 1000 | tf_op jit(solution)/shard_map/pallas_call | solution.py:357
  63.3 0.6 collective-permute-start.14
  64.0 4.0 %collective-permute-start.15 = (f32[6,4,64,128]{3,2,1,0:T(8,128)S(1)}, f32[6,4,64,128]{3,2,1,0:T(8,128)S(1)}, u32[]{:S(2)}, u32[]{:S(2)}) collective-permute-start(f32[6,4,64,128]{3,2,1,0:T(8,128)S(1)} %get-tuple-element.117.refs_1_), channel_id=1, source_target_pairs={{64,128},{128,64},{65,129},{129,65},{66,130},{130,66},{67,131},{13... | collective-permute-start | bytes 2359304 | tf_op jit(solution)/shard_map/ppermute | solution.py:369
  68.0 0.1 collective-permute-start.16
  68.1 1.2 %collective-permute-done.16 = f32[8,128]{1,0:T(8,128)S(1)} collective-permute-done((f32[8,128]{1,0:T(8,128)S(1)}, f32[8,128]{1,0:T(8,128)S(1)}, u32[]{:S(2)}, u32[]{:S(2)}) %collective-permute-start.16) | collective-permute-done | bytes 4128 | tf_op jit(solution)/shard_map/ppermute | solution.py:369
  69.3 3.6 %collective-permute-done.17 = f32[8,128]{1,0:T(8,128)S(1)} collective-permute-done((f32[8,128]{1,0:T(8,128)S(1)}, f32[8,128]{1,0:T(8,128)S(1)}, u32[]{:S(2)}, u32[]{:S(2)}) %collective-permute-start.17) | collective-permute-done | bytes 4128 | tf_op jit(solution)/shard_map/ppermute | solution.py:479
  72.9 4.8 %collective-permute-done.18 = f32[8,128]{1,0:T(8,128)S(1)} collective-permute-done((f32[8,128]{1,0:T(8,128)S(1)}, f32[8,128]{1,0:T(8,128)S(1)}, u32[]{:S(2)}, u32[]{:S(2)}) %collective-permute-start.18) | collective-permute-done | bytes 4128 | tf_op jit(solution)/shard_map/ppermute | solution.py:479
  77.7 3.6 %collective-permute-done.19 = f32[8,128]{1,0:T(8,128)S(1)} collective-permute-done((f32[8,128]{1,0:T(8,128)S(1)}, f32[8,128]{1,0:T(8,128)S(1)}, u32[]{:S(2)}, u32[]{:S(2)}) %collective-permute-start.19) | collective-permute-done | bytes 4128 | tf_op jit(solution)/shard_map/ppermute | solution.py:479
  81.3 0.5 collective-permute-start.20
  81.8 1.2 %collective-permute-done.15.refs_3_ = f32[6,4,64,128]{3,2,1,0:T(8,128)S(1)} collective-permute-done((f32[6,4,64,128]{3,2,1,0:T(8,128)S(1)}, f32[6,4,64,128]{3,2,1,0:T(8,128)S(1)}, u32[]{:S(2)}, u32[]{:S(2)}) %collective-permute-start.15) | collective-permute-done | bytes 786464 | tf_op jit(solution)/shard_map/ppermute | solution.py:369
  83.0 1.4 %shard_map.86 = f32[4,256,128]{2,1,0:T(8,128)} custom-call(s32[2]{0:T(128)S(1)} %pad_add_fusion.refs_7_.refs_0_, f32[6,4,64,128]{3,2,1,0:T(8,128)S(1)} %get-tuple-element.117.refs_1_, f32[6,4,64,128]{3,2,1,0:T(8,128)S(1)} %collective-permute-done.14.refs_2_, f32[6,4,64,128]{3,2,1,0:T(8,128)S(1)} %collective-permute-done.15.refs_3_, ...), custom_call_target="tpu_custom_call" | custom-call | flops 4000 | bytes 1000 | tf_op jit(solution)/shard_map/pallas_call | solution.py:357
  84.5 1.4 %collective-permute-done.20.refs_1_ = f32[8,128]{1,0:T(8,128)S(1)} collective-permute-done((f32[8,128]{1,0:T(8,128)S(1)}, f32[8,128]{1,0:T(8,128)S(1)}, u32[]{:S(2)}, u32[]{:S(2)}) %collective-permute-start.20) | collective-permute-done | bytes 4128 | tf_op jit(solution)/shard_map/ppermute | solution.py:479
  85.8 0.2 collective-permute-start.21
  86.1 1.4 %shard_map.87 = f32[4,256,128]{2,1,0:T(8,128)} custom-call(s32[2]{0:T(128)S(1)} %pad_add_fusion.refs_7_.refs_0_, f32[6,4,64,128]{3,2,1,0:T(8,128)S(1)} %get-tuple-element.117.refs_1_, f32[6,4,64,128]{3,2,1,0:T(8,128)S(1)} %collective-permute-done.14.refs_2_, f32[6,4,64,128]{3,2,1,0:T(8,128)S(1)} %collective-permute-done.15.refs_3_), custom_call_target="tpu_custom_call" | custom-call | flops 4000 | bytes 1000 | tf_op jit(solution)/shard_map/pallas_call | solution.py:357
  87.5 3.2 %collective-permute-done.21.refs_1_ = f32[8,128]{1,0:T(8,128)S(1)} collective-permute-done((f32[8,128]{1,0:T(8,128)S(1)}, f32[8,128]{1,0:T(8,128)S(1)}, u32[]{:S(2)}, u32[]{:S(2)}) %collective-permute-start.21) | collective-permute-done | bytes 4128 | tf_op jit(solution)/shard_map/ppermute | solution.py:479
  90.7 0.1 slice_reduce_fusion
  90.8 0.5 multiply_bitcast_fusion
  (22 shorter events, 0.1 us)
Async XLA Ops:
  3.1 12.9 %collective-permute-start = (f32[4,4,8,128]{3,2,1,0:T(8,128)S(1)}, f32[4,4,8,128]{3,2,1,0:T(8,128)S(1)}, u32[]{:S(2)}, u32[]{:S(2)}) collective-permute-start(f32[4,4,8,128]{3,2,1,0:T(8,128)S(1)} %get-tuple-element.61), channel_id=1, source_target_pairs={{0,1},{1,0},{2,3},{3,2},{4,5},{5,4},{6,7},{7,6},{8,9},{9,8},{10,11... | collective-permute-start | bytes 196616 | tf_op jit(solution)/shard_map/ppermute | solution.py:369
  5.1 10.9 %collective-permute-start.1 = (f32[4,4,8,128]{3,2,1,0:T(8,128)S(1)}, f32[4,4,8,128]{3,2,1,0:T(8,128)S(1)}, u32[]{:S(2)}, u32[]{:S(2)}) collective-permute-start(f32[4,4,8,128]{3,2,1,0:T(8,128)S(1)} %get-tuple-element.62), channel_id=1, source_target_pairs={{0,3},{1,2},{2,1},{3,0},{4,7},{5,6},{6,5},{7,4},{8,11},{9,10},{10,... | collective-permute-start | bytes 196616 | tf_op jit(solution)/shard_map/ppermute | solution.py:369
  8.0 12.2 %collective-permute-start.3 = (f32[4,64,128]{2,1,0:T(8,128)S(1)}, f32[4,64,128]{2,1,0:T(8,128)S(1)}, u32[]{:S(2)}, u32[]{:S(2)}) collective-permute-start(f32[4,64,128]{2,1,0:T(8,128)S(1)} %get-tuple-element.66.refs_2_.refs_3_), channel_id=1, source_target_pairs={{0,60},{4,8},{8,4},{12,16},{16,12},{20,24},{24,20},{28,32},{32,28}... | collective-permute-start | bytes 393224 | tf_op jit(solution)/shard_map/ppermute | solution.py:369
  14.7 5.4 %collective-permute-start.4 = (f32[4,64,128]{2,1,0:T(8,128)S(1)}, f32[4,64,128]{2,1,0:T(8,128)S(1)}, u32[]{:S(2)}, u32[]{:S(2)}) collective-permute-start(f32[4,64,128]{2,1,0:T(8,128)S(1)} %get-tuple-element.70.refs_5_), channel_id=1, source_target_pairs={{0,4},{4,0},{8,12},{12,8},{16,20},{20,16},{24,28},{28,24},{32,36},... | collective-permute-start | bytes 393224 | tf_op jit(solution)/shard_map/ppermute | solution.py:369
  16.7 22.1 %collective-permute-start.2 = (f32[592,128]{1,0:T(8,128)S(1)}, f32[592,128]{1,0:T(8,128)S(1)}, u32[]{:S(2)}, u32[]{:S(2)}) collective-permute-start(f32[592,128]{1,0:T(8,128)S(1)} %get-tuple-element.65), channel_id=1, source_target_pairs={{0,60},{4,8},{8,4},{12,16},{16,12},{20,24},{24,20},{28,32},{32,28}... | collective-permute-start | bytes 909320 | tf_op jit(solution)/shard_map/ppermute | solution.py:369
  18.9 1.2 %collective-permute-start.5 = (f32[4,8,128]{2,1,0:T(8,128)S(1)}, f32[4,8,128]{2,1,0:T(8,128)S(1)}, u32[]{:S(2)}, u32[]{:S(2)}) collective-permute-start(f32[4,8,128]{2,1,0:T(8,128)S(1)} %get-tuple-element.74), channel_id=1, source_target_pairs={{0,4},{4,0},{8,12},{12,8},{16,20},{20,16},{24,28},{28,24},{32,36},... | collective-permute-start | bytes 49160 | tf_op jit(solution)/shard_map/ppermute | solution.py:369
  22.5 2.9 %collective-permute-start.6 = (f32[4,72,128]{2,1,0:T(8,128)S(1)}, f32[4,72,128]{2,1,0:T(8,128)S(1)}, u32[]{:S(2)}, u32[]{:S(2)}) collective-permute-start(f32[4,72,128]{2,1,0:T(8,128)S(1)} %get-tuple-element.84.refs_4_), channel_id=1, source_target_pairs={{0,4},{4,0},{8,12},{12,8},{16,20},{20,16},{24,28},{28,24},{32,36},... | collective-permute-start | bytes 442376 | tf_op jit(solution)/shard_map/ppermute | solution.py:369
  22.8 0.7 copy-start
  26.9 14.5 %collective-permute-start.7 = (f32[4,72,128]{2,1,0:T(8,128)S(1)}, f32[4,72,128]{2,1,0:T(8,128)S(1)}, u32[]{:S(2)}, u32[]{:S(2)}) collective-permute-start(f32[4,72,128]{2,1,0:T(8,128)S(1)} %get-tuple-element.88.refs_6_), channel_id=1, source_target_pairs={{0,4},{4,0},{8,12},{12,8},{16,20},{20,16},{24,28},{28,24},{32,36},... | collective-permute-start | bytes 442376 | tf_op jit(solution)/shard_map/ppermute | solution.py:369
  27.3 18.6 %collective-permute-start.9 = (f32[288,128]{1,0:T(8,128)S(1)}, f32[288,128]{1,0:T(8,128)S(1)}, u32[]{:S(2)}, u32[]{:S(2)}) collective-permute-start(f32[288,128]{1,0:T(8,128)S(1)} %get-tuple-element.91), channel_id=1, source_target_pairs={{0,60},{4,8},{8,4},{12,16},{16,12},{20,24},{24,20},{28,32},{32,28}... | collective-permute-start | bytes 442376 | tf_op jit(solution)/shard_map/ppermute | solution.py:369
  43.5 4.6 %collective-permute-start.10 = (f32[4,72,128]{2,1,0:T(8,128)S(1)}, f32[4,72,128]{2,1,0:T(8,128)S(1)}, u32[]{:S(2)}, u32[]{:S(2)}) collective-permute-start(f32[4,72,128]{2,1,0:T(8,128)S(1)} %get-tuple-element.106.refs_4_), channel_id=1, source_target_pairs={{0,4},{4,0},{8,12},{12,8},{16,20},{20,16},{24,28},{28,24},{32,36},... | collective-permute-start | bytes 442376 | tf_op jit(solution)/shard_map/ppermute | solution.py:369
  43.6 17.3 %collective-permute-start.8 = (f32[528,128]{1,0:T(8,128)S(1)}, f32[528,128]{1,0:T(8,128)S(1)}, u32[]{:S(2)}, u32[]{:S(2)}) collective-permute-start(f32[528,128]{1,0:T(8,128)S(1)} %get-tuple-element.90), channel_id=1, source_target_pairs={{0,60},{4,8},{8,4},{12,16},{16,12},{20,24},{24,20},{28,32},{32,28}... | collective-permute-start | bytes 811016 | tf_op jit(solution)/shard_map/ppermute | solution.py:369
  49.6 11.3 %collective-permute-start.12 = (f32[2,4,64,128]{3,2,1,0:T(8,128)S(1)}, f32[2,4,64,128]{3,2,1,0:T(8,128)S(1)}, u32[]{:S(2)}, u32[]{:S(2)}) collective-permute-start(f32[2,4,64,128]{3,2,1,0:T(8,128)S(1)} %get-tuple-element.116.refs_4_), channel_id=1, source_target_pairs={{0,64},{64,0},{128,192},{192,128},{1,65},{65,1},{129,193},{193,129... | collective-permute-start | bytes 786440 | tf_op jit(solution)/shard_map/ppermute | solution.py:369
  50.2 10.7 %collective-permute-start.13 = (f32[2,4,64,128]{3,2,1,0:T(8,128)S(1)}, f32[2,4,64,128]{3,2,1,0:T(8,128)S(1)}, u32[]{:S(2)}, u32[]{:S(2)}) collective-permute-start(f32[2,4,64,128]{3,2,1,0:T(8,128)S(1)} %get-tuple-element.116.refs_4_), channel_id=1, source_target_pairs={{64,128},{128,64},{65,129},{129,65},{66,130},{130,66},{67,131},{13... | collective-permute-start | bytes 786440 | tf_op jit(solution)/shard_map/ppermute | solution.py:369
  54.2 1.6 %collective-permute-start.11 = (f32[4,72,128]{2,1,0:T(8,128)S(1)}, f32[4,72,128]{2,1,0:T(8,128)S(1)}, u32[]{:S(2)}, u32[]{:S(2)}) collective-permute-start(f32[4,72,128]{2,1,0:T(8,128)S(1)} %get-tuple-element.110.refs_4_), channel_id=1, source_target_pairs={{0,4},{4,0},{8,12},{12,8},{16,20},{20,16},{24,28},{28,24},{32,36},... | collective-permute-start | bytes 442376 | tf_op jit(solution)/shard_map/ppermute | solution.py:369
  63.3 18.5 %collective-permute-start.14 = (f32[6,4,64,128]{3,2,1,0:T(8,128)S(1)}, f32[6,4,64,128]{3,2,1,0:T(8,128)S(1)}, u32[]{:S(2)}, u32[]{:S(2)}) collective-permute-start(f32[6,4,64,128]{3,2,1,0:T(8,128)S(1)} %get-tuple-element.117.refs_1_), channel_id=1, source_target_pairs={{0,64},{64,0},{128,192},{192,128},{1,65},{65,1},{129,193},{193,129... | collective-permute-start | bytes 2359304 | tf_op jit(solution)/shard_map/ppermute | solution.py:369
  64.0 19.1 %collective-permute-start.15 = (f32[6,4,64,128]{3,2,1,0:T(8,128)S(1)}, f32[6,4,64,128]{3,2,1,0:T(8,128)S(1)}, u32[]{:S(2)}, u32[]{:S(2)}) collective-permute-start(f32[6,4,64,128]{3,2,1,0:T(8,128)S(1)} %get-tuple-element.117.refs_1_), channel_id=1, source_target_pairs={{64,128},{128,64},{65,129},{129,65},{66,130},{130,66},{67,131},{13... | collective-permute-start | bytes 2359304 | tf_op jit(solution)/shard_map/ppermute | solution.py:369
  68.0 1.3 %collective-permute-start.16 = (f32[8,128]{1,0:T(8,128)S(1)}, f32[8,128]{1,0:T(8,128)S(1)}, u32[]{:S(2)}, u32[]{:S(2)}) collective-permute-start(f32[8,128]{1,0:T(8,128)S(1)} %get-tuple-element.118), channel_id=1, source_target_pairs={{0,4},{4,0},{8,12},{12,8},{16,20},{20,16},{24,28},{28,24},{32,36},... | collective-permute-start | bytes 12296 | tf_op jit(solution)/shard_map/ppermute | solution.py:369
  69.3 3.6 %collective-permute-start.17 = (f32[8,128]{1,0:T(8,128)S(1)}, f32[8,128]{1,0:T(8,128)S(1)}, u32[]{:S(2)}, u32[]{:S(2)}) collective-permute-start(f32[8,128]{1,0:T(8,128)S(1)} %add.25), channel_id=1, source_target_pairs={{0,16},{4,20},{8,24},{12,28},{16,0},{20,4},{24,8},{28,12},{32,48},... | collective-permute-start | bytes 12296 | tf_op jit(solution)/shard_map/ppermute | solution.py:479
  72.9 4.8 %collective-permute-start.18 = (f32[8,128]{1,0:T(8,128)S(1)}, f32[8,128]{1,0:T(8,128)S(1)}, u32[]{:S(2)}, u32[]{:S(2)}) collective-permute-start(f32[8,128]{1,0:T(8,128)S(1)} %add.26), channel_id=1, source_target_pairs={{0,48},{4,52},{8,56},{12,60},{16,32},{20,36},{24,40},{28,44},{32,1... | collective-permute-start | bytes 12296 | tf_op jit(solution)/shard_map/ppermute | solution.py:479
  77.7 3.6 %collective-permute-start.19 = (f32[8,128]{1,0:T(8,128)S(1)}, f32[8,128]{1,0:T(8,128)S(1)}, u32[]{:S(2)}, u32[]{:S(2)}) collective-permute-start(f32[8,128]{1,0:T(8,128)S(1)} %add.27), channel_id=1, source_target_pairs={{0,1},{1,0},{2,3},{3,2},{4,5},{5,4},{6,7},{7,6},{8,9},{9,8},{10,11... | collective-permute-start | bytes 12296 | tf_op jit(solution)/shard_map/ppermute | solution.py:479
  81.3 4.5 %collective-permute-start.20 = (f32[8,128]{1,0:T(8,128)S(1)}, f32[8,128]{1,0:T(8,128)S(1)}, u32[]{:S(2)}, u32[]{:S(2)}) collective-permute-start(f32[8,128]{1,0:T(8,128)S(1)} %add.28.refs_0_), channel_id=1, source_target_pairs={{0,2},{1,3},{2,0},{3,1},{4,6},{5,7},{6,4},{7,5},{8,10},{9,11},{10,... | collective-permute-start | bytes 12296 | tf_op jit(solution)/shard_map/ppermute | solution.py:479
  85.8 4.8 %collective-permute-start.21 = (f32[8,128]{1,0:T(8,128)S(1)}, f32[8,128]{1,0:T(8,128)S(1)}, u32[]{:S(2)}, u32[]{:S(2)}) collective-permute-start(f32[8,128]{1,0:T(8,128)S(1)} %shard_map.88.refs_0_), channel_id=1, source_target_pairs={{0,11},{1,10},{2,9},{3,8},{4,15},{5,14},{6,13},{7,12},{8,3},{9,2},... | collective-permute-start | bytes 12296 | tf_op jit(solution)/shard_map/ppermute | solution.py:479

commit v2 on v1

v2 whole, which is shorter than its diff:
```python
import functools

import jax
import jax.numpy as jnp
from jax import lax
from jax.experimental import pallas as pl
from jax.experimental.pallas import tpu as pltpu
from jax.sharding import PartitionSpec as P

LEAPS = 4
STEP = 0.05
COMPS = 4
NZ = 64
OCT = NZ // 8
WIDE = 4
LANES = 128
SITES = COMPS * NZ


def f32(*shape):
    return jax.ShapeDtypeStruct(shape, jnp.float32)


def lanes():
    return lax.broadcasted_iota(jnp.int32, (8, LANES), 1)


def rows():
    return lax.broadcasted_iota(jnp.int32, (8, LANES), 0)


def packed(load):
    octet = lanes() // 16
    out = None
    for o in range(OCT):
        moved = pltpu.roll(load(o), (16 * o + 8) % LANES, 1)
        out = moved if out is None else jnp.where(octet == o, moved, out)
    return out


def layer_of(main, edge=None):
    return (lambda c, o: main[c, 8 * o : 8 * o + 8, :], None if edge is None else (lambda c: edge[c]))


def joint(ref):
    return (lambda c, o: ref[c, 8 * o : 8 * o + 8, :], lambda c: ref[c, NZ : NZ + 8, :])


def store_main(q, p):
    def put(c, o, new_p, new_q):
        if p is not None:
            p[c, 8 * o : 8 * o + 8, :] = new_p
        if q is not None:
            q[c, 8 * o : 8 * o + 8, :] = new_q

    return put


def store_edge(q, p):
    def put(c, new_p, new_q):
        p[c, NZ : NZ + 8, :] = new_p
        q[c, NZ : NZ + 8, :] = new_q

    return put


def settings(ref):
    row = lax.broadcasted_iota(jnp.int32, (LANES, LANES), 0)
    lane = lax.broadcasted_iota(jnp.int32, (LANES, LANES), 1)
    mix = jnp.where(jnp.abs(row - lane) == 1, 1.0, 0.0).astype(jnp.bfloat16)
    return (ref[0], ref[1], jnp.concatenate([mix, mix], axis=0))


def main_eval(down, here, up, mom, put, par, dt, energy):
    kap, qua, mix = par
    lane, row = (lanes(), rows())
    zero_lane, last_lane = (lane == 0, lane == LANES - 1)
    first_row, last_row = (row == 0, row == 7)
    nsums = {}
    for c in range(COMPS):
        cells = [here[0](c, o) for o in range(OCT)]
        edge = here[1](c)
        whole = jnp.concatenate(cells, axis=0)
        high = whole.astype(jnp.bfloat16)
        low = (whole - high.astype(jnp.float32)).astype(jnp.bfloat16)
        beside = jnp.dot(jnp.concatenate([high, low], axis=1), mix, preferred_element_type=jnp.float32)
        left = [pltpu.roll(edge, (121 - 16 * o) % LANES, 1) for o in range(OCT)]
        right = [pltpu.roll(edge, (119 - 16 * o) % LANES, 1) for o in range(OCT)]
        above = [pltpu.roll(q, 7, 0) for q in cells]
        below = [pltpu.roll(q, 1, 0) for q in cells]
        for o in range(OCT):
            z_up = jnp.where(last_row, above[(o + 1) % OCT], above[o])
            z_down = jnp.where(first_row, below[o - 1], below[o])
            ghost = jnp.where(zero_lane, left[o], jnp.where(last_lane, right[o], 0.0))
            y_sum = beside[8 * o : 8 * o + 8] + ghost
            nsums[c, o] = (down[0](c, o) + up[0](c, o)) + y_sum + (z_up + z_down)
    waiting = []
    for o in range(OCT):
        cells = [here[0](c, o) for c in range(COMPS)]
        moms = [mom[0](c, o) for c in range(COMPS)]
        square = cells[0] * cells[0]
        for c in range(1, COMPS):
            square = square + cells[c] * cells[c]
        coef = (2.0 - 4.0 * qua) + (4.0 * qua) * square
        dots = None
        results = []
        for c in range(COMPS):
            q, p, nsum = (cells[c], moms[c], nsums[c, o])
            new = p + dt * ((2.0 * kap) * nsum - coef * q)
            results.append((new, q + STEP * new))
            if energy is not None:
                dots = q * nsum if dots is None else dots + q * nsum
                kin = new if energy[1] else p
                energy[0] = energy[0] + 0.5 * (kin * kin)
        if energy is not None:
            energy[0] = energy[0] + (square - kap * dots + qua * ((square - 1.0) * (square - 1.0)))
        waiting.append((o, results))
        while len(waiting) > (2 if o < OCT - 1 else 0):
            at, ready = waiting.pop(0)
            for c in range(COMPS):
                put(c, at, *ready[c])


def edge_eval(jobs, par, dt):
    kap, qua, _ = par
    lane, row = (lanes(), rows())
    slot = lane % 16
    first_row, last_row = (row == 0, row == 7)
    results = []
    for down, here, up, mom, _ in jobs:
        cells = [here[1](c) for c in range(COMPS)]
        square = cells[0] * cells[0]
        for c in range(1, COMPS):
            square = square + cells[c] * cells[c]
        coef = (2.0 - 4.0 * qua) + (4.0 * qua) * square
        for c in range(COMPS):
            q = cells[c]
            own = packed(lambda o: here[0](c, o))
            right = pltpu.roll(jnp.where(slot == 8, own, q), LANES - 1, 1)
            left = pltpu.roll(jnp.where(slot == 7, own, q), 1, 1)
            above = pltpu.roll(q, 7, 0)
            below = pltpu.roll(q, 1, 0)
            z_up = jnp.where(last_row, pltpu.roll(above, LANES - 16, 1), above)
            z_down = jnp.where(first_row, pltpu.roll(below, 16, 1), below)
            nsum = (down[1](c) + up[1](c)) + (left + right) + (z_up + z_down)
            new = mom[1](c) + dt * ((2.0 * kap) * nsum - coef * q)
            results.append((new, q + STEP * new))

    def store():
        for job, (*_, put) in enumerate(jobs):
            for c in range(COMPS):
                put(c, *results[job * COMPS + c])

    return store


def ingest_kernel(flags, field, momenta, *refs):
    mains, messages, (held, sems) = ((refs[:4], refs[4:8]), refs[8:10], refs[10:])
    copies = {
        (k, c): pltpu.make_async_copy(src.at[c], held.at[k, c], sems.at[k, c])
        for c in range(COMPS)
        for k, src in enumerate((field, momenta))
    }
    for copy in copies.values():
        copy.start()
    low = lanes() % 16 < 8
    odd = flags[1] == 1
    mirrored = jnp.broadcast_to(flags[0, :1, :], (NZ, LANES)) == 1
    for c in range(COMPS):
        copies[0, c].wait()
        copies[1, c].wait()
        lines = [[held[k, c, pl.ds(x, NZ, stride=WIDE), :] for x in range(WIDE)] for k in range(2)]
        for u in range(WIDE):
            packs = []
            for k in range(2):
                value = jnp.where(mirrored, lines[k][WIDE - 1 - u], lines[k][u])
                mains[k][u][c] = value
                packs.append(packed(lambda o: value[8 * o : 8 * o + 8, :]))
            right = jnp.where(low, packs[0], pltpu.roll(packs[1], 8, 1))
            left = jnp.where(low, pltpu.roll(packs[0], LANES - 8, 1), packs[1])
            messages[0][u, c] = jnp.where(odd, left, right)
            messages[1][u, c] = jnp.where(odd, right, left)


def ghost_kernel(flags, first, second, m1, k0, qg, pg, near, far):
    low = lanes() % 16 < 8
    odd = flags[1] == 1
    for u in range(WIDE):
        for c in range(COMPS):
            left = jnp.where(odd, first[u, c], second[u, c])
            right = jnp.where(odd, second[u, c], first[u, c])
            q = jnp.where(low, left, pltpu.roll(right, 8, 1))
            p = jnp.where(low, pltpu.roll(left, LANES - 8, 1), right)
            qg[u, c] = q
            pg[u, c] = p
            if u == WIDE - 1:
                near[c] = q
    write_main(far, 0, lambda c, o: m1[c, 8 * o : 8 * o + 8, :])
    write_main(far, SITES, lambda c, o: k0[c, 8 * o : 8 * o + 8, :])
    write_edge(far, 2 * SITES, lambda c: qg[0, c])
    write_edge(far, 2 * SITES + 16, lambda c: qg[1, c])
    write_edge(far, 2 * SITES + 32, lambda c: pg[0, c])


def fresh():
    return jnp.zeros((8, LANES), jnp.float32)


def step(around, moms, outs, par, dt, energy=None, edges=True):
    spans = [around[i : i + 3] for i in range(len(moms))]
    store = None
    if edges:
        jobs = [(*span, mom, store_edge(*out)) for span, mom, out in zip(spans, moms, outs)]
        store = edge_eval(jobs, par, dt)
    for span, mom, out in zip(spans, moms, outs):
        main_eval(*span, mom, store_main(*out), par, dt, energy)
    if edges:
        store()


def inside(ref, main, edge):
    def ghosts(c):
        value = ref[edge + 8 * (c % 2) : edge + 8 * (c % 2) + 8, :]
        return value if c < 2 else pltpu.roll(value, LANES - 8, 1)

    return (lambda c, o: ref[main + NZ * c + 8 * o : main + NZ * c + 8 * o + 8, :], ghosts)


def write_main(ref, main, load):
    for c in range(COMPS):
        for o in range(OCT):
            ref[main + NZ * c + 8 * o : main + NZ * c + 8 * o + 8, :] = load(c, o)


def write_edge(ref, edge, load):
    slot = lanes() % 16
    for c in range(2):
        both = jnp.where((slot >= 4) & (slot < 12), load(c), pltpu.roll(load(c + 2), 8, 1))
        ref[edge + 8 * c : edge + 8 * c + 8, :] = both


def inner_start(
    par, far, m0, m1, m2, m3, k0, k1, k2, k3, qg, pg, near, near_g, z, zp, q1, p1, q2, p2, q3, p3, energy, msg, msg_near
):
    par = settings(par)
    around = [layer_of(main, qg.at[u]) for u, main in enumerate((m0, m1, m2, m3))] + [layer_of(near, near_g)]
    total = [fresh(), False]
    held = [layer_of(mom, pg.at[u + 1]) for u, mom in enumerate((k1, k2, k3))]
    step(around, held, [(q1, p1), (q2, p2), (q3, p3)], par, 0.5 * STEP, total)
    write_main(msg, 0, joint(q1)[0])
    write_edge(msg, SITES, joint(q1)[1])
    write_main(msg_near, 0, joint(q3)[0])
    write_edge(msg_near, SITES, joint(q3)[1])
    store = store_main(z, zp)
    main_eval(layer_of(far), around[0], around[1], layer_of(k0), store, par, 0.5 * STEP, total)
    energy[...] = total[0]


def outer_first(par, beyond, far, m0, qg, pg, z, zp, q1, p1, q2, zg, n1, r1, hq, hp, nz, nzp, zpg):
    par = settings(par)
    outer, halo = (inside(beyond, 0, 2 * SITES + 16), inside(beyond, 0, 2 * SITES))
    halo = (layer_of(far)[0], halo[1])
    here = layer_of(m0, qg.at[0])

    def put(c, new_p, new_q):
        zpg[c] = new_p
        zg[c] = new_q

    edge_eval([(halo, here, (None, lambda c: qg[1, c]), (None, lambda c: pg[0, c]), put)], par, 0.5 * STEP)()
    step([outer, halo, here], [inside(beyond, SITES, 2 * SITES + 32)], [(hq, hp)], par, 0.5 * STEP)
    step([layer_of(z, zg), joint(q1), joint(q2)], [joint(p1)], [(n1, r1)], par, STEP)
    step([joint(hq), layer_of(z, zg), joint(q1)], [layer_of(zp, zpg)], [(nz, nzp)], par, STEP)


def inner_second(par, z, q1, p1, q2, p2, q3, p3, near, n1, r1, n2, r2, n3, r3, msg, msg_near):
    around = [joint(z), joint(q1), joint(q2), joint(q3), inside(near, 0, SITES)]
    moms = [joint(p1), joint(p2), joint(p3)]
    step(around, moms, [(n1, r1), (n2, r2), (n3, r3)], settings(par), STEP)
    write_main(msg, 0, joint(q1)[0])
    write_edge(msg, SITES, joint(q1)[1])
    write_main(msg, SITES + 16, joint(n1)[0])
    write_main(msg_near, 0, joint(n3)[0])
    write_edge(msg_near, SITES, joint(n3)[1])


def outer_kernel(par, beyond, hq, hp, zold, zold_g, z, zp, old1, q1, p1, q2, nhq, nhp, nz, nzp, n1, r1):
    par = settings(par)
    step([inside(beyond, 0, SITES), joint(hq), layer_of(zold, zold_g)], [joint(hp)], [(nhq, nhp)], par, STEP)
    step([joint(nhq), joint(z), joint(old1)], [joint(zp)], [(nz, nzp)], par, STEP)
    step([joint(nz), joint(q1), joint(q2)], [joint(p1)], [(n1, r1)], par, STEP)


def inner_kernel(par, q1, q2, p2, q3, p3, near, n2, r2, n3, r3, msg):
    around = [joint(q1), joint(q2), joint(q3), inside(near, 0, SITES)]
    step(around, [joint(p2), joint(p3)], [(n2, r2), (n3, r3)], settings(par), STEP)
    write_main(msg, 0, joint(n3)[0])
    write_edge(msg, SITES, joint(n3)[1])


def inner_third(par, q1, q2, p2, q3, p3, near, n2, r2, n3, r3, msg, whole):
    around = [joint(q1), joint(q2), joint(q3), inside(near, 0, SITES)]
    step(around, [joint(p2), joint(p3)], [(n2, r2), (n3, r3)], settings(par), STEP)
    write_main(msg, 0, joint(n3)[0])
    for u, ref in enumerate((n2, n3)):
        for c in range(COMPS):
            whole[u, c] = ref[c, :NZ, :]


def inner_final(par, q1, q2, p2, q3, p3, near, r2, r3, energy):
    around = [joint(q1), joint(q2), joint(q3), inside(near, 0, 0)]
    total = [fresh(), True]
    outs = [(None, r2), (None, r3)]
    step(around, [joint(p2), joint(p3)], outs, settings(par), 0.5 * STEP, total, False)
    energy[...] = total[0]


def outer_last(
    par, beyond, hq, hp, zold, z, zp, old1, q1, p1, q2, r2, r3, start, more,
    whole, energy, nhq, nhp, nz, nzp, last,
):
    par = settings(par)
    step([inside(beyond, 0, SITES), joint(hq), joint(zold)], [joint(hp)], [(nhq, nhp)], par, STEP)
    step([joint(nhq), joint(z), joint(old1)], [joint(zp)], [(nz, nzp)], par, STEP)
    store = store_main(last, None)
    outer = inside(beyond, SITES + 16, 0)
    main_eval(outer, joint(nhq), joint(z), joint(nhp), store, par, STEP, None)
    total = [more[...], True]
    store = store_main(None, whole.at[2])
    main_eval(layer_of(last), joint(nz), joint(q1), joint(nzp), store, par, 0.5 * STEP, total)
    store = store_main(None, whole.at[3])
    main_eval(joint(nz), joint(q1), joint(q2), joint(p1), store, par, 0.5 * STEP, total)
    before = jnp.sum(start[...], axis=0, keepdims=True)
    after = jnp.sum(total[0], axis=0, keepdims=True)
    row = rows()
    energy[...] = jnp.where(row == 0, before, jnp.where(row == 1, after, 0.0))
    for c in range(COMPS):
        whole[0, c] = nz[c, :NZ, :]
        whole[1, c] = q1[c, :NZ, :]
        whole[4, c] = r2[c]
        whole[5, c] = r3[c]


def place_kernel(choice, *refs):
    late, early, (new_q, new_p, held, sems) = (refs[:3], refs[3:6], refs[6:])
    mirrored, first, second = (jnp.broadcast_to(choice[i, :1, :], (NZ, LANES)) == 1 for i in range(3))

    def picked(sources, u, c):
        return jnp.where(first, sources[1][u, c], jnp.where(second, sources[2][u, c], sources[0][u, c]))

    copies = []
    for k, out in enumerate((new_q, new_p)):
        for c in range(COMPS):
            if k == 1:
                layers = [picked(late, u + 2, c) for u in range(WIDE)]
            else:
                layers = [picked(late, u, c) if u < 2 else picked(early, u - 2, c) for u in range(WIDE)]
            for x in range(WIDE):
                value = jnp.where(mirrored, layers[WIDE - 1 - x], layers[x])
                held[k, c, pl.ds(x, NZ, stride=WIDE), :] = value
            copies.append(pltpu.make_async_copy(held.at[k, c], out.at[c], sems.at[k, c]))
            copies[-1].start()
    for copy in copies:
        copy.wait()


def add_kernel(*refs):
    *parts, out = refs
    out[...] = sum((ref[...] for ref in parts[1:]), parts[0][...])


def run(kernel, outs, arrays, scratch=(), raw=(), after=(), held=True):
    vmem, hbm = (pl.BlockSpec(memory_space=pltpu.VMEM), pl.BlockSpec(memory_space=pltpu.HBM))
    given = len(arrays) + len(raw)

    def body(*refs):
        kernel(*refs[:given], *refs[given + len(after) :])

    space = pltpu.VMEM if held else pltpu.HBM
    return pl.pallas_call(
        body,
        out_shape=[space(out.shape, out.dtype) for out in outs],
        in_specs=[vmem] * len(arrays) + [hbm] * len(raw) + [pl.BlockSpec(memory_space=pl.ANY)] * len(after),
        out_specs=[vmem if held else hbm] * len(outs),
        scratch_shapes=list(scratch),
        cost_estimate=pl.CostEstimate(flops=4000, bytes_accessed=1000, transcendentals=0),
        compiler_params=pltpu.CompilerParams(vmem_limit_bytes=12 * 1024 * 1024),
    )(
        *(pltpu.with_memory_space_constraint(value, pltpu.VMEM) for value in arrays),
        *(pltpu.with_memory_space_constraint(value, pltpu.HBM) for value in raw),
        *after,
    )


def pair_swap(value, axis, other):
    return lax.ppermute(value, axis, [(i, other(i)) for i in range(lax.axis_size(axis)) if other(i) is not None])


def local(field, momenta, kappa, quartic, acceptance):
    gx, gy, reps = (lax.axis_size("gx"), lax.axis_size("gy"), lax.axis_size("rep"))
    volume = NZ * WIDE * LANES * gx * gy
    core = lax.axis_index("gx") % 2
    spread = lambda values: jnp.broadcast_to(jnp.stack(values)[:, None, None], (len(values), 8, LANES))
    flags = spread([core, lax.axis_index("gy") % 2]).astype(jnp.int32)
    position = lax.axis_index("rep")
    partner = acceptance[position]
    first, second = (partner == position ^ 1, (partner != position) & (partner != position ^ 1))
    choice = spread([core, first.astype(core.dtype), second.astype(core.dtype)]).astype(jnp.int32)
    par = spread([kappa[0], quartic[0]])

    def far(value):
        return pair_swap(value, "gx", lambda i: (i + 1) % gx if i % 2 == 1 else (i - 1) % gx)

    def near(value):
        return pair_swap(value, "gx", lambda i: i ^ 1)

    def beside(value, parity):
        return pair_swap(value, "gy", lambda i: (i + 1) % gy if i % 2 == parity else (i - 1) % gy)

    def exchanged(value):
        first = pair_swap(value, "rep", lambda i: i ^ 1 if i ^ 1 < reps else None)
        second = pair_swap(value, "rep", lambda i: ((i - 1) ^ 1) + 1 if 0 < i and ((i - 1) ^ 1) + 1 < reps else None)
        return (first, second)

    main, both = (f32(COMPS, NZ, LANES), f32(COMPS, NZ + 8, LANES))
    edges, whole, vreg = (f32(WIDE, COMPS, 8, LANES), f32(WIDE, COMPS, NZ, LANES), f32(8, LANES))
    edge, side = (f32(COMPS, 8, LANES), f32(SITES + 16, LANES))

    m0, m1, m2, m3, k0, k1, k2, k3, to_first, to_second = run(
        ingest_kernel,
        [main] * 8 + [edges] * 2,
        [flags],
        scratch=[pltpu.VMEM((2, COMPS, NZ * WIDE, LANES), jnp.float32), pltpu.SemaphoreType.DMA((2, COMPS))],
        raw=[value.reshape(COMPS, NZ * WIDE, LANES) for value in (field, momenta)],
    )
    far0, near0 = (far(m0), near(m3))
    first, second = (beside(to_first, 0), beside(to_second, 1))
    qg, pg, near_g, to_far = run(
        ghost_kernel, [edges, edges, edge, f32(2 * SITES + 48, LANES)], [flags, first, second, m1, k0]
    )
    near_ghost, beyond0 = (near(near_g), far(to_far))
    z1, zp1, a1, b1, a2, b2, a3, b3, start, msg, to_near = run(
        inner_start,
        [main, main] + [both] * 6 + [vreg, f32(SITES + 24, LANES), side],
        [par, far0, m0, m1, m2, m3, k0, k1, k2, k3, qg, pg, near0, near_ghost],
    )
    beyond1, near1 = (far(msg), near(to_near))
    arrays = [par, a1, a2, b2, a3, b3, near1]
    c2, d2, c3, d3, to_near = run(inner_kernel, [both] * 4 + [side], arrays, after=[choice])
    near2 = near(to_near)
    zg1, c1, d1, hq1, hp1, z2, zp2 = run(
        outer_first,
        [edge] + [both] * 6,
        [par, beyond0, far0, m0, qg, pg, z1, zp1, a1, b1, a2],
        scratch=[pltpu.VMEM((COMPS, 8, LANES), jnp.float32)],
    )
    e1, f1, e2, f2, e3, f3, msg, to_near = run(
        inner_second,
        [both] * 6 + [f32(2 * SITES + 16, LANES), side],
        [par, z2, c1, d1, c2, d2, c3, d3, near2],
    )
    beyond2 = far(msg)
    near3 = near(to_near)
    hq2, hp2, z3, zp3, g1, h1 = run(
        outer_kernel,
        [both] * 6,
        [par, beyond1, hq1, hp1, z1, zg1, z2, zp2, c1, e1, f1, e2],
    )
    g2, h2, g3, h3, to_near, early = run(
        inner_third,
        [both] * 4 + [f32(SITES, LANES), f32(2, COMPS, NZ, LANES)],
        [par, e1, e2, f2, e3, f3, near3],
        after=[beyond1],
    )
    near4 = near(to_near)
    first_early, second_early = exchanged(early)
    r2, r3, more = run(inner_final, [main, main, vreg], [par, g1, g2, h2, g3, h3, near4])
    late, energy = run(
        outer_last,
        [f32(6, COMPS, NZ, LANES), vreg],
        [par, beyond2, hq2, hp2, z2, z3, zp3, e1, g1, h1, g2, r2, r3, start, more],
        after=[first_early, second_early],
        scratch=[pltpu.VMEM((COMPS, NZ + 8, LANES), jnp.float32)] * 4 + [pltpu.VMEM((COMPS, NZ, LANES), jnp.float32)],
    )
    first_late, second_late = exchanged(late)

    new_q, new_p = run(
        place_kernel,
        [f32(COMPS, NZ * WIDE, LANES)] * 2,
        [choice, late, first_late, second_late, early, first_early, second_early],
        scratch=[pltpu.VMEM((2, COMPS, NZ * WIDE, LANES), jnp.float32), pltpu.SemaphoreType.DMA((2, COMPS))],
        held=False,
    )
    energy = energy + near(energy)
    moved = [pair_swap(energy, "gx", lambda i, k=k: i ^ (4 * k)) for k in range(1, gx // 4)]
    energy = sum(moved, energy)
    energy = energy + pair_swap(energy, "gy", lambda i: i ^ 1)

    def across(i_bit, j_bit):
        pairs = [(i * gy + j, (i ^ i_bit) * gy + (j ^ j_bit)) for i in range(gx) for j in range(gy)]
        return lax.ppermute(energy, ("gx", "gy"), pairs)

    parts = [energy, across(0, 2), across(2, 2), across(2, 1)]
    placed_first = [pltpu.with_memory_space_constraint(value, pltpu.HBM) for value in (new_q, new_p)]
    (energy,) = run(add_kernel, [vreg], parts, after=placed_first)
    energy = (jnp.sum(energy[:2], axis=1) / volume)[None, :]
    return (new_q.reshape(field.shape), new_p.reshape(field.shape), energy)


def solution(mesh):
    placed = (
        P("rep", None, None, "gx", "gy"),
        P("rep", None, None, "gx", "gy"),
        P("rep"),
        P("rep"),
        P(),
    )
    return jax.shard_map(
        local,
        mesh=mesh,
        in_specs=placed,
        out_specs=(
            P("rep", None, None, "gx", "gy"),
            P("rep", None, None, "gx", "gy"),
            P("rep", None),
        ),
        check_vma=False,
    )
```

time: 91.5 us -> 84.7 us (0.926)
  Pallas kernels: 21.5 us -> 10.3 us
  starting transfers between devices: 33.9 us -> 42.8 us
  waiting for transfers between devices: 30.3 us -> 24.9 us
    ppermute x5 -> x3, waiting for transfers between devices: 16.5 us -> 4.58 us  [across(): return lax.ppermute(energy, ('gx', 'gy'), pairs)]
    pallas_call x14 -> x12, Pallas kernels: 21.5 us -> 10.3 us  [run(): pl.pallas_call(body, out_shape=[space(out.shape, out.dtype) for out in ou...]
    ppermute x17 -> x21, waiting for transfers between devices: 13.8 us -> 20.4 us  [pair_swap(): lax.ppermute(value, axis, [(i, other(i)) for i in range(lax.axis_size(axi...]
    ppermute x5 -> x3, starting transfers between devices: 0.73 us -> 5.56 us  [across(): return lax.ppermute(energy, ('gx', 'gy'), pairs)]
    ppermute x17 -> x21, starting transfers between devices: 33.2 us -> 37.3 us  [pair_swap(): lax.ppermute(value, axis, [(i, other(i)) for i in range(lax.axis_size(axi...]
  transfers between devices with their start and end apart: 22 -> 24, of which waited for: 11 -> 11; matrix products, arithmetic and copies ran while one was open for 1% -> 1% of each run, Pallas kernels for 18% -> 9%
where the time goes in v2:
time: 84.7 us; the launch traced here: 84.5 us
  starting transfers between devices  42.8 us (51%)
  waiting for transfers between devices  24.9 us (29%)
  Pallas kernels  10.3 us (12%)
  between operations  4.07 us (5%)
  local copies, waits for them, and re-layouts  1.45 us (2%)
  other arithmetic  0.87 us (1%)
    ppermute x21, starting transfers between devices, pair_swap(): lax.ppermute(value, axis, [(i, other(i)) for i in range(lax.axis_size(axi...  37.3 us
    ppermute x21, waiting for transfers between devices, pair_swap(): lax.ppermute(value, axis, [(i, other(i)) for i in range(lax.axis_size(axi...  20.4 us
    pallas_call x12, Pallas kernels, run(): pl.pallas_call(body, out_shape=[space(out.shape, out.dtype) for out in ou...  10.3 us
    ppermute x3, starting transfers between devices, across(): return lax.ppermute(energy, ('gx', 'gy'), pairs)  5.56 us
    ppermute x3, waiting for transfers between devices, across(): return lax.ppermute(energy, ('gx', 'gy'), pairs)  4.58 us
  transfers between devices with their start and end apart: 24, of which 11 were waited for; matrix products, arithmetic and copies ran while one was open for 1% of the time, Pallas kernels for 9%

profile of v2, /device:TPU:2, one launch (start us, length us, event | category | flops | bytes accessed | tf_op | source)
XLA Modules:
  0.0 84.5 jit_solution(11551837297374136461)
XLA Ops:
  0.8 1.9 %shard_map.76 = (f32[4,64,128]{2,1,0:T(8,128)S(1)}, f32[4,64,128]{2,1,0:T(8,128)S(1)}, f32[4,64,128]{2,1,0:T(8,128)S(1)}, f32[4,64,128]{2,1,0:T(8,128)S(1)}, f32...) custom-call(s32[2,8,128]{2,1,0:T(8,128)S(1)} %broadcast_in_dim.8.ref, ...), custom_call_target="tpu_custom_call" | custom-call | flops 4000 | bytes 1000 | tf_op jit(solution)/shard_map/pallas_call | solution.py:379
  2.7 2.0 %collective-permute-start = (f32[4,4,8,128]{3,2,1,0:T(8,128)S(1)}, f32[4,4,8,128]{3,2,1,0:T(8,128)S(1)}, u32[]{:S(2)}, u32[]{:S(2)}) collective-permute-start(f32[4,4,8,128]{3,2,1,0:T(8,128)S(1)} %get-tuple-element.67), channel_id=1, source_target_pairs={{0,1},{1,0},{2,3},{3,2},{4,5},{5,4},{6,7},{7,6},{8,9},{9,8},{10,11... | collective-permute-start | bytes 196616 | tf_op jit(solution)/shard_map/ppermute | solution.py:395
  4.7 2.8 %collective-permute-start.1 = (f32[4,4,8,128]{3,2,1,0:T(8,128)S(1)}, f32[4,4,8,128]{3,2,1,0:T(8,128)S(1)}, u32[]{:S(2)}, u32[]{:S(2)}) collective-permute-start(f32[4,4,8,128]{3,2,1,0:T(8,128)S(1)} %get-tuple-element.68), channel_id=1, source_target_pairs={{0,3},{1,2},{2,1},{3,0},{4,7},{5,6},{6,5},{7,4},{8,11},{9,10},{10,... | collective-permute-start | bytes 196616 | tf_op jit(solution)/shard_map/ppermute | solution.py:395
  7.5 6.7 %collective-permute-start.3 = (f32[4,64,128]{2,1,0:T(8,128)S(1)}, f32[4,64,128]{2,1,0:T(8,128)S(1)}, u32[]{:S(2)}, u32[]{:S(2)}) collective-permute-start(f32[4,64,128]{2,1,0:T(8,128)S(1)} %get-tuple-element.72.refs_2_.refs_3_), channel_id=1, source_target_pairs={{0,60},{4,8},{8,4},{12,16},{16,12},{20,24},{24,20},{28,32},{32,28}... | collective-permute-start | bytes 393224 | tf_op jit(solution)/shard_map/ppermute | solution.py:395
  15.5 0.1 shard_map.77
  15.7 2.3 %collective-permute-start.2 = (f32[560,128]{1,0:T(8,128)S(1)}, f32[560,128]{1,0:T(8,128)S(1)}, u32[]{:S(2)}, u32[]{:S(2)}) collective-permute-start(f32[560,128]{1,0:T(8,128)S(1)} %get-tuple-element.71), channel_id=1, source_target_pairs={{0,60},{4,8},{8,4},{12,16},{16,12},{20,24},{24,20},{28,32},{32,28}... | collective-permute-start | bytes 860168 | tf_op jit(solution)/shard_map/ppermute | solution.py:395
  17.9 0.1 collective-permute-start.5
  18.1 1.0 %collective-permute-done.5.refs_13_ = f32[4,8,128]{2,1,0:T(8,128)S(1)} collective-permute-done((f32[4,8,128]{2,1,0:T(8,128)S(1)}, f32[4,8,128]{2,1,0:T(8,128)S(1)}, u32[]{:S(2)}, u32[]{:S(2)}) %collective-permute-start.5) | collective-permute-done | bytes 16416 | tf_op jit(solution)/shard_map/ppermute | solution.py:395
  19.2 1.2 %shard_map.78 = (f32[4,64,128]{2,1,0:T(8,128)S(1)}, f32[4,64,128]{2,1,0:T(8,128)S(1)}, f32[4,72,128]{2,1,0:T(8,128)S(1)}, f32[4,72,128]{2,1,0:T(8,128)S(1)}, f32...) custom-call(f32[2,8,128]{2,1,0:T(8,128)S(1)} %broadcast_in_dim.7.ref, ...), custom_call_target="tpu_custom_call" | custom-call | flops 4000 | bytes 1000 | tf_op jit(solution)/shard_map/pallas_call | solution.py:379
  20.5 0.3 collective-permute-start.6
  20.7 0.7 copy-done
  21.4 0.6 dynamic_slice.3
  24.1 0.6 shard_map.80
  24.6 0.4 collective-permute-start.7
  25.1 7.0 %collective-permute-start.9 = (f32[280,128]{1,0:T(8,128)S(1)}, f32[280,128]{1,0:T(8,128)S(1)}, u32[]{:S(2)}, u32[]{:S(2)}) collective-permute-start(f32[280,128]{1,0:T(8,128)S(1)} %get-tuple-element.99), channel_id=1, source_target_pairs={{0,60},{4,8},{8,4},{12,16},{16,12},{20,24},{24,20},{28,32},{32,28}... | collective-permute-start | bytes 430088 | tf_op jit(solution)/shard_map/ppermute | solution.py:395
  32.1 5.5 %collective-permute-done.2.refs_1_ = f32[560,128]{1,0:T(8,128)S(1)} collective-permute-done((f32[560,128]{1,0:T(8,128)S(1)}, f32[560,128]{1,0:T(8,128)S(1)}, u32[]{:S(2)}, u32[]{:S(2)}) %collective-permute-start.2) | collective-permute-done | bytes 286752 | tf_op jit(solution)/shard_map/ppermute | solution.py:395
  37.6 1.4 %shard_map.79 = (f32[4,8,128]{2,1,0:T(8,128)S(1)}, f32[4,72,128]{2,1,0:T(8,128)S(1)}, f32[4,72,128]{2,1,0:T(8,128)S(1)}, f32[4,72,128]{2,1,0:T(8,128)S(1)}, f32[...) custom-call(f32[2,8,128]{2,1,0:T(8,128)S(1)} %broadcast_in_dim.7.refs_0_, ...), custom_call_target="tpu_custom_call" | custom-call | flops 4000 | bytes 1000 | tf_op jit(solution)/shard_map/pallas_call | solution.py:379
  39.0 1.0 %shard_map.81 = (f32[4,72,128]{2,1,0:T(8,128)S(1)}, f32[4,72,128]{2,1,0:T(8,128)S(1)}, f32[4,72,128]{2,1,0:T(8,128)S(1)}, f32[4,72,128]{2,1,0:T(8,128)S(1)}, f32...) custom-call(f32[2,8,128]{2,1,0:T(8,128)S(1)} %broadcast_in_dim.7.refs_0_, ...), custom_call_target="tpu_custom_call" | custom-call | flops 4000 | bytes 1000 | tf_op jit(solution)/shard_map/pallas_call | solution.py:379
  40.0 0.1 collective-permute-start.10
  40.1 1.8 %collective-permute-start.8 = (f32[528,128]{1,0:T(8,128)S(1)}, f32[528,128]{1,0:T(8,128)S(1)}, u32[]{:S(2)}, u32[]{:S(2)}) collective-permute-start(f32[528,128]{1,0:T(8,128)S(1)} %get-tuple-element.98), channel_id=1, source_target_pairs={{0,60},{4,8},{8,4},{12,16},{16,12},{20,24},{24,20},{28,32},{32,28}... | collective-permute-start | bytes 811016 | tf_op jit(solution)/shard_map/ppermute | solution.py:395
  41.9 0.6 shard_map.83
  42.5 0.6 collective-permute-start.12
  43.1 4.1 %collective-permute-start.13 = (f32[2,4,64,128]{3,2,1,0:T(8,128)S(1)}, f32[2,4,64,128]{3,2,1,0:T(8,128)S(1)}, u32[]{:S(2)}, u32[]{:S(2)}) collective-permute-start(f32[2,4,64,128]{3,2,1,0:T(8,128)S(1)} %get-tuple-element.126.refs_4_), channel_id=1, source_target_pairs={{64,128},{128,64},{65,129},{129,65},{66,130},{130,66},{67,131},{13... | collective-permute-start | bytes 786440 | tf_op jit(solution)/shard_map/ppermute | solution.py:395
  47.1 0.3 collective-permute-start.11
  47.4 1.1 %shard_map.82 = (f32[4,72,128]{2,1,0:T(8,128)S(1)}, f32[4,72,128]{2,1,0:T(8,128)S(1)}, f32[4,72,128]{2,1,0:T(8,128)S(1)}, f32[4,72,128]{2,1,0:T(8,128)S(1)}, f32...) custom-call(f32[2,8,128]{2,1,0:T(8,128)S(1)} %broadcast_in_dim.7.refs_0_, ...), custom_call_target="tpu_custom_call" | custom-call | flops 4000 | bytes 1000 | tf_op jit(solution)/shard_map/pallas_call | solution.py:379
  48.5 0.2 collective-permute-done.11.refs_6_
  48.8 0.4 shard_map.84
  49.1 7.2 %collective-permute-done.8.refs_1_ = f32[528,128]{1,0:T(8,128)S(1)} collective-permute-done((f32[528,128]{1,0:T(8,128)S(1)}, f32[528,128]{1,0:T(8,128)S(1)}, u32[]{:S(2)}, u32[]{:S(2)}) %collective-permute-start.8) | collective-permute-done | bytes 270368 | tf_op jit(solution)/shard_map/ppermute | solution.py:395
  56.3 1.0 %shard_map.85 = (f32[6,4,64,128]{3,2,1,0:T(8,128)S(1)}, f32[8,128]{1,0:T(8,128)S(1)}) custom-call(f32[2,8,128]{2,1,0:T(8,128)S(1)} %broadcast_in_dim.7.refs_0_, f32[528,128]{1,0:T(8,128)S(1)} %collective-permute-done.8.refs_1_, f32[4,72,128]{2,1,0:T(8,128)S(1)} %get-tuple-element.107.refs_2_, f32[4,72,128]{2,1,0:T(8,128)S(1)} %get-tuple-element.108.refs_3_, ...), custom_call_target="tpu_custom_call" | custom-call | flops 4000 | bytes 1000 | tf_op jit(solution)/shard_map/pallas_call | solution.py:379
  57.4 0.6 collective-permute-start.14
  58.0 4.1 %collective-permute-start.15 = (f32[6,4,64,128]{3,2,1,0:T(8,128)S(1)}, f32[6,4,64,128]{3,2,1,0:T(8,128)S(1)}, u32[]{:S(2)}, u32[]{:S(2)}) collective-permute-start(f32[6,4,64,128]{3,2,1,0:T(8,128)S(1)} %get-tuple-element.127.refs_1_), channel_id=1, source_target_pairs={{64,128},{128,64},{65,129},{129,65},{66,130},{130,66},{67,131},{13... | collective-permute-start | bytes 2359304 | tf_op jit(solution)/shard_map/ppermute | solution.py:395
  62.1 0.1 collective-permute-start.16
  62.2 1.2 %collective-permute-done.16 = f32[8,128]{1,0:T(8,128)S(1)} collective-permute-done((f32[8,128]{1,0:T(8,128)S(1)}, f32[8,128]{1,0:T(8,128)S(1)}, u32[]{:S(2)}, u32[]{:S(2)}) %collective-permute-start.16) | collective-permute-done | bytes 4128 | tf_op jit(solution)/shard_map/ppermute | solution.py:395
  63.3 0.4 collective-permute-start.19
  63.7 1.1 %collective-permute-start.18 = (f32[8,128]{1,0:T(8,128)S(1)}, f32[8,128]{1,0:T(8,128)S(1)}, u32[]{:S(2)}, u32[]{:S(2)}) collective-permute-start(f32[8,128]{1,0:T(8,128)S(1)} %add.28), channel_id=1, source_target_pairs={{0,32},{4,36},{8,40},{12,44},{16,48},{20,52},{24,56},{28,60},{32,0... | collective-permute-start | bytes 12296 | tf_op jit(solution)/shard_map/ppermute | solution.py:395
  64.9 2.5 %collective-permute-start.17 = (f32[8,128]{1,0:T(8,128)S(1)}, f32[8,128]{1,0:T(8,128)S(1)}, u32[]{:S(2)}, u32[]{:S(2)}) collective-permute-start(f32[8,128]{1,0:T(8,128)S(1)} %add.28), channel_id=1, source_target_pairs={{0,16},{4,20},{8,24},{12,28},{16,0},{20,4},{24,8},{28,12},{32,48},... | collective-permute-start | bytes 12296 | tf_op jit(solution)/shard_map/ppermute | solution.py:395
  67.4 0.7 collective-permute-done.19
  68.1 0.7 collective-permute-done.18
  68.9 0.2 collective-permute-done.17
  69.0 3.6 %collective-permute-done.20 = f32[8,128]{1,0:T(8,128)S(1)} collective-permute-done((f32[8,128]{1,0:T(8,128)S(1)}, f32[8,128]{1,0:T(8,128)S(1)}, u32[]{:S(2)}, u32[]{:S(2)}) %collective-permute-start.20) | collective-permute-done | bytes 4128 | tf_op jit(solution)/shard_map/ppermute | solution.py:395
  72.7 1.4 %collective-permute-start.21 = (f32[8,128]{1,0:T(8,128)S(1)}, f32[8,128]{1,0:T(8,128)S(1)}, u32[]{:S(2)}, u32[]{:S(2)}) collective-permute-start(f32[8,128]{1,0:T(8,128)S(1)} %add.32.refs_0_), channel_id=1, source_target_pairs={{0,2},{1,3},{2,0},{3,1},{4,6},{5,7},{6,4},{7,5},{8,10},{9,11},{10,... | collective-permute-start | bytes 12296 | tf_op jit(solution)/shard_map/ppermute | solution.py:500
  74.1 3.2 %collective-permute-start.22 = (f32[8,128]{1,0:T(8,128)S(1)}, f32[8,128]{1,0:T(8,128)S(1)}, u32[]{:S(2)}, u32[]{:S(2)}) collective-permute-start(f32[8,128]{1,0:T(8,128)S(1)} %add.32.refs_0_), channel_id=1, source_target_pairs={{0,10},{1,11},{2,8},{3,9},{4,14},{5,15},{6,12},{7,13},{8,2},{9,3},... | collective-permute-start | bytes 12296 | tf_op jit(solution)/shard_map/ppermute | solution.py:500
  77.3 1.0 %collective-permute-start.23 = (f32[8,128]{1,0:T(8,128)S(1)}, f32[8,128]{1,0:T(8,128)S(1)}, u32[]{:S(2)}, u32[]{:S(2)}) collective-permute-start(f32[8,128]{1,0:T(8,128)S(1)} %add.32.refs_0_), channel_id=1, source_target_pairs={{0,9},{1,8},{2,11},{3,10},{4,13},{5,12},{6,15},{7,14},{8,1},{9,0},... | collective-permute-start | bytes 12296 | tf_op jit(solution)/shard_map/ppermute | solution.py:500
  78.2 1.0 %shard_map.86 = (f32[4,256,128]{2,1,0:T(8,128)}, f32[4,256,128]{2,1,0:T(8,128)}) custom-call(s32[3,8,128]{2,1,0:T(8,128)S(1)} %broadcast_in_dim.6.refs_7_.refs_0_, f32[6,4,64,128]{3,2,1,0:T(8,128)S(1)} %get-tuple-element.127.refs_1_, f32[6,4,64,128]{3,2,1,0:T(8,128)S(1)} %collective-permute-done.14.refs_2_, ...), custom_call_target="tpu_custom_call" | custom-call | flops 4000 | bytes 1000 | tf_op jit(solution)/shard_map/pallas_call | solution.py:379
  79.3 0.5 collective-permute-done.22.refs_2_
  79.8 4.1 %collective-permute-done.23.refs_3_ = f32[8,128]{1,0:T(8,128)S(1)} collective-permute-done((f32[8,128]{1,0:T(8,128)S(1)}, f32[8,128]{1,0:T(8,128)S(1)}, u32[]{:S(2)}, u32[]{:S(2)}) %collective-permute-start.23) | collective-permute-done | bytes 4128 | tf_op jit(solution)/shard_map/ppermute | solution.py:500
  83.9 0.1 slice_reduce_fusion
  84.0 0.5 multiply_bitcast_fusion
  (26 shorter events, 0.5 us)
Async XLA Ops:
  2.7 12.8 %collective-permute-start = (f32[4,4,8,128]{3,2,1,0:T(8,128)S(1)}, f32[4,4,8,128]{3,2,1,0:T(8,128)S(1)}, u32[]{:S(2)}, u32[]{:S(2)}) collective-permute-start(f32[4,4,8,128]{3,2,1,0:T(8,128)S(1)} %get-tuple-element.67), channel_id=1, source_target_pairs={{0,1},{1,0},{2,3},{3,2},{4,5},{5,4},{6,7},{7,6},{8,9},{9,8},{10,11... | collective-permute-start | bytes 196616 | tf_op jit(solution)/shard_map/ppermute | solution.py:395
  4.7 10.9 %collective-permute-start.1 = (f32[4,4,8,128]{3,2,1,0:T(8,128)S(1)}, f32[4,4,8,128]{3,2,1,0:T(8,128)S(1)}, u32[]{:S(2)}, u32[]{:S(2)}) collective-permute-start(f32[4,4,8,128]{3,2,1,0:T(8,128)S(1)} %get-tuple-element.68), channel_id=1, source_target_pairs={{0,3},{1,2},{2,1},{3,0},{4,7},{5,6},{6,5},{7,4},{8,11},{9,10},{10,... | collective-permute-start | bytes 196616 | tf_op jit(solution)/shard_map/ppermute | solution.py:395
  7.5 11.6 %collective-permute-start.3 = (f32[4,64,128]{2,1,0:T(8,128)S(1)}, f32[4,64,128]{2,1,0:T(8,128)S(1)}, u32[]{:S(2)}, u32[]{:S(2)}) collective-permute-start(f32[4,64,128]{2,1,0:T(8,128)S(1)} %get-tuple-element.72.refs_2_.refs_3_), channel_id=1, source_target_pairs={{0,60},{4,8},{8,4},{12,16},{16,12},{20,24},{24,20},{28,32},{32,28}... | collective-permute-start | bytes 393224 | tf_op jit(solution)/shard_map/ppermute | solution.py:395
  14.2 4.9 %collective-permute-start.4 = (f32[4,64,128]{2,1,0:T(8,128)S(1)}, f32[4,64,128]{2,1,0:T(8,128)S(1)}, u32[]{:S(2)}, u32[]{:S(2)}) collective-permute-start(f32[4,64,128]{2,1,0:T(8,128)S(1)} %get-tuple-element.76.refs_5_), channel_id=1, source_target_pairs={{0,4},{4,0},{8,12},{12,8},{16,20},{20,16},{24,28},{28,24},{32,36},... | collective-permute-start | bytes 393224 | tf_op jit(solution)/shard_map/ppermute | solution.py:395
  15.7 21.9 %collective-permute-start.2 = (f32[560,128]{1,0:T(8,128)S(1)}, f32[560,128]{1,0:T(8,128)S(1)}, u32[]{:S(2)}, u32[]{:S(2)}) collective-permute-start(f32[560,128]{1,0:T(8,128)S(1)} %get-tuple-element.71), channel_id=1, source_target_pairs={{0,60},{4,8},{8,4},{12,16},{16,12},{20,24},{24,20},{28,32},{32,28}... | collective-permute-start | bytes 860168 | tf_op jit(solution)/shard_map/ppermute | solution.py:395
  17.9 1.2 %collective-permute-start.5 = (f32[4,8,128]{2,1,0:T(8,128)S(1)}, f32[4,8,128]{2,1,0:T(8,128)S(1)}, u32[]{:S(2)}, u32[]{:S(2)}) collective-permute-start(f32[4,8,128]{2,1,0:T(8,128)S(1)} %get-tuple-element.80), channel_id=1, source_target_pairs={{0,4},{4,0},{8,12},{12,8},{16,20},{20,16},{24,28},{28,24},{32,36},... | collective-permute-start | bytes 49160 | tf_op jit(solution)/shard_map/ppermute | solution.py:395
  20.5 3.5 %collective-permute-start.6 = (f32[272,128]{1,0:T(8,128)S(1)}, f32[272,128]{1,0:T(8,128)S(1)}, u32[]{:S(2)}, u32[]{:S(2)}) collective-permute-start(f32[272,128]{1,0:T(8,128)S(1)} %get-tuple-element.92), channel_id=1, source_target_pairs={{0,4},{4,0},{8,12},{12,8},{16,20},{20,16},{24,28},{28,24},{32,36},... | collective-permute-start | bytes 417800 | tf_op jit(solution)/shard_map/ppermute | solution.py:395
  20.7 0.7 copy-start
  24.6 14.3 %collective-permute-start.7 = (f32[272,128]{1,0:T(8,128)S(1)}, f32[272,128]{1,0:T(8,128)S(1)}, u32[]{:S(2)}, u32[]{:S(2)}) collective-permute-start(f32[272,128]{1,0:T(8,128)S(1)} %get-tuple-element.97), channel_id=1, source_target_pairs={{0,4},{4,0},{8,12},{12,8},{16,20},{20,16},{24,28},{28,24},{32,36},... | collective-permute-start | bytes 417800 | tf_op jit(solution)/shard_map/ppermute | solution.py:395
  25.1 16.8 %collective-permute-start.9 = (f32[280,128]{1,0:T(8,128)S(1)}, f32[280,128]{1,0:T(8,128)S(1)}, u32[]{:S(2)}, u32[]{:S(2)}) collective-permute-start(f32[280,128]{1,0:T(8,128)S(1)} %get-tuple-element.99), channel_id=1, source_target_pairs={{0,60},{4,8},{8,4},{12,16},{16,12},{20,24},{24,20},{28,32},{32,28}... | collective-permute-start | bytes 430088 | tf_op jit(solution)/shard_map/ppermute | solution.py:395
  40.0 1.9 %collective-permute-start.10 = (f32[272,128]{1,0:T(8,128)S(1)}, f32[272,128]{1,0:T(8,128)S(1)}, u32[]{:S(2)}, u32[]{:S(2)}) collective-permute-start(f32[272,128]{1,0:T(8,128)S(1)} %get-tuple-element.116), channel_id=1, source_target_pairs={{0,4},{4,0},{8,12},{12,8},{16,20},{20,16},{24,28},{28,24},{32,36},... | collective-permute-start | bytes 417800 | tf_op jit(solution)/shard_map/ppermute | solution.py:395
  40.1 16.3 %collective-permute-start.8 = (f32[528,128]{1,0:T(8,128)S(1)}, f32[528,128]{1,0:T(8,128)S(1)}, u32[]{:S(2)}, u32[]{:S(2)}) collective-permute-start(f32[528,128]{1,0:T(8,128)S(1)} %get-tuple-element.98), channel_id=1, source_target_pairs={{0,60},{4,8},{8,4},{12,16},{16,12},{20,24},{24,20},{28,32},{32,28}... | collective-permute-start | bytes 811016 | tf_op jit(solution)/shard_map/ppermute | solution.py:395
  42.5 13.9 %collective-permute-start.12 = (f32[2,4,64,128]{3,2,1,0:T(8,128)S(1)}, f32[2,4,64,128]{3,2,1,0:T(8,128)S(1)}, u32[]{:S(2)}, u32[]{:S(2)}) collective-permute-start(f32[2,4,64,128]{3,2,1,0:T(8,128)S(1)} %get-tuple-element.126.refs_4_), channel_id=1, source_target_pairs={{0,64},{64,0},{128,192},{192,128},{1,65},{65,1},{129,193},{193,129... | collective-permute-start | bytes 786440 | tf_op jit(solution)/shard_map/ppermute | solution.py:395
  43.1 13.3 %collective-permute-start.13 = (f32[2,4,64,128]{3,2,1,0:T(8,128)S(1)}, f32[2,4,64,128]{3,2,1,0:T(8,128)S(1)}, u32[]{:S(2)}, u32[]{:S(2)}) collective-permute-start(f32[2,4,64,128]{3,2,1,0:T(8,128)S(1)} %get-tuple-element.126.refs_4_), channel_id=1, source_target_pairs={{64,128},{128,64},{65,129},{129,65},{66,130},{130,66},{67,131},{13... | collective-permute-start | bytes 786440 | tf_op jit(solution)/shard_map/ppermute | solution.py:395
  47.1 1.6 %collective-permute-start.11 = (f32[256,128]{1,0:T(8,128)S(1)}, f32[256,128]{1,0:T(8,128)S(1)}, u32[]{:S(2)}, u32[]{:S(2)}) collective-permute-start(f32[256,128]{1,0:T(8,128)S(1)} %get-tuple-element.121), channel_id=1, source_target_pairs={{0,4},{4,0},{8,12},{12,8},{16,20},{20,16},{24,28},{28,24},{32,36},... | collective-permute-start | bytes 393224 | tf_op jit(solution)/shard_map/ppermute | solution.py:395
  57.4 20.8 %collective-permute-start.14 = (f32[6,4,64,128]{3,2,1,0:T(8,128)S(1)}, f32[6,4,64,128]{3,2,1,0:T(8,128)S(1)}, u32[]{:S(2)}, u32[]{:S(2)}) collective-permute-start(f32[6,4,64,128]{3,2,1,0:T(8,128)S(1)} %get-tuple-element.127.refs_1_), channel_id=1, source_target_pairs={{0,64},{64,0},{128,192},{192,128},{1,65},{65,1},{129,193},{193,129... | collective-permute-start | bytes 2359304 | tf_op jit(solution)/shard_map/ppermute | solution.py:395
  58.0 20.2 %collective-permute-start.15 = (f32[6,4,64,128]{3,2,1,0:T(8,128)S(1)}, f32[6,4,64,128]{3,2,1,0:T(8,128)S(1)}, u32[]{:S(2)}, u32[]{:S(2)}) collective-permute-start(f32[6,4,64,128]{3,2,1,0:T(8,128)S(1)} %get-tuple-element.127.refs_1_), channel_id=1, source_target_pairs={{64,128},{128,64},{65,129},{129,65},{66,130},{130,66},{67,131},{13... | collective-permute-start | bytes 2359304 | tf_op jit(solution)/shard_map/ppermute | solution.py:395
  62.1 1.3 %collective-permute-start.16 = (f32[8,128]{1,0:T(8,128)S(1)}, f32[8,128]{1,0:T(8,128)S(1)}, u32[]{:S(2)}, u32[]{:S(2)}) collective-permute-start(f32[8,128]{1,0:T(8,128)S(1)} %get-tuple-element.130), channel_id=1, source_target_pairs={{0,4},{4,0},{8,12},{12,8},{16,20},{20,16},{24,28},{28,24},{32,36},... | collective-permute-start | bytes 12296 | tf_op jit(solution)/shard_map/ppermute | solution.py:395
  63.3 4.8 %collective-permute-start.19 = (f32[8,128]{1,0:T(8,128)S(1)}, f32[8,128]{1,0:T(8,128)S(1)}, u32[]{:S(2)}, u32[]{:S(2)}) collective-permute-start(f32[8,128]{1,0:T(8,128)S(1)} %add.28), channel_id=1, source_target_pairs={{0,48},{4,52},{8,56},{12,60},{16,32},{20,36},{24,40},{28,44},{32,1... | collective-permute-start | bytes 12296 | tf_op jit(solution)/shard_map/ppermute | solution.py:395
  63.7 5.1 %collective-permute-start.18 = (f32[8,128]{1,0:T(8,128)S(1)}, f32[8,128]{1,0:T(8,128)S(1)}, u32[]{:S(2)}, u32[]{:S(2)}) collective-permute-start(f32[8,128]{1,0:T(8,128)S(1)} %add.28), channel_id=1, source_target_pairs={{0,32},{4,36},{8,40},{12,44},{16,48},{20,52},{24,56},{28,60},{32,0... | collective-permute-start | bytes 12296 | tf_op jit(solution)/shard_map/ppermute | solution.py:395
  64.9 4.2 %collective-permute-start.17 = (f32[8,128]{1,0:T(8,128)S(1)}, f32[8,128]{1,0:T(8,128)S(1)}, u32[]{:S(2)}, u32[]{:S(2)}) collective-permute-start(f32[8,128]{1,0:T(8,128)S(1)} %add.28), channel_id=1, source_target_pairs={{0,16},{4,20},{8,24},{12,28},{16,0},{20,4},{24,8},{28,12},{32,48},... | collective-permute-start | bytes 12296 | tf_op jit(solution)/shard_map/ppermute | solution.py:395
  69.0 3.6 %collective-permute-start.20 = (f32[8,128]{1,0:T(8,128)S(1)}, f32[8,128]{1,0:T(8,128)S(1)}, u32[]{:S(2)}, u32[]{:S(2)}) collective-permute-start(f32[8,128]{1,0:T(8,128)S(1)} %add_add_fusion), channel_id=1, source_target_pairs={{0,1},{1,0},{2,3},{3,2},{4,5},{5,4},{6,7},{7,6},{8,9},{9,8},{10,11... | collective-permute-start | bytes 12296 | tf_op jit(solution)/shard_map/ppermute | solution.py:395
  72.7 6.6 %collective-permute-start.21 = (f32[8,128]{1,0:T(8,128)S(1)}, f32[8,128]{1,0:T(8,128)S(1)}, u32[]{:S(2)}, u32[]{:S(2)}) collective-permute-start(f32[8,128]{1,0:T(8,128)S(1)} %add.32.refs_0_), channel_id=1, source_target_pairs={{0,2},{1,3},{2,0},{3,1},{4,6},{5,7},{6,4},{7,5},{8,10},{9,11},{10,... | collective-permute-start | bytes 12296 | tf_op jit(solution)/shard_map/ppermute | solution.py:500
  74.1 5.7 %collective-permute-start.22 = (f32[8,128]{1,0:T(8,128)S(1)}, f32[8,128]{1,0:T(8,128)S(1)}, u32[]{:S(2)}, u32[]{:S(2)}) collective-permute-start(f32[8,128]{1,0:T(8,128)S(1)} %add.32.refs_0_), channel_id=1, source_target_pairs={{0,10},{1,11},{2,8},{3,9},{4,14},{5,15},{6,12},{7,13},{8,2},{9,3},... | collective-permute-start | bytes 12296 | tf_op jit(solution)/shard_map/ppermute | solution.py:500
  77.3 6.6 %collective-permute-start.23 = (f32[8,128]{1,0:T(8,128)S(1)}, f32[8,128]{1,0:T(8,128)S(1)}, u32[]{:S(2)}, u32[]{:S(2)}) collective-permute-start(f32[8,128]{1,0:T(8,128)S(1)} %add.32.refs_0_), channel_id=1, source_target_pairs={{0,9},{1,8},{2,11},{3,10},{4,13},{5,12},{6,15},{7,14},{8,1},{9,0},... | collective-permute-start | bytes 12296 | tf_op jit(solution)/shard_map/ppermute | solution.py:500

commit v3 on v2

--- a/solution.py
+++ b/solution.py
@@ -340,6 +340,21 @@
         whole[5, c] = r3[c]
 
 
+def pack_kernel(late, out):
+    out[...] = late[...]
+
+
+def pick_kernel(acceptance, flags, choice):
+    position = flags[2]
+    partner = position
+    for replica in range(acceptance.shape[0]):
+        partner = jnp.where(position == replica, acceptance[replica], partner)
+    beside = position ^ 1
+    choice[0] = flags[0]
+    choice[1] = (partner == beside).astype(jnp.int32)
+    choice[2] = ((partner != beside) & (partner != position)).astype(jnp.int32)
+
+
 def place_kernel(choice, *refs):
     late, early, (new_q, new_p, held, sems) = (refs[:3], refs[3:6], refs[6:])
     mirrored, first, second = (jnp.broadcast_to(choice[i, :1, :], (NZ, LANES)) == 1 for i in range(3))
@@ -363,14 +378,17 @@
         copy.wait()
 
 
-def add_kernel(*refs):
+def total_kernel(volume, *refs):
     *parts, out = refs
-    out[...] = sum((ref[...] for ref in parts[1:]), parts[0][...])
-
-
-def run(kernel, outs, arrays, scratch=(), raw=(), after=(), held=True):
+    total = sum((ref[...] for ref in parts[1:]), parts[0][...])
+    start, finish = (jnp.sum(total[i : i + 1, :], axis=1, keepdims=True) for i in range(2))
+    lane = lax.broadcasted_iota(jnp.int32, (1, 2), 1)
+    out[...] = jnp.where(lane == 0, start, finish) * (1.0 / volume)
+
+
+def run(kernel, outs, arrays, scratch=(), raw=(), after=(), held=True, scalars=()):
     vmem, hbm = (pl.BlockSpec(memory_space=pltpu.VMEM), pl.BlockSpec(memory_space=pltpu.HBM))
-    given = len(arrays) + len(raw)
+    given = len(scalars) + len(arrays) + len(raw)
 
     def body(*refs):
         kernel(*refs[:given], *refs[given + len(after) :])
@@ -379,12 +397,14 @@
     return pl.pallas_call(
         body,
         out_shape=[space(out.shape, out.dtype) for out in outs],
-        in_specs=[vmem] * len(arrays) + [hbm] * len(raw) + [pl.BlockSpec(memory_space=pl.ANY)] * len(after),
+        in_specs=[pl.BlockSpec(memory_space=pltpu.SMEM)] * len(scalars)
+        + [vmem] * len(arrays) + [hbm] * len(raw) + [pl.BlockSpec(memory_space=pl.ANY)] * len(after),
         out_specs=[vmem if held else hbm] * len(outs),
         scratch_shapes=list(scratch),
         cost_estimate=pl.CostEstimate(flops=4000, bytes_accessed=1000, transcendentals=0),
         compiler_params=pltpu.CompilerParams(vmem_limit_bytes=12 * 1024 * 1024),
     )(
+        *scalars,
         *(pltpu.with_memory_space_constraint(value, pltpu.VMEM) for value in arrays),
         *(pltpu.with_memory_space_constraint(value, pltpu.HBM) for value in raw),
         *after,
@@ -399,13 +419,10 @@
     gx, gy, reps = (lax.axis_size("gx"), lax.axis_size("gy"), lax.axis_size("rep"))
     volume = NZ * WIDE * LANES * gx * gy
     core = lax.axis_index("gx") % 2
-    spread = lambda values: jnp.broadcast_to(jnp.stack(values)[:, None, None], (len(values), 8, LANES))
-    flags = spread([core, lax.axis_index("gy") % 2]).astype(jnp.int32)
-    position = lax.axis_index("rep")
-    partner = acceptance[position]
-    first, second = (partner == position ^ 1, (partner != position) & (partner != position ^ 1))
-    choice = spread([core, first.astype(core.dtype), second.astype(core.dtype)]).astype(jnp.int32)
-    par = spread([kappa[0], quartic[0]])
+    places = [core, lax.axis_index("gy") % 2, lax.axis_index("rep")]
+    flags = jnp.broadcast_to(jnp.stack(places)[:, None, None], (3, 8, LANES)).astype(jnp.int32)
+    par = jnp.broadcast_to(jnp.concatenate([kappa, quartic])[:, None, None], (2, 8, LANES))
+    (choice,) = run(pick_kernel, [jax.ShapeDtypeStruct((3, 8, LANES), jnp.int32)], [flags], scalars=[acceptance])
 
     def far(value):
         return pair_swap(value, "gx", lambda i: (i + 1) % gx if i % 2 == 1 else (i - 1) % gx)
@@ -478,9 +495,9 @@
         outer_last,
         [f32(6, COMPS, NZ, LANES), vreg],
         [par, beyond2, hq2, hp2, z2, z3, zp3, e1, g1, h1, g2, r2, r3, start, more],
-        after=[first_early, second_early],
         scratch=[pltpu.VMEM((COMPS, NZ + 8, LANES), jnp.float32)] * 4 + [pltpu.VMEM((COMPS, NZ, LANES), jnp.float32)],
     )
+    (late,) = run(pack_kernel, [f32(6, COMPS, NZ, LANES)], [late], after=[first_early, second_early])
     first_late, second_late = exchanged(late)
 
     new_q, new_p = run(
@@ -493,16 +510,16 @@
     energy = energy + near(energy)
     moved = [pair_swap(energy, "gx", lambda i, k=k: i ^ (4 * k)) for k in range(1, gx // 4)]
     energy = sum(moved, energy)
-    energy = energy + pair_swap(energy, "gy", lambda i: i ^ 1)
+    for bit in (1, 2):
+        energy = energy + pair_swap(energy, "gy", lambda i, bit=bit: i ^ bit)
 
     def across(i_bit, j_bit):
         pairs = [(i * gy + j, (i ^ i_bit) * gy + (j ^ j_bit)) for i in range(gx) for j in range(gy)]
         return lax.ppermute(energy, ("gx", "gy"), pairs)
 
-    parts = [energy, across(0, 2), across(2, 2), across(2, 1)]
+    parts = [energy, across(2, 3)]
     placed_first = [pltpu.with_memory_space_constraint(value, pltpu.HBM) for value in (new_q, new_p)]
-    (energy,) = run(add_kernel, [vreg], parts, after=placed_first)
-    energy = (jnp.sum(energy[:2], axis=1) / volume)[None, :]
+    (energy,) = run(functools.partial(total_kernel, volume), [f32(1, 2)], parts, after=placed_first)
     return (new_q.reshape(field.shape), new_p.reshape(field.shape), energy)
 
 

time: 84.7 us -> 83.3 us (0.983)
  between operations: 4.07 us -> 2.14 us
    ppermute x21 -> x22, waiting for transfers between devices: 20.4 us -> 24.2 us  [pair_swap(): lax.ppermute(value, axis, [(i, other(i)) for i in range(lax.axis_size(axi...]
    ppermute x3 -> x1, waiting for transfers between devices: 4.58 us -> 0.97 us  [across(): return lax.ppermute(energy, ('gx', 'gy'), pairs)]
    ppermute x21 -> x22, starting transfers between devices: 37.3 us -> 40.2 us  [pair_swap(): lax.ppermute(value, axis, [(i, other(i)) for i in range(lax.axis_size(axi...]
    ppermute x3 -> x1, starting transfers between devices: 5.56 us -> 2.78 us  [across(): return lax.ppermute(energy, ('gx', 'gy'), pairs)]
    pallas_call x12 -> x14, Pallas kernels: 10.3 us -> 11.1 us  [run(): pl.pallas_call(body, out_shape=[space(out.shape, out.dtype) for out in ou...]
  transfers between devices with their start and end apart: 24 -> 23, of which waited for: 11 -> 12; matrix products, arithmetic and copies ran while one was open for 1% -> 0% of each run, Pallas kernels for 9% -> 11%
where the time goes in v3:
time: 83.3 us; the launch traced here: 82.5 us
  starting transfers between devices  43 us (52%)
  waiting for transfers between devices  25.2 us (30%)
  Pallas kernels  11.1 us (13%)
  between operations  2.14 us (3%)
  local copies, waits for them, and re-layouts  1.05 us (1%)
    ppermute x22, starting transfers between devices, pair_swap(): lax.ppermute(value, axis, [(i, other(i)) for i in range(lax.axis_size(axi...  40.2 us
    ppermute x22, waiting for transfers between devices, pair_swap(): lax.ppermute(value, axis, [(i, other(i)) for i in range(lax.axis_size(axi...  24.2 us
    pallas_call x14, Pallas kernels, run(): pl.pallas_call(body, out_shape=[space(out.shape, out.dtype) for out in ou...  11.1 us
    ppermute x1, starting transfers between devices, across(): return lax.ppermute(energy, ('gx', 'gy'), pairs)  2.78 us
  transfers between devices with their start and end apart: 23, of which 12 were waited for; matrix products, arithmetic and copies ran while one was open for 0% of the time, Pallas kernels for 11%

profile of v3, /device:TPU:2, one launch (start us, length us, event | category | flops | bytes accessed | tf_op | source)
XLA Modules:
  0.0 82.5 jit_solution(16020987610494439903)
XLA Ops:
  0.8 1.9 %shard_map.77 = (f32[4,64,128]{2,1,0:T(8,128)S(1)}, f32[4,64,128]{2,1,0:T(8,128)S(1)}, f32[4,64,128]{2,1,0:T(8,128)S(1)}, f32[4,64,128]{2,1,0:T(8,128)S(1)}, f32...) custom-call(s32[3,8,128]{2,1,0:T(8,128)S(1)} %broadcast_in_dim.4.ref, ...), custom_call_target="tpu_custom_call" | custom-call | flops 4000 | bytes 1000 | tf_op jit(solution)/shard_map/pallas_call | solution.py:397
  2.7 2.0 %collective-permute-start = (f32[4,4,8,128]{3,2,1,0:T(8,128)S(1)}, f32[4,4,8,128]{3,2,1,0:T(8,128)S(1)}, u32[]{:S(2)}, u32[]{:S(2)}) collective-permute-start(f32[4,4,8,128]{3,2,1,0:T(8,128)S(1)} %get-tuple-element.67), channel_id=1, source_target_pairs={{0,1},{1,0},{2,3},{3,2},{4,5},{5,4},{6,7},{7,6},{8,9},{9,8},{10,11... | collective-permute-start | bytes 196616 | tf_op jit(solution)/shard_map/ppermute | solution.py:415
  4.7 2.8 %collective-permute-start.1 = (f32[4,4,8,128]{3,2,1,0:T(8,128)S(1)}, f32[4,4,8,128]{3,2,1,0:T(8,128)S(1)}, u32[]{:S(2)}, u32[]{:S(2)}) collective-permute-start(f32[4,4,8,128]{3,2,1,0:T(8,128)S(1)} %get-tuple-element.68), channel_id=1, source_target_pairs={{0,3},{1,2},{2,1},{3,0},{4,7},{5,6},{6,5},{7,4},{8,11},{9,10},{10,... | collective-permute-start | bytes 196616 | tf_op jit(solution)/shard_map/ppermute | solution.py:415
  7.5 6.7 %collective-permute-start.3 = (f32[4,64,128]{2,1,0:T(8,128)S(1)}, f32[4,64,128]{2,1,0:T(8,128)S(1)}, u32[]{:S(2)}, u32[]{:S(2)}) collective-permute-start(f32[4,64,128]{2,1,0:T(8,128)S(1)} %get-tuple-element.72.refs_2_.refs_3_), channel_id=1, source_target_pairs={{0,60},{4,8},{8,4},{12,16},{16,12},{20,24},{24,20},{28,32},{32,28}... | collective-permute-start | bytes 393224 | tf_op jit(solution)/shard_map/ppermute | solution.py:415
  15.5 0.1 shard_map.78
  15.7 2.3 %collective-permute-start.2 = (f32[560,128]{1,0:T(8,128)S(1)}, f32[560,128]{1,0:T(8,128)S(1)}, u32[]{:S(2)}, u32[]{:S(2)}) collective-permute-start(f32[560,128]{1,0:T(8,128)S(1)} %get-tuple-element.71), channel_id=1, source_target_pairs={{0,60},{4,8},{8,4},{12,16},{16,12},{20,24},{24,20},{28,32},{32,28}... | collective-permute-start | bytes 860168 | tf_op jit(solution)/shard_map/ppermute | solution.py:415
  17.9 0.1 collective-permute-start.5
  18.1 1.0 %collective-permute-done.5.refs_13_ = f32[4,8,128]{2,1,0:T(8,128)S(1)} collective-permute-done((f32[4,8,128]{2,1,0:T(8,128)S(1)}, f32[4,8,128]{2,1,0:T(8,128)S(1)}, u32[]{:S(2)}, u32[]{:S(2)}) %collective-permute-start.5) | collective-permute-done | bytes 16416 | tf_op jit(solution)/shard_map/ppermute | solution.py:415
  19.2 1.3 %shard_map.79 = (f32[4,64,128]{2,1,0:T(8,128)S(1)}, f32[4,64,128]{2,1,0:T(8,128)S(1)}, f32[4,72,128]{2,1,0:T(8,128)S(1)}, f32[4,72,128]{2,1,0:T(8,128)S(1)}, f32...) custom-call(f32[2,8,128]{2,1,0:T(8,128)S(1)} %broadcast_in_dim.5.ref, ...), custom_call_target="tpu_custom_call" | custom-call | flops 4000 | bytes 1000 | tf_op jit(solution)/shard_map/pallas_call | solution.py:397
  20.5 0.3 collective-permute-start.6
  20.7 0.4 copy-done
  21.1 0.5 shard_map.76.refs_7_.refs_0_
  21.7 0.2 collective-permute-done.6.refs_6_
  21.9 0.6 shard_map.81
  22.5 0.3 collective-permute-start.7
  22.8 7.0 %collective-permute-start.9 = (f32[280,128]{1,0:T(8,128)S(1)}, f32[280,128]{1,0:T(8,128)S(1)}, u32[]{:S(2)}, u32[]{:S(2)}) collective-permute-start(f32[280,128]{1,0:T(8,128)S(1)} %get-tuple-element.99), channel_id=1, source_target_pairs={{0,60},{4,8},{8,4},{12,16},{16,12},{20,24},{24,20},{28,32},{32,28}... | collective-permute-start | bytes 430088 | tf_op jit(solution)/shard_map/ppermute | solution.py:415
  29.8 7.9 %collective-permute-done.2.refs_1_ = f32[560,128]{1,0:T(8,128)S(1)} collective-permute-done((f32[560,128]{1,0:T(8,128)S(1)}, f32[560,128]{1,0:T(8,128)S(1)}, u32[]{:S(2)}, u32[]{:S(2)}) %collective-permute-start.2) | collective-permute-done | bytes 286752 | tf_op jit(solution)/shard_map/ppermute | solution.py:415
  37.6 1.4 %shard_map.80 = (f32[4,8,128]{2,1,0:T(8,128)S(1)}, f32[4,72,128]{2,1,0:T(8,128)S(1)}, f32[4,72,128]{2,1,0:T(8,128)S(1)}, f32[4,72,128]{2,1,0:T(8,128)S(1)}, f32[...) custom-call(f32[2,8,128]{2,1,0:T(8,128)S(1)} %broadcast_in_dim.5.refs_0_, ...), custom_call_target="tpu_custom_call" | custom-call | flops 4000 | bytes 1000 | tf_op jit(solution)/shard_map/pallas_call | solution.py:397
  39.0 1.0 %shard_map.82 = (f32[4,72,128]{2,1,0:T(8,128)S(1)}, f32[4,72,128]{2,1,0:T(8,128)S(1)}, f32[4,72,128]{2,1,0:T(8,128)S(1)}, f32[4,72,128]{2,1,0:T(8,128)S(1)}, f32...) custom-call(f32[2,8,128]{2,1,0:T(8,128)S(1)} %broadcast_in_dim.5.refs_0_, ...), custom_call_target="tpu_custom_call" | custom-call | flops 4000 | bytes 1000 | tf_op jit(solution)/shard_map/pallas_call | solution.py:397
  40.1 0.8 collective-permute-start.10
  40.8 3.0 %collective-permute-start.8 = (f32[528,128]{1,0:T(8,128)S(1)}, f32[528,128]{1,0:T(8,128)S(1)}, u32[]{:S(2)}, u32[]{:S(2)}) collective-permute-start(f32[528,128]{1,0:T(8,128)S(1)} %get-tuple-element.98), channel_id=1, source_target_pairs={{0,60},{4,8},{8,4},{12,16},{16,12},{20,24},{24,20},{28,32},{32,28}... | collective-permute-start | bytes 811016 | tf_op jit(solution)/shard_map/ppermute | solution.py:415
  43.8 0.6 shard_map.84
  44.4 0.6 collective-permute-start.12
  45.1 4.1 %collective-permute-start.13 = (f32[2,4,64,128]{3,2,1,0:T(8,128)S(1)}, f32[2,4,64,128]{3,2,1,0:T(8,128)S(1)}, u32[]{:S(2)}, u32[]{:S(2)}) collective-permute-start(f32[2,4,64,128]{3,2,1,0:T(8,128)S(1)} %get-tuple-element.127.refs_4_), channel_id=1, source_target_pairs={{64,128},{128,64},{65,129},{129,65},{66,130},{130,66},{67,131},{13... | collective-permute-start | bytes 786440 | tf_op jit(solution)/shard_map/ppermute | solution.py:415
  49.1 0.3 collective-permute-start.11
  49.4 1.1 %shard_map.83 = (f32[4,72,128]{2,1,0:T(8,128)S(1)}, f32[4,72,128]{2,1,0:T(8,128)S(1)}, f32[4,72,128]{2,1,0:T(8,128)S(1)}, f32[4,72,128]{2,1,0:T(8,128)S(1)}, f32...) custom-call(f32[2,8,128]{2,1,0:T(8,128)S(1)} %broadcast_in_dim.5.refs_0_, ...), custom_call_target="tpu_custom_call" | custom-call | flops 4000 | bytes 1000 | tf_op jit(solution)/shard_map/pallas_call | solution.py:397
  50.5 0.2 collective-permute-done.11.refs_6_
  50.7 0.4 shard_map.85
  51.1 5.1 %collective-permute-done.8.refs_1_ = f32[528,128]{1,0:T(8,128)S(1)} collective-permute-done((f32[528,128]{1,0:T(8,128)S(1)}, f32[528,128]{1,0:T(8,128)S(1)}, u32[]{:S(2)}, u32[]{:S(2)}) %collective-permute-start.8) | collective-permute-done | bytes 270368 | tf_op jit(solution)/shard_map/ppermute | solution.py:415
  56.2 1.0 %shard_map.86 = (f32[6,4,64,128]{3,2,1,0:T(8,128)S(1)}, f32[8,128]{1,0:T(8,128)S(1)}) custom-call(f32[2,8,128]{2,1,0:T(8,128)S(1)} %broadcast_in_dim.5.refs_0_, f32[528,128]{1,0:T(8,128)S(1)} %collective-permute-done.8.refs_1_, f32[4,72,128]{2,1,0:T(8,128)S(1)} %get-tuple-element.107.refs_2_, f32[4,72,128]{2,1,0:T(8,128)S(1)} %get-tuple-element.108.refs_3_, ...), custom_call_target="tpu_custom_call" | custom-call | flops 4000 | bytes 1000 | tf_op jit(solution)/shard_map/pallas_call | solution.py:397
  57.3 0.6 collective-permute-start.14
  58.0 4.0 %collective-permute-start.15 = (f32[6,4,64,128]{3,2,1,0:T(8,128)S(1)}, f32[6,4,64,128]{3,2,1,0:T(8,128)S(1)}, u32[]{:S(2)}, u32[]{:S(2)}) collective-permute-start(f32[6,4,64,128]{3,2,1,0:T(8,128)S(1)} %shard_map.87.refs_1_), channel_id=1, source_target_pairs={{64,128},{128,64},{65,129},{129,65},{66,130},{130,66},{67,131},{13... | collective-permute-start | bytes 2359304 | tf_op jit(solution)/shard_map/ppermute | solution.py:415
  62.0 0.1 collective-permute-start.16
  62.1 1.2 %collective-permute-done.16 = f32[8,128]{1,0:T(8,128)S(1)} collective-permute-done((f32[8,128]{1,0:T(8,128)S(1)}, f32[8,128]{1,0:T(8,128)S(1)}, u32[]{:S(2)}, u32[]{:S(2)}) %collective-permute-start.16) | collective-permute-done | bytes 4128 | tf_op jit(solution)/shard_map/ppermute | solution.py:415
  63.3 0.4 collective-permute-start.19
  63.7 0.8 collective-permute-start.18
  64.5 2.9 %collective-permute-start.17 = (f32[8,128]{1,0:T(8,128)S(1)}, f32[8,128]{1,0:T(8,128)S(1)}, u32[]{:S(2)}, u32[]{:S(2)}) collective-permute-start(f32[8,128]{1,0:T(8,128)S(1)} %add.27), channel_id=1, source_target_pairs={{0,16},{4,20},{8,24},{12,28},{16,0},{20,4},{24,8},{28,12},{32,48},... | collective-permute-start | bytes 12296 | tf_op jit(solution)/shard_map/ppermute | solution.py:415
  67.4 0.7 collective-permute-done.19
  68.1 0.7 collective-permute-done.18
  68.8 0.2 collective-permute-done.17
  69.0 3.6 %collective-permute-done.20 = f32[8,128]{1,0:T(8,128)S(1)} collective-permute-done((f32[8,128]{1,0:T(8,128)S(1)}, f32[8,128]{1,0:T(8,128)S(1)}, u32[]{:S(2)}, u32[]{:S(2)}) %collective-permute-start.20) | collective-permute-done | bytes 4128 | tf_op jit(solution)/shard_map/ppermute | solution.py:415
  72.6 1.2 %collective-permute-start.21 = (f32[8,128]{1,0:T(8,128)S(1)}, f32[8,128]{1,0:T(8,128)S(1)}, u32[]{:S(2)}, u32[]{:S(2)}) collective-permute-start(f32[8,128]{1,0:T(8,128)S(1)} %add.31), channel_id=1, source_target_pairs={{0,2},{1,3},{2,0},{3,1},{4,6},{5,7},{6,4},{7,5},{8,10},{9,11},{10,... | collective-permute-start | bytes 12296 | tf_op jit(solution)/shard_map/ppermute | solution.py:415
  73.8 3.3 %collective-permute-done.21 = f32[8,128]{1,0:T(8,128)S(1)} collective-permute-done((f32[8,128]{1,0:T(8,128)S(1)}, f32[8,128]{1,0:T(8,128)S(1)}, u32[]{:S(2)}, u32[]{:S(2)}) %collective-permute-start.21) | collective-permute-done | bytes 4128 | tf_op jit(solution)/shard_map/ppermute | solution.py:415
  77.1 2.8 %collective-permute-start.22 = (f32[8,128]{1,0:T(8,128)S(1)}, f32[8,128]{1,0:T(8,128)S(1)}, u32[]{:S(2)}, u32[]{:S(2)}) collective-permute-start(f32[8,128]{1,0:T(8,128)S(1)} %add.32.refs_0_), channel_id=1, source_target_pairs={{0,11},{1,10},{2,9},{3,8},{4,15},{5,14},{6,13},{7,12},{8,3},{9,2},... | collective-permute-start | bytes 12296 | tf_op jit(solution)/shard_map/ppermute | solution.py:518
  79.9 1.0 %shard_map.88 = (f32[4,256,128]{2,1,0:T(8,128)}, f32[4,256,128]{2,1,0:T(8,128)}) custom-call(s32[3,8,128]{2,1,0:T(8,128)S(1)} %shard_map.76.refs_7_.refs_0_, f32[6,4,64,128]{3,2,1,0:T(8,128)S(1)} %shard_map.87.refs_1_, f32[6,4,64,128]{3,2,1,0:T(8,128)S(1)} %collective-permute-done.14.refs_2_, f32[6,4,64,128]{3,2,1,0:T(8,128)S(1)} %collective-permute-done.15.refs_3_, ...), custom_call_target="tpu_custom_call" | custom-call | flops 4000 | bytes 1000 | tf_op jit(solution)/shard_map/pallas_call | solution.py:397
  81.0 1.0 %collective-permute-done.22.refs_1_ = f32[8,128]{1,0:T(8,128)S(1)} collective-permute-done((f32[8,128]{1,0:T(8,128)S(1)}, f32[8,128]{1,0:T(8,128)S(1)}, u32[]{:S(2)}, u32[]{:S(2)}) %collective-permute-start.22) | collective-permute-done | bytes 4128 | tf_op jit(solution)/shard_map/ppermute | solution.py:518
  82.0 0.1 shard_map.89
  82.0 0.5 copy.8
  (23 shorter events, 0.4 us)
Async XLA Ops:
  2.7 12.8 %collective-permute-start = (f32[4,4,8,128]{3,2,1,0:T(8,128)S(1)}, f32[4,4,8,128]{3,2,1,0:T(8,128)S(1)}, u32[]{:S(2)}, u32[]{:S(2)}) collective-permute-start(f32[4,4,8,128]{3,2,1,0:T(8,128)S(1)} %get-tuple-element.67), channel_id=1, source_target_pairs={{0,1},{1,0},{2,3},{3,2},{4,5},{5,4},{6,7},{7,6},{8,9},{9,8},{10,11... | collective-permute-start | bytes 196616 | tf_op jit(solution)/shard_map/ppermute | solution.py:415
  4.7 10.9 %collective-permute-start.1 = (f32[4,4,8,128]{3,2,1,0:T(8,128)S(1)}, f32[4,4,8,128]{3,2,1,0:T(8,128)S(1)}, u32[]{:S(2)}, u32[]{:S(2)}) collective-permute-start(f32[4,4,8,128]{3,2,1,0:T(8,128)S(1)} %get-tuple-element.68), channel_id=1, source_target_pairs={{0,3},{1,2},{2,1},{3,0},{4,7},{5,6},{6,5},{7,4},{8,11},{9,10},{10,... | collective-permute-start | bytes 196616 | tf_op jit(solution)/shard_map/ppermute | solution.py:415
  7.5 11.6 %collective-permute-start.3 = (f32[4,64,128]{2,1,0:T(8,128)S(1)}, f32[4,64,128]{2,1,0:T(8,128)S(1)}, u32[]{:S(2)}, u32[]{:S(2)}) collective-permute-start(f32[4,64,128]{2,1,0:T(8,128)S(1)} %get-tuple-element.72.refs_2_.refs_3_), channel_id=1, source_target_pairs={{0,60},{4,8},{8,4},{12,16},{16,12},{20,24},{24,20},{28,32},{32,28}... | collective-permute-start | bytes 393224 | tf_op jit(solution)/shard_map/ppermute | solution.py:415
  14.2 4.9 %collective-permute-start.4 = (f32[4,64,128]{2,1,0:T(8,128)S(1)}, f32[4,64,128]{2,1,0:T(8,128)S(1)}, u32[]{:S(2)}, u32[]{:S(2)}) collective-permute-start(f32[4,64,128]{2,1,0:T(8,128)S(1)} %get-tuple-element.76.refs_5_), channel_id=1, source_target_pairs={{0,4},{4,0},{8,12},{12,8},{16,20},{20,16},{24,28},{28,24},{32,36},... | collective-permute-start | bytes 393224 | tf_op jit(solution)/shard_map/ppermute | solution.py:415
  15.7 22.0 %collective-permute-start.2 = (f32[560,128]{1,0:T(8,128)S(1)}, f32[560,128]{1,0:T(8,128)S(1)}, u32[]{:S(2)}, u32[]{:S(2)}) collective-permute-start(f32[560,128]{1,0:T(8,128)S(1)} %get-tuple-element.71), channel_id=1, source_target_pairs={{0,60},{4,8},{8,4},{12,16},{16,12},{20,24},{24,20},{28,32},{32,28}... | collective-permute-start | bytes 860168 | tf_op jit(solution)/shard_map/ppermute | solution.py:415
  17.9 1.2 %collective-permute-start.5 = (f32[4,8,128]{2,1,0:T(8,128)S(1)}, f32[4,8,128]{2,1,0:T(8,128)S(1)}, u32[]{:S(2)}, u32[]{:S(2)}) collective-permute-start(f32[4,8,128]{2,1,0:T(8,128)S(1)} %get-tuple-element.80), channel_id=1, source_target_pairs={{0,4},{4,0},{8,12},{12,8},{16,20},{20,16},{24,28},{28,24},{32,36},... | collective-permute-start | bytes 49160 | tf_op jit(solution)/shard_map/ppermute | solution.py:415
  20.5 0.7 copy-start
  20.5 1.4 %collective-permute-start.6 = (f32[272,128]{1,0:T(8,128)S(1)}, f32[272,128]{1,0:T(8,128)S(1)}, u32[]{:S(2)}, u32[]{:S(2)}) collective-permute-start(f32[272,128]{1,0:T(8,128)S(1)} %get-tuple-element.92), channel_id=1, source_target_pairs={{0,4},{4,0},{8,12},{12,8},{16,20},{20,16},{24,28},{28,24},{32,36},... | collective-permute-start | bytes 417800 | tf_op jit(solution)/shard_map/ppermute | solution.py:415
  22.5 16.5 %collective-permute-start.7 = (f32[272,128]{1,0:T(8,128)S(1)}, f32[272,128]{1,0:T(8,128)S(1)}, u32[]{:S(2)}, u32[]{:S(2)}) collective-permute-start(f32[272,128]{1,0:T(8,128)S(1)} %get-tuple-element.97), channel_id=1, source_target_pairs={{0,4},{4,0},{8,12},{12,8},{16,20},{20,16},{24,28},{28,24},{32,36},... | collective-permute-start | bytes 417800 | tf_op jit(solution)/shard_map/ppermute | solution.py:415
  22.8 21.0 %collective-permute-start.9 = (f32[280,128]{1,0:T(8,128)S(1)}, f32[280,128]{1,0:T(8,128)S(1)}, u32[]{:S(2)}, u32[]{:S(2)}) collective-permute-start(f32[280,128]{1,0:T(8,128)S(1)} %get-tuple-element.99), channel_id=1, source_target_pairs={{0,60},{4,8},{8,4},{12,16},{16,12},{20,24},{24,20},{28,32},{32,28}... | collective-permute-start | bytes 430088 | tf_op jit(solution)/shard_map/ppermute | solution.py:415
  40.1 3.8 %collective-permute-start.10 = (f32[272,128]{1,0:T(8,128)S(1)}, f32[272,128]{1,0:T(8,128)S(1)}, u32[]{:S(2)}, u32[]{:S(2)}) collective-permute-start(f32[272,128]{1,0:T(8,128)S(1)} %get-tuple-element.116), channel_id=1, source_target_pairs={{0,4},{4,0},{8,12},{12,8},{16,20},{20,16},{24,28},{28,24},{32,36},... | collective-permute-start | bytes 417800 | tf_op jit(solution)/shard_map/ppermute | solution.py:415
  40.8 15.4 %collective-permute-start.8 = (f32[528,128]{1,0:T(8,128)S(1)}, f32[528,128]{1,0:T(8,128)S(1)}, u32[]{:S(2)}, u32[]{:S(2)}) collective-permute-start(f32[528,128]{1,0:T(8,128)S(1)} %get-tuple-element.98), channel_id=1, source_target_pairs={{0,60},{4,8},{8,4},{12,16},{16,12},{20,24},{24,20},{28,32},{32,28}... | collective-permute-start | bytes 811016 | tf_op jit(solution)/shard_map/ppermute | solution.py:415
  44.4 12.8 %collective-permute-start.12 = (f32[2,4,64,128]{3,2,1,0:T(8,128)S(1)}, f32[2,4,64,128]{3,2,1,0:T(8,128)S(1)}, u32[]{:S(2)}, u32[]{:S(2)}) collective-permute-start(f32[2,4,64,128]{3,2,1,0:T(8,128)S(1)} %get-tuple-element.127.refs_4_), channel_id=1, source_target_pairs={{0,64},{64,0},{128,192},{192,128},{1,65},{65,1},{129,193},{193,129... | collective-permute-start | bytes 786440 | tf_op jit(solution)/shard_map/ppermute | solution.py:415
  45.1 12.2 %collective-permute-start.13 = (f32[2,4,64,128]{3,2,1,0:T(8,128)S(1)}, f32[2,4,64,128]{3,2,1,0:T(8,128)S(1)}, u32[]{:S(2)}, u32[]{:S(2)}) collective-permute-start(f32[2,4,64,128]{3,2,1,0:T(8,128)S(1)} %get-tuple-element.127.refs_4_), channel_id=1, source_target_pairs={{64,128},{128,64},{65,129},{129,65},{66,130},{130,66},{67,131},{13... | collective-permute-start | bytes 786440 | tf_op jit(solution)/shard_map/ppermute | solution.py:415
  49.1 1.6 %collective-permute-start.11 = (f32[256,128]{1,0:T(8,128)S(1)}, f32[256,128]{1,0:T(8,128)S(1)}, u32[]{:S(2)}, u32[]{:S(2)}) collective-permute-start(f32[256,128]{1,0:T(8,128)S(1)} %get-tuple-element.121), channel_id=1, source_target_pairs={{0,4},{4,0},{8,12},{12,8},{16,20},{20,16},{24,28},{28,24},{32,36},... | collective-permute-start | bytes 393224 | tf_op jit(solution)/shard_map/ppermute | solution.py:415
  57.3 22.6 %collective-permute-start.14 = (f32[6,4,64,128]{3,2,1,0:T(8,128)S(1)}, f32[6,4,64,128]{3,2,1,0:T(8,128)S(1)}, u32[]{:S(2)}, u32[]{:S(2)}) collective-permute-start(f32[6,4,64,128]{3,2,1,0:T(8,128)S(1)} %shard_map.87.refs_1_), channel_id=1, source_target_pairs={{0,64},{64,0},{128,192},{192,128},{1,65},{65,1},{129,193},{193,129... | collective-permute-start | bytes 2359304 | tf_op jit(solution)/shard_map/ppermute | solution.py:415
  58.0 22.0 %collective-permute-start.15 = (f32[6,4,64,128]{3,2,1,0:T(8,128)S(1)}, f32[6,4,64,128]{3,2,1,0:T(8,128)S(1)}, u32[]{:S(2)}, u32[]{:S(2)}) collective-permute-start(f32[6,4,64,128]{3,2,1,0:T(8,128)S(1)} %shard_map.87.refs_1_), channel_id=1, source_target_pairs={{64,128},{128,64},{65,129},{129,65},{66,130},{130,66},{67,131},{13... | collective-permute-start | bytes 2359304 | tf_op jit(solution)/shard_map/ppermute | solution.py:415
  62.0 1.3 %collective-permute-start.16 = (f32[8,128]{1,0:T(8,128)S(1)}, f32[8,128]{1,0:T(8,128)S(1)}, u32[]{:S(2)}, u32[]{:S(2)}) collective-permute-start(f32[8,128]{1,0:T(8,128)S(1)} %get-tuple-element.130), channel_id=1, source_target_pairs={{0,4},{4,0},{8,12},{12,8},{16,20},{20,16},{24,28},{28,24},{32,36},... | collective-permute-start | bytes 12296 | tf_op jit(solution)/shard_map/ppermute | solution.py:415
  63.3 4.8 %collective-permute-start.19 = (f32[8,128]{1,0:T(8,128)S(1)}, f32[8,128]{1,0:T(8,128)S(1)}, u32[]{:S(2)}, u32[]{:S(2)}) collective-permute-start(f32[8,128]{1,0:T(8,128)S(1)} %add.27), channel_id=1, source_target_pairs={{0,48},{4,52},{8,56},{12,60},{16,32},{20,36},{24,40},{28,44},{32,1... | collective-permute-start | bytes 12296 | tf_op jit(solution)/shard_map/ppermute | solution.py:415
  63.7 5.1 %collective-permute-start.18 = (f32[8,128]{1,0:T(8,128)S(1)}, f32[8,128]{1,0:T(8,128)S(1)}, u32[]{:S(2)}, u32[]{:S(2)}) collective-permute-start(f32[8,128]{1,0:T(8,128)S(1)} %add.27), channel_id=1, source_target_pairs={{0,32},{4,36},{8,40},{12,44},{16,48},{20,52},{24,56},{28,60},{32,0... | collective-permute-start | bytes 12296 | tf_op jit(solution)/shard_map/ppermute | solution.py:415
  64.5 4.5 %collective-permute-start.17 = (f32[8,128]{1,0:T(8,128)S(1)}, f32[8,128]{1,0:T(8,128)S(1)}, u32[]{:S(2)}, u32[]{:S(2)}) collective-permute-start(f32[8,128]{1,0:T(8,128)S(1)} %add.27), channel_id=1, source_target_pairs={{0,16},{4,20},{8,24},{12,28},{16,0},{20,4},{24,8},{28,12},{32,48},... | collective-permute-start | bytes 12296 | tf_op jit(solution)/shard_map/ppermute | solution.py:415
  69.0 3.6 %collective-permute-start.20 = (f32[8,128]{1,0:T(8,128)S(1)}, f32[8,128]{1,0:T(8,128)S(1)}, u32[]{:S(2)}, u32[]{:S(2)}) collective-permute-start(f32[8,128]{1,0:T(8,128)S(1)} %add_add_fusion), channel_id=1, source_target_pairs={{0,1},{1,0},{2,3},{3,2},{4,5},{5,4},{6,7},{7,6},{8,9},{9,8},{10,11... | collective-permute-start | bytes 12296 | tf_op jit(solution)/shard_map/ppermute | solution.py:415
  72.6 4.5 %collective-permute-start.21 = (f32[8,128]{1,0:T(8,128)S(1)}, f32[8,128]{1,0:T(8,128)S(1)}, u32[]{:S(2)}, u32[]{:S(2)}) collective-permute-start(f32[8,128]{1,0:T(8,128)S(1)} %add.31), channel_id=1, source_target_pairs={{0,2},{1,3},{2,0},{3,1},{4,6},{5,7},{6,4},{7,5},{8,10},{9,11},{10,... | collective-permute-start | bytes 12296 | tf_op jit(solution)/shard_map/ppermute | solution.py:415
  77.1 4.8 %collective-permute-start.22 = (f32[8,128]{1,0:T(8,128)S(1)}, f32[8,128]{1,0:T(8,128)S(1)}, u32[]{:S(2)}, u32[]{:S(2)}) collective-permute-start(f32[8,128]{1,0:T(8,128)S(1)} %add.32.refs_0_), channel_id=1, source_target_pairs={{0,11},{1,10},{2,9},{3,8},{4,15},{5,14},{6,13},{7,12},{8,3},{9,2},... | collective-permute-start | bytes 12296 | tf_op jit(solution)/shard_map/ppermute | solution.py:518

commit v4 on v3

--- a/solution.py
+++ b/solution.py
@@ -507,17 +507,14 @@
         scratch=[pltpu.VMEM((2, COMPS, NZ * WIDE, LANES), jnp.float32), pltpu.SemaphoreType.DMA((2, COMPS))],
         held=False,
     )
-    energy = energy + near(energy)
-    moved = [pair_swap(energy, "gx", lambda i, k=k: i ^ (4 * k)) for k in range(1, gx // 4)]
-    energy = sum(moved, energy)
-    for bit in (1, 2):
-        energy = energy + pair_swap(energy, "gy", lambda i, bit=bit: i ^ bit)
-
-    def across(i_bit, j_bit):
-        pairs = [(i * gy + j, (i ^ i_bit) * gy + (j ^ j_bit)) for i in range(gx) for j in range(gy)]
-        return lax.ppermute(energy, ("gx", "gy"), pairs)
-
-    parts = [energy, across(2, 3)]
+    def across(value, i_bits, j_bits):
+        pairs = [(i * gy + j, (i ^ i_bits) * gy + (j ^ j_bits)) for i in range(gx) for j in range(gy)]
+        return lax.ppermute(value, ("gx", "gy"), pairs)
+
+    energy = sum([across(energy, 4 * k, 0) for k in range(1, gx // 4)], energy)
+    energy = energy + near(energy) + across(energy, 0, 1) + across(energy, 1, 1)
+    energy = energy + across(energy, 0, 2)
+    parts = [energy, across(energy, 2, 3)]
     placed_first = [pltpu.with_memory_space_constraint(value, pltpu.HBM) for value in (new_q, new_p)]
     (energy,) = run(functools.partial(total_kernel, volume), [f32(1, 2)], parts, after=placed_first)
     return (new_q.reshape(field.shape), new_p.reshape(field.shape), energy)

time: 83.3 us -> 82.3 us (0.988)
  waiting for transfers between devices: 25.2 us -> 22.2 us
  starting transfers between devices: 43 us -> 44.9 us
    ppermute x22 -> x17, waiting for transfers between devices: 24.2 us -> 14.5 us  [pair_swap(): lax.ppermute(value, axis, [(i, other(i)) for i in range(lax.axis_size(axi...]
    ppermute x1 -> x7, waiting for transfers between devices: 0.97 us -> 7.74 us  [across(): return lax.ppermute(value, ('gx', 'gy'), pairs)]
    ppermute x1 -> x7, starting transfers between devices: 2.78 us -> 8.35 us  [across(): return lax.ppermute(value, ('gx', 'gy'), pairs)]
    ppermute x22 -> x17, starting transfers between devices: 40.2 us -> 36.5 us  [pair_swap(): lax.ppermute(value, axis, [(i, other(i)) for i in range(lax.axis_size(axi...]
  transfers between devices with their start and end apart: 23 -> 24, of which waited for: 12 -> 12; matrix products, arithmetic and copies ran while one was open for 0% -> 0% of each run, Pallas kernels for 11% -> 11%
where the time goes in v4:
time: 82.3 us; the launch traced here: 81.6 us
  starting transfers between devices  44.9 us (55%)
  waiting for transfers between devices  22.2 us (27%)
  Pallas kernels  11.1 us (13%)
  between operations  2.14 us (3%)
  local copies, waits for them, and re-layouts  1.05 us (1%)
    ppermute x17, starting transfers between devices, pair_swap(): lax.ppermute(value, axis, [(i, other(i)) for i in range(lax.axis_size(axi...  36.5 us
    ppermute x17, waiting for transfers between devices, pair_swap(): lax.ppermute(value, axis, [(i, other(i)) for i in range(lax.axis_size(axi...  14.5 us
    pallas_call x14, Pallas kernels, run(): pl.pallas_call(body, out_shape=[space(out.shape, out.dtype) for out in ou...  11.1 us
    ppermute x7, starting transfers between devices, across(): return lax.ppermute(value, ('gx', 'gy'), pairs)  8.35 us
    ppermute x7, waiting for transfers between devices, across(): return lax.ppermute(value, ('gx', 'gy'), pairs)  7.74 us
  transfers between devices with their start and end apart: 24, of which 12 were waited for; matrix products, arithmetic and copies ran while one was open for 0% of the time, Pallas kernels for 11%

profile of v4, /device:TPU:2, one launch (start us, length us, event | category | flops | bytes accessed | tf_op | source)
XLA Modules:
  0.0 81.6 jit_solution(14057085800235123180)
XLA Ops:
  0.8 1.9 %shard_map.77 = (f32[4,64,128]{2,1,0:T(8,128)S(1)}, f32[4,64,128]{2,1,0:T(8,128)S(1)}, f32[4,64,128]{2,1,0:T(8,128)S(1)}, f32[4,64,128]{2,1,0:T(8,128)S(1)}, f32...) custom-call(s32[3,8,128]{2,1,0:T(8,128)S(1)} %broadcast_in_dim.4.ref, ...), custom_call_target="tpu_custom_call" | custom-call | flops 4000 | bytes 1000 | tf_op jit(solution)/shard_map/pallas_call | solution.py:397
  2.7 2.0 %collective-permute-start = (f32[4,4,8,128]{3,2,1,0:T(8,128)S(1)}, f32[4,4,8,128]{3,2,1,0:T(8,128)S(1)}, u32[]{:S(2)}, u32[]{:S(2)}) collective-permute-start(f32[4,4,8,128]{3,2,1,0:T(8,128)S(1)} %get-tuple-element.67), channel_id=1, source_target_pairs={{0,1},{1,0},{2,3},{3,2},{4,5},{5,4},{6,7},{7,6},{8,9},{9,8},{10,11... | collective-permute-start | bytes 196616 | tf_op jit(solution)/shard_map/ppermute | solution.py:415
  4.7 2.8 %collective-permute-start.1 = (f32[4,4,8,128]{3,2,1,0:T(8,128)S(1)}, f32[4,4,8,128]{3,2,1,0:T(8,128)S(1)}, u32[]{:S(2)}, u32[]{:S(2)}) collective-permute-start(f32[4,4,8,128]{3,2,1,0:T(8,128)S(1)} %get-tuple-element.68), channel_id=1, source_target_pairs={{0,3},{1,2},{2,1},{3,0},{4,7},{5,6},{6,5},{7,4},{8,11},{9,10},{10,... | collective-permute-start | bytes 196616 | tf_op jit(solution)/shard_map/ppermute | solution.py:415
  7.5 6.7 %collective-permute-start.3 = (f32[4,64,128]{2,1,0:T(8,128)S(1)}, f32[4,64,128]{2,1,0:T(8,128)S(1)}, u32[]{:S(2)}, u32[]{:S(2)}) collective-permute-start(f32[4,64,128]{2,1,0:T(8,128)S(1)} %get-tuple-element.72.refs_2_.refs_3_), channel_id=1, source_target_pairs={{0,60},{4,8},{8,4},{12,16},{16,12},{20,24},{24,20},{28,32},{32,28}... | collective-permute-start | bytes 393224 | tf_op jit(solution)/shard_map/ppermute | solution.py:415
  15.5 0.1 shard_map.78
  15.7 2.3 %collective-permute-start.2 = (f32[560,128]{1,0:T(8,128)S(1)}, f32[560,128]{1,0:T(8,128)S(1)}, u32[]{:S(2)}, u32[]{:S(2)}) collective-permute-start(f32[560,128]{1,0:T(8,128)S(1)} %get-tuple-element.71), channel_id=1, source_target_pairs={{0,60},{4,8},{8,4},{12,16},{16,12},{20,24},{24,20},{28,32},{32,28}... | collective-permute-start | bytes 860168 | tf_op jit(solution)/shard_map/ppermute | solution.py:415
  17.9 0.1 collective-permute-start.5
  18.1 1.0 %collective-permute-done.5.refs_13_ = f32[4,8,128]{2,1,0:T(8,128)S(1)} collective-permute-done((f32[4,8,128]{2,1,0:T(8,128)S(1)}, f32[4,8,128]{2,1,0:T(8,128)S(1)}, u32[]{:S(2)}, u32[]{:S(2)}) %collective-permute-start.5) | collective-permute-done | bytes 16416 | tf_op jit(solution)/shard_map/ppermute | solution.py:415
  19.2 1.3 %shard_map.79 = (f32[4,64,128]{2,1,0:T(8,128)S(1)}, f32[4,64,128]{2,1,0:T(8,128)S(1)}, f32[4,72,128]{2,1,0:T(8,128)S(1)}, f32[4,72,128]{2,1,0:T(8,128)S(1)}, f32...) custom-call(f32[2,8,128]{2,1,0:T(8,128)S(1)} %broadcast_in_dim.5.ref, ...), custom_call_target="tpu_custom_call" | custom-call | flops 4000 | bytes 1000 | tf_op jit(solution)/shard_map/pallas_call | solution.py:397
  20.5 0.3 collective-permute-start.6
  20.7 0.4 copy-done
  21.1 0.5 shard_map.76.refs_7_.refs_0_
  21.7 0.2 collective-permute-done.6.refs_6_
  21.9 0.6 shard_map.81
  22.5 0.3 collective-permute-start.7
  22.8 7.0 %collective-permute-start.9 = (f32[280,128]{1,0:T(8,128)S(1)}, f32[280,128]{1,0:T(8,128)S(1)}, u32[]{:S(2)}, u32[]{:S(2)}) collective-permute-start(f32[280,128]{1,0:T(8,128)S(1)} %get-tuple-element.99), channel_id=1, source_target_pairs={{0,60},{4,8},{8,4},{12,16},{16,12},{20,24},{24,20},{28,32},{32,28}... | collective-permute-start | bytes 430088 | tf_op jit(solution)/shard_map/ppermute | solution.py:415
  29.8 7.9 %collective-permute-done.2.refs_1_ = f32[560,128]{1,0:T(8,128)S(1)} collective-permute-done((f32[560,128]{1,0:T(8,128)S(1)}, f32[560,128]{1,0:T(8,128)S(1)}, u32[]{:S(2)}, u32[]{:S(2)}) %collective-permute-start.2) | collective-permute-done | bytes 286752 | tf_op jit(solution)/shard_map/ppermute | solution.py:415
  37.6 1.4 %shard_map.80 = (f32[4,8,128]{2,1,0:T(8,128)S(1)}, f32[4,72,128]{2,1,0:T(8,128)S(1)}, f32[4,72,128]{2,1,0:T(8,128)S(1)}, f32[4,72,128]{2,1,0:T(8,128)S(1)}, f32[...) custom-call(f32[2,8,128]{2,1,0:T(8,128)S(1)} %broadcast_in_dim.5.refs_0_, ...), custom_call_target="tpu_custom_call" | custom-call | flops 4000 | bytes 1000 | tf_op jit(solution)/shard_map/pallas_call | solution.py:397
  39.0 1.0 %shard_map.82 = (f32[4,72,128]{2,1,0:T(8,128)S(1)}, f32[4,72,128]{2,1,0:T(8,128)S(1)}, f32[4,72,128]{2,1,0:T(8,128)S(1)}, f32[4,72,128]{2,1,0:T(8,128)S(1)}, f32...) custom-call(f32[2,8,128]{2,1,0:T(8,128)S(1)} %broadcast_in_dim.5.refs_0_, ...), custom_call_target="tpu_custom_call" | custom-call | flops 4000 | bytes 1000 | tf_op jit(solution)/shard_map/pallas_call | solution.py:397
  40.1 0.8 collective-permute-start.10
  40.8 3.0 %collective-permute-start.8 = (f32[528,128]{1,0:T(8,128)S(1)}, f32[528,128]{1,0:T(8,128)S(1)}, u32[]{:S(2)}, u32[]{:S(2)}) collective-permute-start(f32[528,128]{1,0:T(8,128)S(1)} %get-tuple-element.98), channel_id=1, source_target_pairs={{0,60},{4,8},{8,4},{12,16},{16,12},{20,24},{24,20},{28,32},{32,28}... | collective-permute-start | bytes 811016 | tf_op jit(solution)/shard_map/ppermute | solution.py:415
  43.8 0.6 shard_map.84
  44.4 0.6 collective-permute-start.12
  45.1 4.1 %collective-permute-start.13 = (f32[2,4,64,128]{3,2,1,0:T(8,128)S(1)}, f32[2,4,64,128]{3,2,1,0:T(8,128)S(1)}, u32[]{:S(2)}, u32[]{:S(2)}) collective-permute-start(f32[2,4,64,128]{3,2,1,0:T(8,128)S(1)} %get-tuple-element.127.refs_4_), channel_id=1, source_target_pairs={{64,128},{128,64},{65,129},{129,65},{66,130},{130,66},{67,131},{13... | collective-permute-start | bytes 786440 | tf_op jit(solution)/shard_map/ppermute | solution.py:415
  49.1 0.3 collective-permute-start.11
  49.4 1.1 %shard_map.83 = (f32[4,72,128]{2,1,0:T(8,128)S(1)}, f32[4,72,128]{2,1,0:T(8,128)S(1)}, f32[4,72,128]{2,1,0:T(8,128)S(1)}, f32[4,72,128]{2,1,0:T(8,128)S(1)}, f32...) custom-call(f32[2,8,128]{2,1,0:T(8,128)S(1)} %broadcast_in_dim.5.refs_0_, ...), custom_call_target="tpu_custom_call" | custom-call | flops 4000 | bytes 1000 | tf_op jit(solution)/shard_map/pallas_call | solution.py:397
  50.5 0.2 collective-permute-done.11.refs_6_
  50.7 0.4 shard_map.85
  51.1 5.1 %collective-permute-done.8.refs_1_ = f32[528,128]{1,0:T(8,128)S(1)} collective-permute-done((f32[528,128]{1,0:T(8,128)S(1)}, f32[528,128]{1,0:T(8,128)S(1)}, u32[]{:S(2)}, u32[]{:S(2)}) %collective-permute-start.8) | collective-permute-done | bytes 270368 | tf_op jit(solution)/shard_map/ppermute | solution.py:415
  56.2 1.0 %shard_map.86 = (f32[6,4,64,128]{3,2,1,0:T(8,128)S(1)}, f32[8,128]{1,0:T(8,128)S(1)}) custom-call(f32[2,8,128]{2,1,0:T(8,128)S(1)} %broadcast_in_dim.5.refs_0_, f32[528,128]{1,0:T(8,128)S(1)} %collective-permute-done.8.refs_1_, f32[4,72,128]{2,1,0:T(8,128)S(1)} %get-tuple-element.107.refs_2_, f32[4,72,128]{2,1,0:T(8,128)S(1)} %get-tuple-element.108.refs_3_, ...), custom_call_target="tpu_custom_call" | custom-call | flops 4000 | bytes 1000 | tf_op jit(solution)/shard_map/pallas_call | solution.py:397
  57.3 0.6 collective-permute-start.14
  58.0 4.0 %collective-permute-start.15 = (f32[6,4,64,128]{3,2,1,0:T(8,128)S(1)}, f32[6,4,64,128]{3,2,1,0:T(8,128)S(1)}, u32[]{:S(2)}, u32[]{:S(2)}) collective-permute-start(f32[6,4,64,128]{3,2,1,0:T(8,128)S(1)} %shard_map.87.refs_1_), channel_id=1, source_target_pairs={{64,128},{128,64},{65,129},{129,65},{66,130},{130,66},{67,131},{13... | collective-permute-start | bytes 2359304 | tf_op jit(solution)/shard_map/ppermute | solution.py:415
  62.0 0.5 collective-permute-start.18
  62.5 0.8 collective-permute-start.17
  63.3 2.9 %collective-permute-start.16 = (f32[8,128]{1,0:T(8,128)S(1)}, f32[8,128]{1,0:T(8,128)S(1)}, u32[]{:S(2)}, u32[]{:S(2)}) collective-permute-start(f32[8,128]{1,0:T(8,128)S(1)} %get-tuple-element.130), channel_id=1, source_target_pairs={{0,16},{1,17},{2,18},{3,19},{4,20},{5,21},{6,22},{7,23},{8,24},{9,... | collective-permute-start | bytes 12296 | tf_op jit(solution)/shard_map/ppermute | solution.py:512
  66.2 0.7 collective-permute-done.18
  66.9 0.7 collective-permute-done.17
  67.6 0.2 collective-permute-done.16
  67.8 0.1 collective-permute-start.20
  67.9 1.8 %collective-permute-start.19 = (f32[8,128]{1,0:T(8,128)S(1)}, f32[8,128]{1,0:T(8,128)S(1)}, u32[]{:S(2)}, u32[]{:S(2)}) collective-permute-start(f32[8,128]{1,0:T(8,128)S(1)} %add_add_fusion.1), channel_id=1, source_target_pairs={{0,4},{4,0},{8,12},{12,8},{16,20},{20,16},{24,28},{28,24},{32,36},... | collective-permute-start | bytes 12296 | tf_op jit(solution)/shard_map/ppermute | solution.py:415
  69.7 1.2 %collective-permute-done.21 = f32[8,128]{1,0:T(8,128)S(1)} collective-permute-done((f32[8,128]{1,0:T(8,128)S(1)}, f32[8,128]{1,0:T(8,128)S(1)}, u32[]{:S(2)}, u32[]{:S(2)}) %collective-permute-start.21) | collective-permute-done | bytes 4128 | tf_op jit(solution)/shard_map/ppermute | solution.py:512
  70.9 0.7 collective-permute-done.20
  71.6 1.3 %collective-permute-start.22 = (f32[8,128]{1,0:T(8,128)S(1)}, f32[8,128]{1,0:T(8,128)S(1)}, u32[]{:S(2)}, u32[]{:S(2)}) collective-permute-start(f32[8,128]{1,0:T(8,128)S(1)} %add_add_fusion), channel_id=1, source_target_pairs={{0,2},{1,3},{2,0},{3,1},{4,6},{5,7},{6,4},{7,5},{8,10},{9,11},{10,... | collective-permute-start | bytes 12296 | tf_op jit(solution)/shard_map/ppermute | solution.py:512
  72.8 3.3 %collective-permute-done.22 = f32[8,128]{1,0:T(8,128)S(1)} collective-permute-done((f32[8,128]{1,0:T(8,128)S(1)}, f32[8,128]{1,0:T(8,128)S(1)}, u32[]{:S(2)}, u32[]{:S(2)}) %collective-permute-start.22) | collective-permute-done | bytes 4128 | tf_op jit(solution)/shard_map/ppermute | solution.py:512
  76.2 2.8 %collective-permute-start.23 = (f32[8,128]{1,0:T(8,128)S(1)}, f32[8,128]{1,0:T(8,128)S(1)}, u32[]{:S(2)}, u32[]{:S(2)}) collective-permute-start(f32[8,128]{1,0:T(8,128)S(1)} %add.36.refs_0_), channel_id=1, source_target_pairs={{0,11},{1,10},{2,9},{3,8},{4,15},{5,14},{6,13},{7,12},{8,3},{9,2},... | collective-permute-start | bytes 12296 | tf_op jit(solution)/shard_map/ppermute | solution.py:512
  78.9 1.0 %shard_map.88 = (f32[4,256,128]{2,1,0:T(8,128)}, f32[4,256,128]{2,1,0:T(8,128)}) custom-call(s32[3,8,128]{2,1,0:T(8,128)S(1)} %shard_map.76.refs_7_.refs_0_, f32[6,4,64,128]{3,2,1,0:T(8,128)S(1)} %shard_map.87.refs_1_, f32[6,4,64,128]{3,2,1,0:T(8,128)S(1)} %collective-permute-done.14.refs_2_, f32[6,4,64,128]{3,2,1,0:T(8,128)S(1)} %collective-permute-done.15.refs_3_, ...), custom_call_target="tpu_custom_call" | custom-call | flops 4000 | bytes 1000 | tf_op jit(solution)/shard_map/pallas_call | solution.py:397
  80.0 1.0 %collective-permute-done.23.refs_1_ = f32[8,128]{1,0:T(8,128)S(1)} collective-permute-done((f32[8,128]{1,0:T(8,128)S(1)}, f32[8,128]{1,0:T(8,128)S(1)}, u32[]{:S(2)}, u32[]{:S(2)}) %collective-permute-start.23) | collective-permute-done | bytes 4128 | tf_op jit(solution)/shard_map/ppermute | solution.py:512
  81.0 0.5 copy.8
  (24 shorter events, 0.5 us)
Async XLA Ops:
  2.7 12.8 %collective-permute-start = (f32[4,4,8,128]{3,2,1,0:T(8,128)S(1)}, f32[4,4,8,128]{3,2,1,0:T(8,128)S(1)}, u32[]{:S(2)}, u32[]{:S(2)}) collective-permute-start(f32[4,4,8,128]{3,2,1,0:T(8,128)S(1)} %get-tuple-element.67), channel_id=1, source_target_pairs={{0,1},{1,0},{2,3},{3,2},{4,5},{5,4},{6,7},{7,6},{8,9},{9,8},{10,11... | collective-permute-start | bytes 196616 | tf_op jit(solution)/shard_map/ppermute | solution.py:415
  4.7 10.9 %collective-permute-start.1 = (f32[4,4,8,128]{3,2,1,0:T(8,128)S(1)}, f32[4,4,8,128]{3,2,1,0:T(8,128)S(1)}, u32[]{:S(2)}, u32[]{:S(2)}) collective-permute-start(f32[4,4,8,128]{3,2,1,0:T(8,128)S(1)} %get-tuple-element.68), channel_id=1, source_target_pairs={{0,3},{1,2},{2,1},{3,0},{4,7},{5,6},{6,5},{7,4},{8,11},{9,10},{10,... | collective-permute-start | bytes 196616 | tf_op jit(solution)/shard_map/ppermute | solution.py:415
  7.5 11.6 %collective-permute-start.3 = (f32[4,64,128]{2,1,0:T(8,128)S(1)}, f32[4,64,128]{2,1,0:T(8,128)S(1)}, u32[]{:S(2)}, u32[]{:S(2)}) collective-permute-start(f32[4,64,128]{2,1,0:T(8,128)S(1)} %get-tuple-element.72.refs_2_.refs_3_), channel_id=1, source_target_pairs={{0,60},{4,8},{8,4},{12,16},{16,12},{20,24},{24,20},{28,32},{32,28}... | collective-permute-start | bytes 393224 | tf_op jit(solution)/shard_map/ppermute | solution.py:415
  14.2 4.9 %collective-permute-start.4 = (f32[4,64,128]{2,1,0:T(8,128)S(1)}, f32[4,64,128]{2,1,0:T(8,128)S(1)}, u32[]{:S(2)}, u32[]{:S(2)}) collective-permute-start(f32[4,64,128]{2,1,0:T(8,128)S(1)} %get-tuple-element.76.refs_5_), channel_id=1, source_target_pairs={{0,4},{4,0},{8,12},{12,8},{16,20},{20,16},{24,28},{28,24},{32,36},... | collective-permute-start | bytes 393224 | tf_op jit(solution)/shard_map/ppermute | solution.py:415
  15.7 22.0 %collective-permute-start.2 = (f32[560,128]{1,0:T(8,128)S(1)}, f32[560,128]{1,0:T(8,128)S(1)}, u32[]{:S(2)}, u32[]{:S(2)}) collective-permute-start(f32[560,128]{1,0:T(8,128)S(1)} %get-tuple-element.71), channel_id=1, source_target_pairs={{0,60},{4,8},{8,4},{12,16},{16,12},{20,24},{24,20},{28,32},{32,28}... | collective-permute-start | bytes 860168 | tf_op jit(solution)/shard_map/ppermute | solution.py:415
  17.9 1.2 %collective-permute-start.5 = (f32[4,8,128]{2,1,0:T(8,128)S(1)}, f32[4,8,128]{2,1,0:T(8,128)S(1)}, u32[]{:S(2)}, u32[]{:S(2)}) collective-permute-start(f32[4,8,128]{2,1,0:T(8,128)S(1)} %get-tuple-element.80), channel_id=1, source_target_pairs={{0,4},{4,0},{8,12},{12,8},{16,20},{20,16},{24,28},{28,24},{32,36},... | collective-permute-start | bytes 49160 | tf_op jit(solution)/shard_map/ppermute | solution.py:415
  20.5 0.7 copy-start
  20.5 1.4 %collective-permute-start.6 = (f32[272,128]{1,0:T(8,128)S(1)}, f32[272,128]{1,0:T(8,128)S(1)}, u32[]{:S(2)}, u32[]{:S(2)}) collective-permute-start(f32[272,128]{1,0:T(8,128)S(1)} %get-tuple-element.92), channel_id=1, source_target_pairs={{0,4},{4,0},{8,12},{12,8},{16,20},{20,16},{24,28},{28,24},{32,36},... | collective-permute-start | bytes 417800 | tf_op jit(solution)/shard_map/ppermute | solution.py:415
  22.5 16.5 %collective-permute-start.7 = (f32[272,128]{1,0:T(8,128)S(1)}, f32[272,128]{1,0:T(8,128)S(1)}, u32[]{:S(2)}, u32[]{:S(2)}) collective-permute-start(f32[272,128]{1,0:T(8,128)S(1)} %get-tuple-element.97), channel_id=1, source_target_pairs={{0,4},{4,0},{8,12},{12,8},{16,20},{20,16},{24,28},{28,24},{32,36},... | collective-permute-start | bytes 417800 | tf_op jit(solution)/shard_map/ppermute | solution.py:415
  22.8 21.0 %collective-permute-start.9 = (f32[280,128]{1,0:T(8,128)S(1)}, f32[280,128]{1,0:T(8,128)S(1)}, u32[]{:S(2)}, u32[]{:S(2)}) collective-permute-start(f32[280,128]{1,0:T(8,128)S(1)} %get-tuple-element.99), channel_id=1, source_target_pairs={{0,60},{4,8},{8,4},{12,16},{16,12},{20,24},{24,20},{28,32},{32,28}... | collective-permute-start | bytes 430088 | tf_op jit(solution)/shard_map/ppermute | solution.py:415
  40.1 3.8 %collective-permute-start.10 = (f32[272,128]{1,0:T(8,128)S(1)}, f32[272,128]{1,0:T(8,128)S(1)}, u32[]{:S(2)}, u32[]{:S(2)}) collective-permute-start(f32[272,128]{1,0:T(8,128)S(1)} %get-tuple-element.116), channel_id=1, source_target_pairs={{0,4},{4,0},{8,12},{12,8},{16,20},{20,16},{24,28},{28,24},{32,36},... | collective-permute-start | bytes 417800 | tf_op jit(solution)/shard_map/ppermute | solution.py:415
  40.8 15.4 %collective-permute-start.8 = (f32[528,128]{1,0:T(8,128)S(1)}, f32[528,128]{1,0:T(8,128)S(1)}, u32[]{:S(2)}, u32[]{:S(2)}) collective-permute-start(f32[528,128]{1,0:T(8,128)S(1)} %get-tuple-element.98), channel_id=1, source_target_pairs={{0,60},{4,8},{8,4},{12,16},{16,12},{20,24},{24,20},{28,32},{32,28}... | collective-permute-start | bytes 811016 | tf_op jit(solution)/shard_map/ppermute | solution.py:415
  44.4 12.8 %collective-permute-start.12 = (f32[2,4,64,128]{3,2,1,0:T(8,128)S(1)}, f32[2,4,64,128]{3,2,1,0:T(8,128)S(1)}, u32[]{:S(2)}, u32[]{:S(2)}) collective-permute-start(f32[2,4,64,128]{3,2,1,0:T(8,128)S(1)} %get-tuple-element.127.refs_4_), channel_id=1, source_target_pairs={{0,64},{64,0},{128,192},{192,128},{1,65},{65,1},{129,193},{193,129... | collective-permute-start | bytes 786440 | tf_op jit(solution)/shard_map/ppermute | solution.py:415
  45.1 12.2 %collective-permute-start.13 = (f32[2,4,64,128]{3,2,1,0:T(8,128)S(1)}, f32[2,4,64,128]{3,2,1,0:T(8,128)S(1)}, u32[]{:S(2)}, u32[]{:S(2)}) collective-permute-start(f32[2,4,64,128]{3,2,1,0:T(8,128)S(1)} %get-tuple-element.127.refs_4_), channel_id=1, source_target_pairs={{64,128},{128,64},{65,129},{129,65},{66,130},{130,66},{67,131},{13... | collective-permute-start | bytes 786440 | tf_op jit(solution)/shard_map/ppermute | solution.py:415
  49.1 1.6 %collective-permute-start.11 = (f32[256,128]{1,0:T(8,128)S(1)}, f32[256,128]{1,0:T(8,128)S(1)}, u32[]{:S(2)}, u32[]{:S(2)}) collective-permute-start(f32[256,128]{1,0:T(8,128)S(1)} %get-tuple-element.121), channel_id=1, source_target_pairs={{0,4},{4,0},{8,12},{12,8},{16,20},{20,16},{24,28},{28,24},{32,36},... | collective-permute-start | bytes 393224 | tf_op jit(solution)/shard_map/ppermute | solution.py:415
  57.3 21.6 %collective-permute-start.14 = (f32[6,4,64,128]{3,2,1,0:T(8,128)S(1)}, f32[6,4,64,128]{3,2,1,0:T(8,128)S(1)}, u32[]{:S(2)}, u32[]{:S(2)}) collective-permute-start(f32[6,4,64,128]{3,2,1,0:T(8,128)S(1)} %shard_map.87.refs_1_), channel_id=1, source_target_pairs={{0,64},{64,0},{128,192},{192,128},{1,65},{65,1},{129,193},{193,129... | collective-permute-start | bytes 2359304 | tf_op jit(solution)/shard_map/ppermute | solution.py:415
  58.0 21.0 %collective-permute-start.15 = (f32[6,4,64,128]{3,2,1,0:T(8,128)S(1)}, f32[6,4,64,128]{3,2,1,0:T(8,128)S(1)}, u32[]{:S(2)}, u32[]{:S(2)}) collective-permute-start(f32[6,4,64,128]{3,2,1,0:T(8,128)S(1)} %shard_map.87.refs_1_), channel_id=1, source_target_pairs={{64,128},{128,64},{65,129},{129,65},{66,130},{130,66},{67,131},{13... | collective-permute-start | bytes 2359304 | tf_op jit(solution)/shard_map/ppermute | solution.py:415
  62.0 4.9 %collective-permute-start.18 = (f32[8,128]{1,0:T(8,128)S(1)}, f32[8,128]{1,0:T(8,128)S(1)}, u32[]{:S(2)}, u32[]{:S(2)}) collective-permute-start(f32[8,128]{1,0:T(8,128)S(1)} %get-tuple-element.130), channel_id=1, source_target_pairs={{0,48},{1,49},{2,50},{3,51},{4,52},{5,53},{6,54},{7,55},{8,56},{9,... | collective-permute-start | bytes 12296 | tf_op jit(solution)/shard_map/ppermute | solution.py:512
  62.5 5.1 %collective-permute-start.17 = (f32[8,128]{1,0:T(8,128)S(1)}, f32[8,128]{1,0:T(8,128)S(1)}, u32[]{:S(2)}, u32[]{:S(2)}) collective-permute-start(f32[8,128]{1,0:T(8,128)S(1)} %get-tuple-element.130), channel_id=1, source_target_pairs={{0,32},{1,33},{2,34},{3,35},{4,36},{5,37},{6,38},{7,39},{8,40},{9,... | collective-permute-start | bytes 12296 | tf_op jit(solution)/shard_map/ppermute | solution.py:512
  63.3 4.5 %collective-permute-start.16 = (f32[8,128]{1,0:T(8,128)S(1)}, f32[8,128]{1,0:T(8,128)S(1)}, u32[]{:S(2)}, u32[]{:S(2)}) collective-permute-start(f32[8,128]{1,0:T(8,128)S(1)} %get-tuple-element.130), channel_id=1, source_target_pairs={{0,16},{1,17},{2,18},{3,19},{4,20},{5,21},{6,22},{7,23},{8,24},{9,... | collective-permute-start | bytes 12296 | tf_op jit(solution)/shard_map/ppermute | solution.py:512
  67.8 3.0 %collective-permute-start.21 = (f32[8,128]{1,0:T(8,128)S(1)}, f32[8,128]{1,0:T(8,128)S(1)}, u32[]{:S(2)}, u32[]{:S(2)}) collective-permute-start(f32[8,128]{1,0:T(8,128)S(1)} %add_add_fusion.1), channel_id=1, source_target_pairs={{0,5},{1,4},{2,7},{3,6},{4,1},{5,0},{6,3},{7,2},{8,13},{9,12},{10,... | collective-permute-start | bytes 12296 | tf_op jit(solution)/shard_map/ppermute | solution.py:512
  67.8 3.7 %collective-permute-start.20 = (f32[8,128]{1,0:T(8,128)S(1)}, f32[8,128]{1,0:T(8,128)S(1)}, u32[]{:S(2)}, u32[]{:S(2)}) collective-permute-start(f32[8,128]{1,0:T(8,128)S(1)} %add_add_fusion.1), channel_id=1, source_target_pairs={{0,1},{1,0},{2,3},{3,2},{4,5},{5,4},{6,7},{7,6},{8,9},{9,8},{10,11... | collective-permute-start | bytes 12296 | tf_op jit(solution)/shard_map/ppermute | solution.py:512
  67.9 3.6 %collective-permute-start.19 = (f32[8,128]{1,0:T(8,128)S(1)}, f32[8,128]{1,0:T(8,128)S(1)}, u32[]{:S(2)}, u32[]{:S(2)}) collective-permute-start(f32[8,128]{1,0:T(8,128)S(1)} %add_add_fusion.1), channel_id=1, source_target_pairs={{0,4},{4,0},{8,12},{12,8},{16,20},{20,16},{24,28},{28,24},{32,36},... | collective-permute-start | bytes 12296 | tf_op jit(solution)/shard_map/ppermute | solution.py:415
  71.6 4.6 %collective-permute-start.22 = (f32[8,128]{1,0:T(8,128)S(1)}, f32[8,128]{1,0:T(8,128)S(1)}, u32[]{:S(2)}, u32[]{:S(2)}) collective-permute-start(f32[8,128]{1,0:T(8,128)S(1)} %add_add_fusion), channel_id=1, source_target_pairs={{0,2},{1,3},{2,0},{3,1},{4,6},{5,7},{6,4},{7,5},{8,10},{9,11},{10,... | collective-permute-start | bytes 12296 | tf_op jit(solution)/shard_map/ppermute | solution.py:512
  76.2 4.8 %collective-permute-start.23 = (f32[8,128]{1,0:T(8,128)S(1)}, f32[8,128]{1,0:T(8,128)S(1)}, u32[]{:S(2)}, u32[]{:S(2)}) collective-permute-start(f32[8,128]{1,0:T(8,128)S(1)} %add.36.refs_0_), channel_id=1, source_target_pairs={{0,11},{1,10},{2,9},{3,8},{4,15},{5,14},{6,13},{7,12},{8,3},{9,2},... | collective-permute-start | bytes 12296 | tf_op jit(solution)/shard_map/ppermute | solution.py:512

commit v5 on v4

--- a/solution.py
+++ b/solution.py
@@ -226,6 +226,19 @@
     return (lambda c, o: ref[main + NZ * c + 8 * o : main + NZ * c + 8 * o + 8, :], ghosts)
 
 
+def inside_four(ref, main, edge):
+    ghosts = lambda c: pltpu.roll(ref[edge : edge + 8, :], (6 - 4 * c) % LANES, 1)
+    return (inside(ref, main, edge)[0], ghosts)
+
+
+def write_four(ref, edge, load):
+    part = lanes() % 16 // 4
+    out = pltpu.roll(load(0), LANES - 6, 1)
+    for c in range(1, COMPS):
+        out = jnp.where(part == c, pltpu.roll(load(c), (4 * c - 6) % LANES, 1), out)
+    ref[edge : edge + 8, :] = out
+
+
 def write_main(ref, main, load):
     for c in range(COMPS):
         for o in range(OCT):
@@ -248,7 +261,7 @@
     held = [layer_of(mom, pg.at[u + 1]) for u, mom in enumerate((k1, k2, k3))]
     step(around, held, [(q1, p1), (q2, p2), (q3, p3)], par, 0.5 * STEP, total)
     write_main(msg, 0, joint(q1)[0])
-    write_edge(msg, SITES, joint(q1)[1])
+    write_four(msg, SITES, joint(q1)[1])
     write_main(msg_near, 0, joint(q3)[0])
     write_edge(msg_near, SITES, joint(q3)[1])
     store = store_main(z, zp)
@@ -273,19 +286,19 @@
 
 
 def inner_second(par, z, q1, p1, q2, p2, q3, p3, near, n1, r1, n2, r2, n3, r3, msg, msg_near):
-    around = [joint(z), joint(q1), joint(q2), joint(q3), inside(near, 0, SITES)]
+    around = [joint(z), joint(q1), joint(q2), joint(q3), inside_four(near, 0, SITES)]
     moms = [joint(p1), joint(p2), joint(p3)]
     step(around, moms, [(n1, r1), (n2, r2), (n3, r3)], settings(par), STEP)
     write_main(msg, 0, joint(q1)[0])
-    write_edge(msg, SITES, joint(q1)[1])
-    write_main(msg, SITES + 16, joint(n1)[0])
+    write_four(msg, SITES, joint(q1)[1])
+    write_main(msg, SITES + 8, joint(n1)[0])
     write_main(msg_near, 0, joint(n3)[0])
-    write_edge(msg_near, SITES, joint(n3)[1])
+    write_four(msg_near, SITES, joint(n3)[1])
 
 
 def outer_kernel(par, beyond, hq, hp, zold, zold_g, z, zp, old1, q1, p1, q2, nhq, nhp, nz, nzp, n1, r1):
     par = settings(par)
-    step([inside(beyond, 0, SITES), joint(hq), layer_of(zold, zold_g)], [joint(hp)], [(nhq, nhp)], par, STEP)
+    step([inside_four(beyond, 0, SITES), joint(hq), layer_of(zold, zold_g)], [joint(hp)], [(nhq, nhp)], par, STEP)
     step([joint(nhq), joint(z), joint(old1)], [joint(zp)], [(nz, nzp)], par, STEP)
     step([joint(nz), joint(q1), joint(q2)], [joint(p1)], [(n1, r1)], par, STEP)
 
@@ -294,11 +307,11 @@
     around = [joint(q1), joint(q2), joint(q3), inside(near, 0, SITES)]
     step(around, [joint(p2), joint(p3)], [(n2, r2), (n3, r3)], settings(par), STEP)
     write_main(msg, 0, joint(n3)[0])
-    write_edge(msg, SITES, joint(n3)[1])
+    write_four(msg, SITES, joint(n3)[1])
 
 
 def inner_third(par, q1, q2, p2, q3, p3, near, n2, r2, n3, r3, msg, whole):
-    around = [joint(q1), joint(q2), joint(q3), inside(near, 0, SITES)]
+    around = [joint(q1), joint(q2), joint(q3), inside_four(near, 0, SITES)]
     step(around, [joint(p2), joint(p3)], [(n2, r2), (n3, r3)], settings(par), STEP)
     write_main(msg, 0, joint(n3)[0])
     for u, ref in enumerate((n2, n3)):
@@ -319,10 +332,10 @@
     whole, energy, nhq, nhp, nz, nzp, last,
 ):
     par = settings(par)
-    step([inside(beyond, 0, SITES), joint(hq), joint(zold)], [joint(hp)], [(nhq, nhp)], par, STEP)
+    step([inside_four(beyond, 0, SITES), joint(hq), joint(zold)], [joint(hp)], [(nhq, nhp)], par, STEP)
     step([joint(nhq), joint(z), joint(old1)], [joint(zp)], [(nz, nzp)], par, STEP)
     store = store_main(last, None)
-    outer = inside(beyond, SITES + 16, 0)
+    outer = inside(beyond, SITES + 8, 0)
     main_eval(outer, joint(nhq), joint(z), joint(nhp), store, par, STEP, None)
     total = [more[...], True]
     store = store_main(None, whole.at[2])
@@ -440,7 +453,7 @@
 
     main, both = (f32(COMPS, NZ, LANES), f32(COMPS, NZ + 8, LANES))
     edges, whole, vreg = (f32(WIDE, COMPS, 8, LANES), f32(WIDE, COMPS, NZ, LANES), f32(8, LANES))
-    edge, side = (f32(COMPS, 8, LANES), f32(SITES + 16, LANES))
+    edge, side, slim = (f32(COMPS, 8, LANES), f32(SITES + 16, LANES), f32(SITES + 8, LANES))
 
     m0, m1, m2, m3, k0, k1, k2, k3, to_first, to_second = run(
         ingest_kernel,
@@ -457,12 +470,12 @@
     near_ghost, beyond0 = (near(near_g), far(to_far))
     z1, zp1, a1, b1, a2, b2, a3, b3, start, msg, to_near = run(
         inner_start,
-        [main, main] + [both] * 6 + [vreg, f32(SITES + 24, LANES), side],
+        [main, main] + [both] * 6 + [vreg, f32(SITES + 16, LANES), side],
         [par, far0, m0, m1, m2, m3, k0, k1, k2, k3, qg, pg, near0, near_ghost],
     )
     beyond1, near1 = (far(msg), near(to_near))
     arrays = [par, a1, a2, b2, a3, b3, near1]
-    c2, d2, c3, d3, to_near = run(inner_kernel, [both] * 4 + [side], arrays, after=[choice])
+    c2, d2, c3, d3, to_near = run(inner_kernel, [both] * 4 + [slim], arrays, after=[choice])
     near2 = near(to_near)
     zg1, c1, d1, hq1, hp1, z2, zp2 = run(
         outer_first,
@@ -472,7 +485,7 @@
     )
     e1, f1, e2, f2, e3, f3, msg, to_near = run(
         inner_second,
-        [both] * 6 + [f32(2 * SITES + 16, LANES), side],
+        [both] * 6 + [f32(2 * SITES + 8, LANES), slim],
         [par, z2, c1, d1, c2, d2, c3, d3, near2],
     )
     beyond2 = far(msg)

time: 82.3 us -> 82 us (level)
  no operation moved by 1% of the time
where the time goes in v5:
time: 82 us; the launch traced here: 81.2 us
  starting transfers between devices  44.9 us (55%)
  waiting for transfers between devices  21.9 us (27%)
  Pallas kernels  11.1 us (14%)
  between operations  2.14 us (3%)
  local copies, waits for them, and re-layouts  1.05 us (1%)
    ppermute x17, starting transfers between devices, pair_swap(): lax.ppermute(value, axis, [(i, other(i)) for i in range(lax.axis_size(axi...  36.5 us
    ppermute x17, waiting for transfers between devices, pair_swap(): lax.ppermute(value, axis, [(i, other(i)) for i in range(lax.axis_size(axi...  14.1 us
    pallas_call x14, Pallas kernels, run(): pl.pallas_call(body, out_shape=[space(out.shape, out.dtype) for out in ou...  11.1 us
    ppermute x7, starting transfers between devices, across(): return lax.ppermute(value, ('gx', 'gy'), pairs)  8.34 us
    ppermute x7, waiting for transfers between devices, across(): return lax.ppermute(value, ('gx', 'gy'), pairs)  7.75 us
  transfers between devices with their start and end apart: 24, of which 12 were waited for; matrix products, arithmetic and copies ran while one was open for 0% of the time, Pallas kernels for 11%

profile of v5, /device:TPU:2, one launch (start us, length us, event | category | flops | bytes accessed | tf_op | source)
XLA Modules:
  0.0 81.2 jit_solution(2588481411293251163)
XLA Ops:
  0.8 1.9 %shard_map.77 = (f32[4,64,128]{2,1,0:T(8,128)S(1)}, f32[4,64,128]{2,1,0:T(8,128)S(1)}, f32[4,64,128]{2,1,0:T(8,128)S(1)}, f32[4,64,128]{2,1,0:T(8,128)S(1)}, f32...) custom-call(s32[3,8,128]{2,1,0:T(8,128)S(1)} %broadcast_in_dim.4.ref, ...), custom_call_target="tpu_custom_call" | custom-call | flops 4000 | bytes 1000 | tf_op jit(solution)/shard_map/pallas_call | solution.py:410
  2.7 2.0 %collective-permute-start = (f32[4,4,8,128]{3,2,1,0:T(8,128)S(1)}, f32[4,4,8,128]{3,2,1,0:T(8,128)S(1)}, u32[]{:S(2)}, u32[]{:S(2)}) collective-permute-start(f32[4,4,8,128]{3,2,1,0:T(8,128)S(1)} %get-tuple-element.67), channel_id=1, source_target_pairs={{0,1},{1,0},{2,3},{3,2},{4,5},{5,4},{6,7},{7,6},{8,9},{9,8},{10,11... | collective-permute-start | bytes 196616 | tf_op jit(solution)/shard_map/ppermute | solution.py:428
  4.7 2.8 %collective-permute-start.1 = (f32[4,4,8,128]{3,2,1,0:T(8,128)S(1)}, f32[4,4,8,128]{3,2,1,0:T(8,128)S(1)}, u32[]{:S(2)}, u32[]{:S(2)}) collective-permute-start(f32[4,4,8,128]{3,2,1,0:T(8,128)S(1)} %get-tuple-element.68), channel_id=1, source_target_pairs={{0,3},{1,2},{2,1},{3,0},{4,7},{5,6},{6,5},{7,4},{8,11},{9,10},{10,... | collective-permute-start | bytes 196616 | tf_op jit(solution)/shard_map/ppermute | solution.py:428
  7.5 6.7 %collective-permute-start.3 = (f32[4,64,128]{2,1,0:T(8,128)S(1)}, f32[4,64,128]{2,1,0:T(8,128)S(1)}, u32[]{:S(2)}, u32[]{:S(2)}) collective-permute-start(f32[4,64,128]{2,1,0:T(8,128)S(1)} %get-tuple-element.72.refs_2_.refs_3_), channel_id=1, source_target_pairs={{0,60},{4,8},{8,4},{12,16},{16,12},{20,24},{24,20},{28,32},{32,28}... | collective-permute-start | bytes 393224 | tf_op jit(solution)/shard_map/ppermute | solution.py:428
  15.5 0.1 shard_map.78
  15.7 2.3 %collective-permute-start.2 = (f32[560,128]{1,0:T(8,128)S(1)}, f32[560,128]{1,0:T(8,128)S(1)}, u32[]{:S(2)}, u32[]{:S(2)}) collective-permute-start(f32[560,128]{1,0:T(8,128)S(1)} %get-tuple-element.71), channel_id=1, source_target_pairs={{0,60},{4,8},{8,4},{12,16},{16,12},{20,24},{24,20},{28,32},{32,28}... | collective-permute-start | bytes 860168 | tf_op jit(solution)/shard_map/ppermute | solution.py:428
  17.9 0.1 collective-permute-start.5
  18.1 1.0 %collective-permute-done.5.refs_13_ = f32[4,8,128]{2,1,0:T(8,128)S(1)} collective-permute-done((f32[4,8,128]{2,1,0:T(8,128)S(1)}, f32[4,8,128]{2,1,0:T(8,128)S(1)}, u32[]{:S(2)}, u32[]{:S(2)}) %collective-permute-start.5) | collective-permute-done | bytes 16416 | tf_op jit(solution)/shard_map/ppermute | solution.py:428
  19.2 1.3 %shard_map.79 = (f32[4,64,128]{2,1,0:T(8,128)S(1)}, f32[4,64,128]{2,1,0:T(8,128)S(1)}, f32[4,72,128]{2,1,0:T(8,128)S(1)}, f32[4,72,128]{2,1,0:T(8,128)S(1)}, f32...) custom-call(f32[2,8,128]{2,1,0:T(8,128)S(1)} %broadcast_in_dim.5.ref, ...), custom_call_target="tpu_custom_call" | custom-call | flops 4000 | bytes 1000 | tf_op jit(solution)/shard_map/pallas_call | solution.py:410
  20.5 0.3 collective-permute-start.6
  20.8 0.4 copy-done
  21.2 0.5 shard_map.76.refs_7_.refs_0_
  21.7 0.2 collective-permute-done.6.refs_6_
  22.0 0.6 shard_map.81
  22.6 0.3 collective-permute-start.7
  22.8 7.0 %collective-permute-start.9 = (f32[272,128]{1,0:T(8,128)S(1)}, f32[272,128]{1,0:T(8,128)S(1)}, u32[]{:S(2)}, u32[]{:S(2)}) collective-permute-start(f32[272,128]{1,0:T(8,128)S(1)} %get-tuple-element.99), channel_id=1, source_target_pairs={{0,60},{4,8},{8,4},{12,16},{16,12},{20,24},{24,20},{28,32},{32,28}... | collective-permute-start | bytes 417800 | tf_op jit(solution)/shard_map/ppermute | solution.py:428
  29.8 7.8 %collective-permute-done.2.refs_1_ = f32[560,128]{1,0:T(8,128)S(1)} collective-permute-done((f32[560,128]{1,0:T(8,128)S(1)}, f32[560,128]{1,0:T(8,128)S(1)}, u32[]{:S(2)}, u32[]{:S(2)}) %collective-permute-start.2) | collective-permute-done | bytes 286752 | tf_op jit(solution)/shard_map/ppermute | solution.py:428
  37.6 1.4 %shard_map.80 = (f32[4,8,128]{2,1,0:T(8,128)S(1)}, f32[4,72,128]{2,1,0:T(8,128)S(1)}, f32[4,72,128]{2,1,0:T(8,128)S(1)}, f32[4,72,128]{2,1,0:T(8,128)S(1)}, f32[...) custom-call(f32[2,8,128]{2,1,0:T(8,128)S(1)} %broadcast_in_dim.5.refs_0_, ...), custom_call_target="tpu_custom_call" | custom-call | flops 4000 | bytes 1000 | tf_op jit(solution)/shard_map/pallas_call | solution.py:410
  39.0 1.0 %shard_map.82 = (f32[4,72,128]{2,1,0:T(8,128)S(1)}, f32[4,72,128]{2,1,0:T(8,128)S(1)}, f32[4,72,128]{2,1,0:T(8,128)S(1)}, f32[4,72,128]{2,1,0:T(8,128)S(1)}, f32...) custom-call(f32[2,8,128]{2,1,0:T(8,128)S(1)} %broadcast_in_dim.5.refs_0_, ...), custom_call_target="tpu_custom_call" | custom-call | flops 4000 | bytes 1000 | tf_op jit(solution)/shard_map/pallas_call | solution.py:410
  40.0 0.7 collective-permute-start.10
  40.8 3.0 %collective-permute-start.8 = (f32[520,128]{1,0:T(8,128)S(1)}, f32[520,128]{1,0:T(8,128)S(1)}, u32[]{:S(2)}, u32[]{:S(2)}) collective-permute-start(f32[520,128]{1,0:T(8,128)S(1)} %get-tuple-element.98), channel_id=1, source_target_pairs={{0,60},{4,8},{8,4},{12,16},{16,12},{20,24},{24,20},{28,32},{32,28}... | collective-permute-start | bytes 798728 | tf_op jit(solution)/shard_map/ppermute | solution.py:428
  43.8 0.6 shard_map.84
  44.4 0.6 collective-permute-start.12
  45.0 4.1 %collective-permute-start.13 = (f32[2,4,64,128]{3,2,1,0:T(8,128)S(1)}, f32[2,4,64,128]{3,2,1,0:T(8,128)S(1)}, u32[]{:S(2)}, u32[]{:S(2)}) collective-permute-start(f32[2,4,64,128]{3,2,1,0:T(8,128)S(1)} %get-tuple-element.127.refs_4_), channel_id=1, source_target_pairs={{64,128},{128,64},{65,129},{129,65},{66,130},{130,66},{67,131},{13... | collective-permute-start | bytes 786440 | tf_op jit(solution)/shard_map/ppermute | solution.py:428
  49.1 0.3 collective-permute-start.11
  49.4 1.1 %shard_map.83 = (f32[4,72,128]{2,1,0:T(8,128)S(1)}, f32[4,72,128]{2,1,0:T(8,128)S(1)}, f32[4,72,128]{2,1,0:T(8,128)S(1)}, f32[4,72,128]{2,1,0:T(8,128)S(1)}, f32...) custom-call(f32[2,8,128]{2,1,0:T(8,128)S(1)} %broadcast_in_dim.5.refs_0_, ...), custom_call_target="tpu_custom_call" | custom-call | flops 4000 | bytes 1000 | tf_op jit(solution)/shard_map/pallas_call | solution.py:410
  50.5 0.2 collective-permute-done.11.refs_6_
  50.7 0.4 shard_map.85
  51.1 4.8 %collective-permute-done.8.refs_1_ = f32[520,128]{1,0:T(8,128)S(1)} collective-permute-done((f32[520,128]{1,0:T(8,128)S(1)}, f32[520,128]{1,0:T(8,128)S(1)}, u32[]{:S(2)}, u32[]{:S(2)}) %collective-permute-start.8) | collective-permute-done | bytes 266272 | tf_op jit(solution)/shard_map/ppermute | solution.py:428
  55.9 1.0 %shard_map.86 = (f32[6,4,64,128]{3,2,1,0:T(8,128)S(1)}, f32[8,128]{1,0:T(8,128)S(1)}) custom-call(f32[2,8,128]{2,1,0:T(8,128)S(1)} %broadcast_in_dim.5.refs_0_, f32[520,128]{1,0:T(8,128)S(1)} %collective-permute-done.8.refs_1_, f32[4,72,128]{2,1,0:T(8,128)S(1)} %get-tuple-element.107.refs_2_, f32[4,72,128]{2,1,0:T(8,128)S(1)} %get-tuple-element.108.refs_3_, ...), custom_call_target="tpu_custom_call" | custom-call | flops 4000 | bytes 1000 | tf_op jit(solution)/shard_map/pallas_call | solution.py:410
  57.0 0.6 collective-permute-start.14
  57.6 4.0 %collective-permute-start.15 = (f32[6,4,64,128]{3,2,1,0:T(8,128)S(1)}, f32[6,4,64,128]{3,2,1,0:T(8,128)S(1)}, u32[]{:S(2)}, u32[]{:S(2)}) collective-permute-start(f32[6,4,64,128]{3,2,1,0:T(8,128)S(1)} %shard_map.87.refs_1_), channel_id=1, source_target_pairs={{64,128},{128,64},{65,129},{129,65},{66,130},{130,66},{67,131},{13... | collective-permute-start | bytes 2359304 | tf_op jit(solution)/shard_map/ppermute | solution.py:428
  61.7 0.4 collective-permute-start.18
  62.1 0.8 collective-permute-start.17
  62.9 3.0 %collective-permute-start.16 = (f32[8,128]{1,0:T(8,128)S(1)}, f32[8,128]{1,0:T(8,128)S(1)}, u32[]{:S(2)}, u32[]{:S(2)}) collective-permute-start(f32[8,128]{1,0:T(8,128)S(1)} %get-tuple-element.130), channel_id=1, source_target_pairs={{0,16},{1,17},{2,18},{3,19},{4,20},{5,21},{6,22},{7,23},{8,24},{9,... | collective-permute-start | bytes 12296 | tf_op jit(solution)/shard_map/ppermute | solution.py:525
  65.9 0.7 collective-permute-done.18
  66.6 0.6 collective-permute-done.17
  67.2 0.3 collective-permute-done.16
  67.5 0.1 collective-permute-start.20
  67.6 1.8 %collective-permute-start.19 = (f32[8,128]{1,0:T(8,128)S(1)}, f32[8,128]{1,0:T(8,128)S(1)}, u32[]{:S(2)}, u32[]{:S(2)}) collective-permute-start(f32[8,128]{1,0:T(8,128)S(1)} %add_add_fusion.1), channel_id=1, source_target_pairs={{0,4},{4,0},{8,12},{12,8},{16,20},{20,16},{24,28},{28,24},{32,36},... | collective-permute-start | bytes 12296 | tf_op jit(solution)/shard_map/ppermute | solution.py:428
  69.4 1.2 %collective-permute-done.21 = f32[8,128]{1,0:T(8,128)S(1)} collective-permute-done((f32[8,128]{1,0:T(8,128)S(1)}, f32[8,128]{1,0:T(8,128)S(1)}, u32[]{:S(2)}, u32[]{:S(2)}) %collective-permute-start.21) | collective-permute-done | bytes 4128 | tf_op jit(solution)/shard_map/ppermute | solution.py:525
  70.5 0.7 collective-permute-done.20
  71.2 1.3 %collective-permute-start.22 = (f32[8,128]{1,0:T(8,128)S(1)}, f32[8,128]{1,0:T(8,128)S(1)}, u32[]{:S(2)}, u32[]{:S(2)}) collective-permute-start(f32[8,128]{1,0:T(8,128)S(1)} %add_add_fusion), channel_id=1, source_target_pairs={{0,2},{1,3},{2,0},{3,1},{4,6},{5,7},{6,4},{7,5},{8,10},{9,11},{10,... | collective-permute-start | bytes 12296 | tf_op jit(solution)/shard_map/ppermute | solution.py:525
  72.5 3.3 %collective-permute-done.22 = f32[8,128]{1,0:T(8,128)S(1)} collective-permute-done((f32[8,128]{1,0:T(8,128)S(1)}, f32[8,128]{1,0:T(8,128)S(1)}, u32[]{:S(2)}, u32[]{:S(2)}) %collective-permute-start.22) | collective-permute-done | bytes 4128 | tf_op jit(solution)/shard_map/ppermute | solution.py:525
  75.8 2.8 %collective-permute-start.23 = (f32[8,128]{1,0:T(8,128)S(1)}, f32[8,128]{1,0:T(8,128)S(1)}, u32[]{:S(2)}, u32[]{:S(2)}) collective-permute-start(f32[8,128]{1,0:T(8,128)S(1)} %add.36.refs_0_), channel_id=1, source_target_pairs={{0,11},{1,10},{2,9},{3,8},{4,15},{5,14},{6,13},{7,12},{8,3},{9,2},... | collective-permute-start | bytes 12296 | tf_op jit(solution)/shard_map/ppermute | solution.py:525
  78.6 1.0 %shard_map.88 = (f32[4,256,128]{2,1,0:T(8,128)}, f32[4,256,128]{2,1,0:T(8,128)}) custom-call(s32[3,8,128]{2,1,0:T(8,128)S(1)} %shard_map.76.refs_7_.refs_0_, f32[6,4,64,128]{3,2,1,0:T(8,128)S(1)} %shard_map.87.refs_1_, f32[6,4,64,128]{3,2,1,0:T(8,128)S(1)} %collective-permute-done.14.refs_2_, f32[6,4,64,128]{3,2,1,0:T(8,128)S(1)} %collective-permute-done.15.refs_3_, ...), custom_call_target="tpu_custom_call" | custom-call | flops 4000 | bytes 1000 | tf_op jit(solution)/shard_map/pallas_call | solution.py:410
  79.6 1.0 %collective-permute-done.23.refs_1_ = f32[8,128]{1,0:T(8,128)S(1)} collective-permute-done((f32[8,128]{1,0:T(8,128)S(1)}, f32[8,128]{1,0:T(8,128)S(1)}, u32[]{:S(2)}, u32[]{:S(2)}) %collective-permute-start.23) | collective-permute-done | bytes 4128 | tf_op jit(solution)/shard_map/ppermute | solution.py:525
  80.7 0.5 copy.8
  (24 shorter events, 0.5 us)
Async XLA Ops:
  2.7 12.8 %collective-permute-start = (f32[4,4,8,128]{3,2,1,0:T(8,128)S(1)}, f32[4,4,8,128]{3,2,1,0:T(8,128)S(1)}, u32[]{:S(2)}, u32[]{:S(2)}) collective-permute-start(f32[4,4,8,128]{3,2,1,0:T(8,128)S(1)} %get-tuple-element.67), channel_id=1, source_target_pairs={{0,1},{1,0},{2,3},{3,2},{4,5},{5,4},{6,7},{7,6},{8,9},{9,8},{10,11... | collective-permute-start | bytes 196616 | tf_op jit(solution)/shard_map/ppermute | solution.py:428
  4.7 10.9 %collective-permute-start.1 = (f32[4,4,8,128]{3,2,1,0:T(8,128)S(1)}, f32[4,4,8,128]{3,2,1,0:T(8,128)S(1)}, u32[]{:S(2)}, u32[]{:S(2)}) collective-permute-start(f32[4,4,8,128]{3,2,1,0:T(8,128)S(1)} %get-tuple-element.68), channel_id=1, source_target_pairs={{0,3},{1,2},{2,1},{3,0},{4,7},{5,6},{6,5},{7,4},{8,11},{9,10},{10,... | collective-permute-start | bytes 196616 | tf_op jit(solution)/shard_map/ppermute | solution.py:428
  7.5 11.6 %collective-permute-start.3 = (f32[4,64,128]{2,1,0:T(8,128)S(1)}, f32[4,64,128]{2,1,0:T(8,128)S(1)}, u32[]{:S(2)}, u32[]{:S(2)}) collective-permute-start(f32[4,64,128]{2,1,0:T(8,128)S(1)} %get-tuple-element.72.refs_2_.refs_3_), channel_id=1, source_target_pairs={{0,60},{4,8},{8,4},{12,16},{16,12},{20,24},{24,20},{28,32},{32,28}... | collective-permute-start | bytes 393224 | tf_op jit(solution)/shard_map/ppermute | solution.py:428
  14.2 4.9 %collective-permute-start.4 = (f32[4,64,128]{2,1,0:T(8,128)S(1)}, f32[4,64,128]{2,1,0:T(8,128)S(1)}, u32[]{:S(2)}, u32[]{:S(2)}) collective-permute-start(f32[4,64,128]{2,1,0:T(8,128)S(1)} %get-tuple-element.76.refs_5_), channel_id=1, source_target_pairs={{0,4},{4,0},{8,12},{12,8},{16,20},{20,16},{24,28},{28,24},{32,36},... | collective-permute-start | bytes 393224 | tf_op jit(solution)/shard_map/ppermute | solution.py:428
  15.7 22.0 %collective-permute-start.2 = (f32[560,128]{1,0:T(8,128)S(1)}, f32[560,128]{1,0:T(8,128)S(1)}, u32[]{:S(2)}, u32[]{:S(2)}) collective-permute-start(f32[560,128]{1,0:T(8,128)S(1)} %get-tuple-element.71), channel_id=1, source_target_pairs={{0,60},{4,8},{8,4},{12,16},{16,12},{20,24},{24,20},{28,32},{32,28}... | collective-permute-start | bytes 860168 | tf_op jit(solution)/shard_map/ppermute | solution.py:428
  17.9 1.2 %collective-permute-start.5 = (f32[4,8,128]{2,1,0:T(8,128)S(1)}, f32[4,8,128]{2,1,0:T(8,128)S(1)}, u32[]{:S(2)}, u32[]{:S(2)}) collective-permute-start(f32[4,8,128]{2,1,0:T(8,128)S(1)} %get-tuple-element.80), channel_id=1, source_target_pairs={{0,4},{4,0},{8,12},{12,8},{16,20},{20,16},{24,28},{28,24},{32,36},... | collective-permute-start | bytes 49160 | tf_op jit(solution)/shard_map/ppermute | solution.py:428
  20.5 0.7 copy-start
  20.5 1.4 %collective-permute-start.6 = (f32[272,128]{1,0:T(8,128)S(1)}, f32[272,128]{1,0:T(8,128)S(1)}, u32[]{:S(2)}, u32[]{:S(2)}) collective-permute-start(f32[272,128]{1,0:T(8,128)S(1)} %get-tuple-element.92), channel_id=1, source_target_pairs={{0,4},{4,0},{8,12},{12,8},{16,20},{20,16},{24,28},{28,24},{32,36},... | collective-permute-start | bytes 417800 | tf_op jit(solution)/shard_map/ppermute | solution.py:428
  22.6 16.4 %collective-permute-start.7 = (f32[264,128]{1,0:T(8,128)S(1)}, f32[264,128]{1,0:T(8,128)S(1)}, u32[]{:S(2)}, u32[]{:S(2)}) collective-permute-start(f32[264,128]{1,0:T(8,128)S(1)} %get-tuple-element.97), channel_id=1, source_target_pairs={{0,4},{4,0},{8,12},{12,8},{16,20},{20,16},{24,28},{28,24},{32,36},... | collective-permute-start | bytes 405512 | tf_op jit(solution)/shard_map/ppermute | solution.py:428
  22.8 21.0 %collective-permute-start.9 = (f32[272,128]{1,0:T(8,128)S(1)}, f32[272,128]{1,0:T(8,128)S(1)}, u32[]{:S(2)}, u32[]{:S(2)}) collective-permute-start(f32[272,128]{1,0:T(8,128)S(1)} %get-tuple-element.99), channel_id=1, source_target_pairs={{0,60},{4,8},{8,4},{12,16},{16,12},{20,24},{24,20},{28,32},{32,28}... | collective-permute-start | bytes 417800 | tf_op jit(solution)/shard_map/ppermute | solution.py:428
  40.0 3.8 %collective-permute-start.10 = (f32[264,128]{1,0:T(8,128)S(1)}, f32[264,128]{1,0:T(8,128)S(1)}, u32[]{:S(2)}, u32[]{:S(2)}) collective-permute-start(f32[264,128]{1,0:T(8,128)S(1)} %get-tuple-element.116), channel_id=1, source_target_pairs={{0,4},{4,0},{8,12},{12,8},{16,20},{20,16},{24,28},{28,24},{32,36},... | collective-permute-start | bytes 405512 | tf_op jit(solution)/shard_map/ppermute | solution.py:428
  40.8 15.1 %collective-permute-start.8 = (f32[520,128]{1,0:T(8,128)S(1)}, f32[520,128]{1,0:T(8,128)S(1)}, u32[]{:S(2)}, u32[]{:S(2)}) collective-permute-start(f32[520,128]{1,0:T(8,128)S(1)} %get-tuple-element.98), channel_id=1, source_target_pairs={{0,60},{4,8},{8,4},{12,16},{16,12},{20,24},{24,20},{28,32},{32,28}... | collective-permute-start | bytes 798728 | tf_op jit(solution)/shard_map/ppermute | solution.py:428
  44.4 12.5 %collective-permute-start.12 = (f32[2,4,64,128]{3,2,1,0:T(8,128)S(1)}, f32[2,4,64,128]{3,2,1,0:T(8,128)S(1)}, u32[]{:S(2)}, u32[]{:S(2)}) collective-permute-start(f32[2,4,64,128]{3,2,1,0:T(8,128)S(1)} %get-tuple-element.127.refs_4_), channel_id=1, source_target_pairs={{0,64},{64,0},{128,192},{192,128},{1,65},{65,1},{129,193},{193,129... | collective-permute-start | bytes 786440 | tf_op jit(solution)/shard_map/ppermute | solution.py:428
  45.0 11.9 %collective-permute-start.13 = (f32[2,4,64,128]{3,2,1,0:T(8,128)S(1)}, f32[2,4,64,128]{3,2,1,0:T(8,128)S(1)}, u32[]{:S(2)}, u32[]{:S(2)}) collective-permute-start(f32[2,4,64,128]{3,2,1,0:T(8,128)S(1)} %get-tuple-element.127.refs_4_), channel_id=1, source_target_pairs={{64,128},{128,64},{65,129},{129,65},{66,130},{130,66},{67,131},{13... | collective-permute-start | bytes 786440 | tf_op jit(solution)/shard_map/ppermute | solution.py:428
  49.1 1.6 %collective-permute-start.11 = (f32[256,128]{1,0:T(8,128)S(1)}, f32[256,128]{1,0:T(8,128)S(1)}, u32[]{:S(2)}, u32[]{:S(2)}) collective-permute-start(f32[256,128]{1,0:T(8,128)S(1)} %get-tuple-element.121), channel_id=1, source_target_pairs={{0,4},{4,0},{8,12},{12,8},{16,20},{20,16},{24,28},{28,24},{32,36},... | collective-permute-start | bytes 393224 | tf_op jit(solution)/shard_map/ppermute | solution.py:428
  57.0 21.6 %collective-permute-start.14 = (f32[6,4,64,128]{3,2,1,0:T(8,128)S(1)}, f32[6,4,64,128]{3,2,1,0:T(8,128)S(1)}, u32[]{:S(2)}, u32[]{:S(2)}) collective-permute-start(f32[6,4,64,128]{3,2,1,0:T(8,128)S(1)} %shard_map.87.refs_1_), channel_id=1, source_target_pairs={{0,64},{64,0},{128,192},{192,128},{1,65},{65,1},{129,193},{193,129... | collective-permute-start | bytes 2359304 | tf_op jit(solution)/shard_map/ppermute | solution.py:428
  57.6 21.0 %collective-permute-start.15 = (f32[6,4,64,128]{3,2,1,0:T(8,128)S(1)}, f32[6,4,64,128]{3,2,1,0:T(8,128)S(1)}, u32[]{:S(2)}, u32[]{:S(2)}) collective-permute-start(f32[6,4,64,128]{3,2,1,0:T(8,128)S(1)} %shard_map.87.refs_1_), channel_id=1, source_target_pairs={{64,128},{128,64},{65,129},{129,65},{66,130},{130,66},{67,131},{13... | collective-permute-start | bytes 2359304 | tf_op jit(solution)/shard_map/ppermute | solution.py:428
  61.7 4.9 %collective-permute-start.18 = (f32[8,128]{1,0:T(8,128)S(1)}, f32[8,128]{1,0:T(8,128)S(1)}, u32[]{:S(2)}, u32[]{:S(2)}) collective-permute-start(f32[8,128]{1,0:T(8,128)S(1)} %get-tuple-element.130), channel_id=1, source_target_pairs={{0,48},{1,49},{2,50},{3,51},{4,52},{5,53},{6,54},{7,55},{8,56},{9,... | collective-permute-start | bytes 12296 | tf_op jit(solution)/shard_map/ppermute | solution.py:525
  62.1 5.1 %collective-permute-start.17 = (f32[8,128]{1,0:T(8,128)S(1)}, f32[8,128]{1,0:T(8,128)S(1)}, u32[]{:S(2)}, u32[]{:S(2)}) collective-permute-start(f32[8,128]{1,0:T(8,128)S(1)} %get-tuple-element.130), channel_id=1, source_target_pairs={{0,32},{1,33},{2,34},{3,35},{4,36},{5,37},{6,38},{7,39},{8,40},{9,... | collective-permute-start | bytes 12296 | tf_op jit(solution)/shard_map/ppermute | solution.py:525
  62.9 4.6 %collective-permute-start.16 = (f32[8,128]{1,0:T(8,128)S(1)}, f32[8,128]{1,0:T(8,128)S(1)}, u32[]{:S(2)}, u32[]{:S(2)}) collective-permute-start(f32[8,128]{1,0:T(8,128)S(1)} %get-tuple-element.130), channel_id=1, source_target_pairs={{0,16},{1,17},{2,18},{3,19},{4,20},{5,21},{6,22},{7,23},{8,24},{9,... | collective-permute-start | bytes 12296 | tf_op jit(solution)/shard_map/ppermute | solution.py:525
  67.5 3.0 %collective-permute-start.21 = (f32[8,128]{1,0:T(8,128)S(1)}, f32[8,128]{1,0:T(8,128)S(1)}, u32[]{:S(2)}, u32[]{:S(2)}) collective-permute-start(f32[8,128]{1,0:T(8,128)S(1)} %add_add_fusion.1), channel_id=1, source_target_pairs={{0,5},{1,4},{2,7},{3,6},{4,1},{5,0},{6,3},{7,2},{8,13},{9,12},{10,... | collective-permute-start | bytes 12296 | tf_op jit(solution)/shard_map/ppermute | solution.py:525
  67.5 3.7 %collective-permute-start.20 = (f32[8,128]{1,0:T(8,128)S(1)}, f32[8,128]{1,0:T(8,128)S(1)}, u32[]{:S(2)}, u32[]{:S(2)}) collective-permute-start(f32[8,128]{1,0:T(8,128)S(1)} %add_add_fusion.1), channel_id=1, source_target_pairs={{0,1},{1,0},{2,3},{3,2},{4,5},{5,4},{6,7},{7,6},{8,9},{9,8},{10,11... | collective-permute-start | bytes 12296 | tf_op jit(solution)/shard_map/ppermute | solution.py:525
  67.6 3.6 %collective-permute-start.19 = (f32[8,128]{1,0:T(8,128)S(1)}, f32[8,128]{1,0:T(8,128)S(1)}, u32[]{:S(2)}, u32[]{:S(2)}) collective-permute-start(f32[8,128]{1,0:T(8,128)S(1)} %add_add_fusion.1), channel_id=1, source_target_pairs={{0,4},{4,0},{8,12},{12,8},{16,20},{20,16},{24,28},{28,24},{32,36},... | collective-permute-start | bytes 12296 | tf_op jit(solution)/shard_map/ppermute | solution.py:428
  71.2 4.6 %collective-permute-start.22 = (f32[8,128]{1,0:T(8,128)S(1)}, f32[8,128]{1,0:T(8,128)S(1)}, u32[]{:S(2)}, u32[]{:S(2)}) collective-permute-start(f32[8,128]{1,0:T(8,128)S(1)} %add_add_fusion), channel_id=1, source_target_pairs={{0,2},{1,3},{2,0},{3,1},{4,6},{5,7},{6,4},{7,5},{8,10},{9,11},{10,... | collective-permute-start | bytes 12296 | tf_op jit(solution)/shard_map/ppermute | solution.py:525
  75.8 4.8 %collective-permute-start.23 = (f32[8,128]{1,0:T(8,128)S(1)}, f32[8,128]{1,0:T(8,128)S(1)}, u32[]{:S(2)}, u32[]{:S(2)}) collective-permute-start(f32[8,128]{1,0:T(8,128)S(1)} %add.36.refs_0_), channel_id=1, source_target_pairs={{0,11},{1,10},{2,9},{3,8},{4,15},{5,14},{6,13},{7,12},{8,3},{9,2},... | collective-permute-start | bytes 12296 | tf_op jit(solution)/shard_map/ppermute | solution.py:525
